TPU v7x, 32 devices: a whole 2x2x4 slice. The times are simulated.
32 devices in a mesh: ctx: 16 (over z, y, core), fsdp: 2 (over x).
Axes of the slice: x: 2, y: 2, z: 4, core: 2. Of those that a mesh axis runs over, the one named last changes fastest.
Arguments:
- tokens: bfloat16 [2, 4096, 2048], P('fsdp', 'ctx'), may hold values from -6 to 6
- lengths: int32 [2, 2], P('fsdp'), may hold values from 1 to 3072, 4096 in all within a row
- dealing: int32 [2, 16, 256], P('fsdp'), may hold values from 0 to 255, each once within a row
- attn_gain: bfloat16 [2048], P('fsdp'), may hold values from 0.25 to 1.75
- query_weight: bfloat16 [2048, 2048], P('fsdp'), may hold values from -0.125 to 0.125
- kv_weight: bfloat16 [2048, 256], P('fsdp'), may hold values from -0.125 to 0.125
- out_weight: bfloat16 [2048, 2048], P('fsdp'), may hold values from -2 to 2
- mlp_gain: bfloat16 [2048], P('fsdp'), may hold values from 0.25 to 1.75
- gate_weight: bfloat16 [2048, 6144], P('fsdp'), may hold values from -0.125 to 0.125
- up_weight: bfloat16 [2048, 6144], P('fsdp'), may hold values from -0.125 to 0.125
- down_weight: bfloat16 [6144, 2048], P('fsdp'), may hold values from -0.078125 to 0.078125
- cotangent: bfloat16 [2, 4096, 2048], P('fsdp', 'ctx'), may hold values from -6 to 6
Outputs:
- block_output: bfloat16 [2, 4096, 2048], P('fsdp', 'ctx')
- token_grad: float32 [2, 4096, 2048], P('fsdp', 'ctx')
- attn_gain_grad: float32 [2048], P(('ctx', 'fsdp'))
- query_weight_grad: float32 [2048, 2048], P(('ctx', 'fsdp'))
- kv_weight_grad: float32 [2048, 256], P(('ctx', 'fsdp'))
- out_weight_grad: float32 [2048, 2048], P(('ctx', 'fsdp'))
- mlp_gain_grad: float32 [2048], P(('ctx', 'fsdp'))
- gate_weight_grad: float32 [2048, 6144], P(('ctx', 'fsdp'))
- up_weight_grad: float32 [2048, 6144], P(('ctx', 'fsdp'))
- down_weight_grad: float32 [6144, 2048], P(('ctx', 'fsdp'))
Inputs may be any that keep to these rules, and one draw needn't show every extreme that they name: In each batch row the 2 lengths sum to 4096 and none exceeds 3072. Each dealing[b, c] holds every number of 0 to 255 once.
All inputs are finite; a program needn't handle non-finite values.
Results may differ from a plain program's by a relative error of at most 0.015.
Values may be sent and summed in bfloat16 or wider, within the bound.
A program may use at most 448 MiB of HBM per device.

v0:
```python
import jax
import jax.numpy as jnp
from jax import lax
from jax.sharding import PartitionSpec as P

H = 16
HD = 128
WINDOW = 1024
QBLK = 128


epsilon = 1e-06
neg_large = -1e30


def rms_norm(values, gain):
    return values * lax.rsqrt(jnp.mean(values * values, axis=-1, keepdims=True) + epsilon) * gain


def gated_gelu(gate, upward):
    return jax.nn.gelu(gate, approximate=True) * upward


def matmul(left, right):
    return jnp.dot(left, right, preferred_element_type=jnp.float32)


def matmul_left(left, right):
    return lax.dot_general(
        left, right, (((0,), (0,)), ((), ())), preferred_element_type=jnp.float32
    )


def matmul_right(left, right):
    return lax.dot_general(
        left, right, (((1,), (1,)), ((), ())), preferred_element_type=jnp.float32
    )


def on_device(
    tokens,
    lengths,
    dealing,
    attn_gain,
    query_weight,
    kv_weight,
    out_weight,
    mlp_gain,
    gate_weight,
    up_weight,
    down_weight,
    cotangent,
):
    shards = (
        attn_gain,
        query_weight,
        kv_weight,
        out_weight,
        mlp_gain,
        gate_weight,
        up_weight,
        down_weight,
    )
    gathered = (
        lax.all_gather(shards[0], "fsdp", axis=0, tiled=True),
        lax.all_gather(shards[1], "fsdp", axis=0, tiled=True),
        lax.all_gather(shards[2], "fsdp", axis=0, tiled=True),
        lax.all_gather(shards[3], "fsdp", axis=0, tiled=True),
        lax.all_gather(shards[4], "fsdp", axis=0, tiled=True),
        lax.all_gather(shards[5], "fsdp", axis=0, tiled=True),
        lax.all_gather(shards[6], "fsdp", axis=0, tiled=True),
        lax.all_gather(shards[7], "fsdp", axis=0, tiled=True),
    )
    inputs = tokens[0].astype(jnp.float32)
    tok_rows = inputs.shape[0]
    ctx_count = lax.axis_size("ctx")
    own_index = lax.axis_index("ctx")
    piece_rows = tok_rows // ctx_count
    group_rows = tok_rows * ctx_count
    key_span = WINDOW + QBLK
    score_scale = HD ** (-0.5)
    all_deals = dealing[0]
    own_deal = lax.dynamic_index_in_dim(all_deals, own_index, 0, keepdims=False)
    inverse = (
        jnp.zeros((tok_rows,), jnp.int32).at[own_deal].set(jnp.arange(tok_rows, dtype=jnp.int32))
    )
    stream = own_index * tok_rows - WINDOW + jnp.arange(WINDOW + tok_rows, dtype=jnp.int32)
    inside = stream >= 0
    clamped = jnp.maximum(stream, 0)
    source = clamped % tok_rows // piece_rows
    send_slot = clamped // tok_rows * piece_rows + clamped % piece_rows
    given_row = source * tok_rows + all_deals.reshape(-1)[source * tok_rows + send_slot]
    seg_ends = jnp.cumsum(lengths[0])
    segment = jnp.sum((clamped[:, None] >= seg_ends[None, :]).astype(jnp.int32), axis=1)
    segment = jnp.where(inside, segment, -1)
    distance = jnp.arange(QBLK)[:, None] + WINDOW - jnp.arange(key_span)[None, :]
    offsets = jnp.arange(tok_rows // QBLK, dtype=jnp.int32) * QBLK
    gain_one, w_query, w_kv, w_out, gain_two, w_gate, w_up, w_down = gathered
    normed = rms_norm(inputs, gain_one.astype(jnp.float32)).astype(jnp.bfloat16)
    queries = matmul(normed, w_query).astype(jnp.bfloat16)
    pairs = matmul(normed, w_kv).astype(jnp.bfloat16)
    stream_queries = lax.all_to_all(
        queries[own_deal], "ctx", split_axis=0, concat_axis=0, tiled=True
    )
    all_pairs = lax.all_gather(pairs, "ctx", axis=0, tiled=True)
    window_pairs = all_pairs[given_row]

    def block_scores(offset):
        query_block = lax.dynamic_slice_in_dim(stream_queries, offset, QBLK, 0).reshape(
            QBLK * H, HD
        )
        pair_block = lax.dynamic_slice_in_dim(window_pairs, offset, key_span, 0)
        seg_query = lax.dynamic_slice_in_dim(segment, WINDOW + offset, QBLK, 0)
        seg_key = lax.dynamic_slice_in_dim(segment, offset, key_span, 0)
        allowed = (seg_query[:, None] == seg_key[None, :]) & (distance >= 0) & (distance < WINDOW)
        scores = (matmul_right(query_block, pair_block[:, :HD]) * score_scale).reshape(
            QBLK, H, key_span
        )
        return (query_block, pair_block, scores, allowed[:, None, :])

    def forward_block(carry, offset):
        query_block, pair_block, scores, allowed = block_scores(offset)
        scores = jnp.where(allowed, scores, neg_large)
        row_max = jnp.max(scores, axis=-1, keepdims=True)
        raised = jnp.exp(scores - row_max)
        row_total = jnp.sum(raised, axis=-1, keepdims=True)
        attn_probs = (raised / row_total).astype(jnp.bfloat16).reshape(QBLK * H, key_span)
        context_block = (
            matmul(attn_probs, pair_block[:, HD:]).astype(jnp.bfloat16).reshape(QBLK, H * HD)
        )
        return (carry, (context_block, row_max + jnp.log(row_total)))

    _, (context_blocks, log_totals) = lax.scan(forward_block, 0, offsets)
    stream_context = context_blocks.reshape(tok_rows, H * HD)
    log_totals = log_totals.reshape(tok_rows, H, 1)
    context = lax.all_to_all(stream_context, "ctx", split_axis=0, concat_axis=0, tiled=True)[
        inverse
    ]
    resid = inputs + matmul(context, w_out)
    normed_mlp = rms_norm(resid, gain_two.astype(jnp.float32)).astype(jnp.bfloat16)
    gate = matmul(normed_mlp, w_gate)
    upward = matmul(normed_mlp, w_up)
    hidden = gated_gelu(gate, upward).astype(jnp.bfloat16)
    block_output = (resid + matmul(hidden, w_down)).astype(jnp.bfloat16)
    gain_two, w_gate, w_up, w_down = (
        lax.all_gather(mlp_gain, "fsdp", axis=0, tiled=True),
        lax.all_gather(gate_weight, "fsdp", axis=0, tiled=True),
        lax.all_gather(up_weight, "fsdp", axis=0, tiled=True),
        lax.all_gather(down_weight, "fsdp", axis=0, tiled=True),
    )
    cot_low = cotangent[0]
    down_grad = matmul_left(hidden, cot_low)
    d_hidden = matmul_right(cot_low, w_down)
    _, pull_gate = jax.vjp(gated_gelu, gate, upward)
    d_gate, d_upward = pull_gate(d_hidden)
    d_gate = d_gate.astype(jnp.bfloat16)
    d_upward = d_upward.astype(jnp.bfloat16)
    gate_grad = matmul_left(normed_mlp, d_gate)
    upward_grad = matmul_left(normed_mlp, d_upward)
    d_normed_mlp = matmul_right(d_gate, w_gate) + matmul_right(d_upward, w_up)
    _, pull_second = jax.vjp(rms_norm, resid, gain_two.astype(jnp.float32))
    d_resid_part, mlp_gain_grad = pull_second(d_normed_mlp)
    mlp_summed = (
        lax.psum_scatter(mlp_gain_grad, ("ctx", "fsdp"), scatter_dimension=0, tiled=True),
        lax.psum_scatter(gate_grad, ("ctx", "fsdp"), scatter_dimension=0, tiled=True),
        lax.psum_scatter(upward_grad, ("ctx", "fsdp"), scatter_dimension=0, tiled=True),
        lax.psum_scatter(down_grad, ("ctx", "fsdp"), scatter_dimension=0, tiled=True),
    )
    d_resid = cot_low.astype(jnp.float32) + d_resid_part
    d_branch = d_resid.astype(jnp.bfloat16)
    gain_one, w_query, w_kv, w_out = (
        lax.all_gather(attn_gain, "fsdp", axis=0, tiled=True),
        lax.all_gather(query_weight, "fsdp", axis=0, tiled=True),
        lax.all_gather(kv_weight, "fsdp", axis=0, tiled=True),
        lax.all_gather(out_weight, "fsdp", axis=0, tiled=True),
    )
    out_grad = matmul_left(context, d_branch)
    d_context = matmul_right(d_branch, w_out).astype(jnp.bfloat16)
    stream_d_context = lax.all_to_all(
        d_context[own_deal], "ctx", split_axis=0, concat_axis=0, tiled=True
    )

    def backward_block(pair_grads, offset):
        query_block, pair_block, scores, allowed = block_scores(offset)
        log_block = lax.dynamic_slice_in_dim(log_totals, offset, QBLK, 0)
        attn_probs = jnp.where(allowed, jnp.exp(scores - log_block), 0.0).reshape(
            QBLK * H, key_span
        )
        d_block = lax.dynamic_slice_in_dim(stream_d_context, offset, QBLK, 0).reshape(QBLK * H, HD)
        d_values = matmul_left(attn_probs.astype(jnp.bfloat16), d_block)
        d_probs = matmul_right(d_block, pair_block[:, HD:])
        row_delta = jnp.sum(attn_probs * d_probs, axis=1, keepdims=True)
        d_scores = (attn_probs * (d_probs - row_delta)).astype(jnp.bfloat16)
        d_query = (
            (matmul(d_scores, pair_block[:, :HD]) * score_scale)
            .astype(jnp.bfloat16)
            .reshape(QBLK, H * HD)
        )
        d_keys = matmul_left(d_scores, query_block) * score_scale
        earlier = lax.dynamic_slice_in_dim(pair_grads, offset, key_span, 0)
        pair_grads = lax.dynamic_update_slice_in_dim(
            pair_grads, earlier + jnp.concatenate([d_keys, d_values], 1), offset, 0
        )
        return (pair_grads, d_query)

    window_grads, d_query_blocks = lax.scan(
        backward_block, jnp.zeros((WINDOW + tok_rows, 2 * HD), jnp.float32), offsets
    )
    window_grads = jnp.where(inside[:, None], window_grads, 0.0)
    stream_d_query = d_query_blocks.reshape(tok_rows, H * HD)
    d_queries = lax.all_to_all(stream_d_query, "ctx", split_axis=0, concat_axis=0, tiled=True)[
        inverse
    ]
    spread_pairs = jnp.zeros((group_rows, 2 * HD), jnp.float32).at[given_row].add(window_grads)
    d_pairs = lax.psum_scatter(
        spread_pairs.astype(jnp.bfloat16), "ctx", scatter_dimension=0, tiled=True
    )
    query_grad = matmul_left(normed, d_queries)
    kv_grad = matmul_left(normed, d_pairs)
    d_normed = matmul_right(d_queries, w_query) + matmul_right(d_pairs, w_kv)
    _, pull_first = jax.vjp(rms_norm, inputs, gain_one.astype(jnp.float32))
    d_inputs, attn_gain_grad = pull_first(d_normed)
    token_grad = (d_resid + d_inputs)[None]
    attn_summed = (
        lax.psum_scatter(attn_gain_grad, ("ctx", "fsdp"), scatter_dimension=0, tiled=True),
        lax.psum_scatter(query_grad, ("ctx", "fsdp"), scatter_dimension=0, tiled=True),
        lax.psum_scatter(kv_grad, ("ctx", "fsdp"), scatter_dimension=0, tiled=True),
        lax.psum_scatter(out_grad, ("ctx", "fsdp"), scatter_dimension=0, tiled=True),
    )
    return (block_output[None], token_grad) + tuple(attn_summed) + tuple(mlp_summed)


def solution(mesh):
    placed = (
        P("fsdp", "ctx", None),
        P("fsdp", None),
        P("fsdp", None, None),
        P("fsdp"),
        P("fsdp", None),
        P("fsdp", None),
        P("fsdp", None),
        P("fsdp"),
        P("fsdp", None),
        P("fsdp", None),
        P("fsdp", None),
        P("fsdp", "ctx", None),
    )
    return jax.shard_map(
        on_device,
        mesh=mesh,
        in_specs=placed,
        out_specs=(
            P("fsdp", "ctx", None),
            P("fsdp", "ctx", None),
            P(("ctx", "fsdp")),
            P(("ctx", "fsdp"), None),
            P(("ctx", "fsdp"), None),
            P(("ctx", "fsdp"), None),
            P(("ctx", "fsdp")),
            P(("ctx", "fsdp"), None),
            P(("ctx", "fsdp"), None),
            P(("ctx", "fsdp"), None),
        ),
        check_vma=False,
    )
```

profile of v0, /device:TPU:20, one launch (start us, length us, event | category | flops | bytes accessed | tf_op | source)
XLA Modules:
  0.0 3640.1 jit_solution(2765740889056884713)
XLA Ops:
  13.9 18.0 all-gather.10.cloned.1.call-done
  37.4 100.1 %all-gather.8.cloned.1.call-done = bf16[2048,2048]{1,0:T(8,128)(2,1)} async-done(((bf16[1024,2048]{1,0:T(8,128)(2,1)}), bf16[2048,2048]{1,0:T(8,128)(2,1)}) %all-gather.8.cloned.1.call-update) | async-done | bytes 8388624 | tf_op jit(solution)/shard_map/all_gather | solution.py:66
  160.4 27.0 all-gather.12.cloned.1.call-done
  194.3 51.3 %while.32 = (s32[]{:T(128)}, bf16[2,128,2048]{2,1,0:T(8,128)(2,1)}, f32[2,128,16,1]{2,1,3,0:T(8,128)S(1)}, s32[2]{0:T(128)}, s32[1280]{0:T(1024)S(1)}, /*index=5...) while((s32[]{:T(128)}, bf16[2,128,2048]{2,1,0:T(8,128)(2,1)}, ...), condition=%wide.region_6.7_spmd.clone.clone, body=%wide.region_3.6_spmd.clone.clone.sunk | while | flops 1227978752 | bytes 90242960 | solution.py:133
  258.2 17.3 all-to-all-done.1
  276.9 17.4 all-gather.14.cloned.1.call-done
  301.7 287.7 %all-gather.16.cloned.1.call-done = bf16[2048,6144]{1,0:T(8,128)(2,1)} async-done(((bf16[1024,6144]{1,0:T(8,128)(2,1)}), bf16[2048,6144]{1,0:T(8,128)(2,1)}) %all-gather.16.cloned.1.call-update) | async-done | bytes 25165840 | tf_op jit(solution)/shard_map/all_gather | solution.py:70
  589.4 16.7 fusion.76
  606.1 278.4 %all-gather.18.cloned.1.call-done = bf16[2048,6144]{1,0:T(8,128)(2,1)} async-done(((bf16[1024,6144]{1,0:T(8,128)(2,1)}), bf16[2048,6144]{1,0:T(8,128)(2,1)}) %all-gather.18.cloned.1.call-update) | async-done | bytes 25165840 | tf_op jit(solution)/shard_map/all_gather | solution.py:71
  901.2 278.7 %all-gather.20.cloned.1.call-done = bf16[6144,2048]{1,0:T(8,128)(2,1)} async-done(((bf16[3072,2048]{1,0:T(8,128)(2,1)}), bf16[6144,2048]{1,0:T(8,128)(2,1)}) %all-gather.20.cloned.1.call-update) | async-done | bytes 25165840 | tf_op jit(solution)/shard_map/all_gather | solution.py:72
  1179.8 20.7 multiply_convert_fusion.1
  1247.4 23.3 all-to-all-done.2
  1272.9 108.7 %while.33 = (s32[]{:T(128)}, f32[1280,256]{0,1:T(8,128)}, bf16[2,128,2048]{2,1,0:T(8,128)(2,1)}, s32[2]{0:T(128)}, s32[1280]{0:T(1024)S(1)}, /*index=5*/bf16[256...) while((s32[]{:T(128)}, f32[1280,256]{0,1:T(8,128)}, ...), condition=%wide.region_12.13_spmd.clone.clone, body=%wide.region_10.12_spmd.clone.clone.sunk | while | flops 3043276800 | bytes 148971504 | solution.py:206
  1397.7 61.2 %reduce-scatter.8.cloned.1.call-done = bf16[256,256]{1,0:T(8,128)(2,1)} async-done(((bf16[4096,256]{1,0:T(8,128)(2,1)}), bf16[256,256]{1,0:T(8,128)(2,1)}) %reduce-scatter.8.cloned.1.call-update) | async-done | bytes 131088 | tf_op jit(solution)/shard_map/reduce_scatter | solution.py:215
  1472.7 28.7 all_to_all.48
  1512.4 21.4 fusion.80
  1533.9 21.4 fusion.81
  1556.5 21.5 fusion.49
  1599.9 46.1 %all-reduce.2 = (f32[2048]{0:T(1024)S(1)}, f32[2048]{0:T(1024)S(1)}) all-reduce(f32[2048]{0:T(1024)S(1)} %get-tuple-element.336, f32[2048]{0:T(1024)S(1)} %copy-done.34), channel_id=3, replica_groups=mesh['ctx'=16,'fsdp'=2] {'ctx','fsdp'}, use_global_device_ids=true, to_apply=%region_17.18.clone | all-reduce | flops 4096 | bytes 32768
  1651.3 307.3 %reduce-scatter.14.cloned.1.call-done = f32[64,2048]{1,0:T(8,128)} async-done(((f32[2048,2048]{1,0:T(8,128)}), f32[64,2048]{1,0:T(8,128)}) %reduce-scatter.14.cloned.1.call-update) | async-done | bytes 524304 | tf_op jit(solution)/shard_map/reduce_scatter | solution.py:228
  1958.6 361.6 %reduce-scatter.10.cloned.1.call-done = f32[64,2048]{1,0:T(8,128)} async-done(((f32[2048,2048]{1,0:T(8,128)}), f32[64,2048]{1,0:T(8,128)}) %reduce-scatter.10.cloned.1.call-update) | async-done | bytes 524304 | tf_op jit(solution)/shard_map/reduce_scatter | solution.py:226
  2320.2 438.0 %reduce-scatter.16.cloned.1.call-done = f32[64,6144]{1,0:T(8,128)} async-done(((f32[2048,6144]{1,0:T(8,128)}), f32[64,6144]{1,0:T(8,128)}) %reduce-scatter.16.cloned.1.call-update) | async-done | bytes 1572880 | tf_op jit(solution)/shard_map/reduce_scatter | solution.py:165
  2758.3 437.6 %reduce-scatter.18.cloned.1.call-done = f32[64,6144]{1,0:T(8,128)} async-done(((f32[2048,6144]{1,0:T(8,128)}), f32[64,6144]{1,0:T(8,128)}) %reduce-scatter.18.cloned.1.call-update) | async-done | bytes 1572880 | tf_op jit(solution)/shard_map/reduce_scatter | solution.py:166
  3195.9 437.5 %reduce-scatter.20.cloned.1.call-done = f32[192,2048]{1,0:T(8,128)} async-done(((f32[6144,2048]{1,0:T(8,128)}), f32[192,2048]{1,0:T(8,128)}) %reduce-scatter.20.cloned.1.call-update) | async-done | bytes 1572880 | tf_op jit(solution)/shard_map/reduce_scatter | solution.py:167
  (262 shorter events, 339.8 us)
Async XLA Ops:
  7.2 24.7 all-gather.10.cloned.1.call-start
  7.9 129.6 %all-gather.8.cloned.1.call-start = ((), (), s32[]{:S(2)}) async-start(), calls=%async_computation.11 | async-start | bytes 12582912 | tf_op jit(solution)/shard_map/all_gather | solution.py:66
  8.7 178.7 %all-gather.12.cloned.1.call-start = ((), (), s32[]{:S(2)}) async-start(), calls=%async_computation.13 | async-start | bytes 2228224 | tf_op jit(solution)/shard_map/all_gather | solution.py:105
  13.1 124.4 %copy-start.24 = (f32[2048]{0:T(1024)}, f32[2048]{0:T(1024)S(1)}, u32[]{:S(2)}) copy-start(f32[2048]{0:T(1024)S(1)} %convert_element_type.87) | copy-start | bytes 24580
  13.9 123.6 %copy-start.26 = (f32[256]{0:T(256)}, f32[256]{0:T(256)S(1)}, u32[]{:S(2)}) copy-start(f32[256]{0:T(256)S(1)} %fusion.65) | copy-start | bytes 3076
  34.3 259.9 %all-gather.14.cloned.1.call-start = ((), (), s32[]{:S(2)}) async-start(), calls=%async_computation.14 | async-start | bytes 12582912 | tf_op jit(solution)/shard_map/all_gather | solution.py:68
  34.9 554.5 %all-gather.16.cloned.1.call-start = ((), (), s32[]{:S(2)}) async-start(), calls=%async_computation.15 | async-start | bytes 37748736 | tf_op jit(solution)/shard_map/all_gather | solution.py:70
  35.5 849.0 %all-gather.18.cloned.1.call-start = ((), (), s32[]{:S(2)}) async-start(), calls=%async_computation.16 | async-start | bytes 37748736 | tf_op jit(solution)/shard_map/all_gather | solution.py:71
  36.1 1143.7 %all-gather.20.cloned.1.call-start = ((), (), s32[]{:S(2)}) async-start(), calls=%async_computation.17 | async-start | bytes 37748736 | tf_op jit(solution)/shard_map/all_gather | solution.py:72
  37.4 105.8 %copy-start.31 = (s32[1024]{0:T(1024)}, s32[1024]{0:T(1024)S(1)}, u32[]{:S(2)}) copy-start(s32[1024]{0:T(1024)S(1)} %pad_clamp_fusion.3) | copy-start | bytes 12292
  145.6 47.6 %all-to-all-start = ((bf16[16,16,2048]{2,1,0:T(8,128)(2,1)}), bf16[16,16,2048]{2,1,0:T(8,128)(2,1)}, u32[]{:S(2)}, u32[]{:S(2)}) async-start(bf16[16,16,2048]{2,1,0:T(8,128)(2,1)} %bitcast.6), calls=%async_computation | async-start | bytes 2097152 | tf_op jit(solution)/shard_map/all_to_all | solution.py:102
  245.7 29.8 all-to-all-start.1
  301.7 582.9 %copy-start.7 = (bf16[256,2048]{1,0:T(8,128)(2,1)}, bf16[256,2048]{1,0:T(8,128)(2,1)S(1)}, u32[]{:S(2)}) copy-start(bf16[256,2048]{1,0:T(8,128)(2,1)S(1)} %multiply_convert_fusion.3) | copy-start | bytes 3145732
  606.1 573.7 %copy-start.11 = (bf16[1,256,2048]{2,1,0:T(8,128)(2,1)S(1)}, bf16[1,256,2048]{2,1,0:T(8,128)(2,1)}, u32[]{:S(2)}) copy-start(bf16[1,256,2048]{2,1,0:T(8,128)(2,1)} %param.27) | copy-start | bytes 3145732
  1241.3 29.4 all-to-all-start.2
  1247.3 211.6 %reduce-scatter.8.cloned.1.call-start = ((), (), s32[]{:S(2)}) async-start(), calls=%async_computation.18 | async-start | bytes 2228224 | tf_op jit(solution)/shard_map/reduce_scatter | solution.py:215
  1393.8 65.1 %copy-start.25 = (f32[2048]{0:T(1024)S(1)}, f32[2048]{0:T(1024)}, u32[]{:S(2)}) copy-start(f32[2048]{0:T(1024)} %copy-done.24) | copy-start | bytes 24580
  1393.8 65.1 %copy-start.27 = (f32[256]{0:T(256)S(1)}, f32[256]{0:T(256)}, u32[]{:S(2)}) copy-start(f32[256]{0:T(256)} %copy-done.26) | copy-start | bytes 3076
  1397.7 253.6 %reduce-scatter.12.cloned.1.call-start = ((), (), s32[]{:S(2)}) async-start(), calls=%async_computation.20 | async-start | bytes 2162688 | tf_op jit(solution)/shard_map/reduce_scatter | solution.py:227
  1461.7 496.9 %reduce-scatter.14.cloned.1.call-start = ((), (), s32[]{:S(2)}) async-start(), calls=%async_computation.21 | async-start | bytes 17301504 | tf_op jit(solution)/shard_map/reduce_scatter | solution.py:228
  1471.5 848.7 %reduce-scatter.10.cloned.1.call-start = ((), (), s32[]{:S(2)}) async-start(), calls=%async_computation.19 | async-start | bytes 17301504 | tf_op jit(solution)/shard_map/reduce_scatter | solution.py:226
  1511.2 1247.1 %reduce-scatter.16.cloned.1.call-start = ((), (), s32[]{:S(2)}) async-start(), calls=%async_computation.22 | async-start | bytes 51904512 | tf_op jit(solution)/shard_map/reduce_scatter | solution.py:165
  1533.8 1662.1 %reduce-scatter.18.cloned.1.call-start = ((), (), s32[]{:S(2)}) async-start(), calls=%async_computation.23 | async-start | bytes 51904512 | tf_op jit(solution)/shard_map/reduce_scatter | solution.py:166
  1555.3 2078.1 %reduce-scatter.20.cloned.1.call-start = ((), (), s32[]{:S(2)}) async-start(), calls=%async_computation.24 | async-start | bytes 51904512 | tf_op jit(solution)/shard_map/reduce_scatter | solution.py:167
  (41 other events, 477.4 us)
Sparse Core Ops, SparseCore 0:
  9.6 22.3 all-gather.9
  33.5 103.9 all-gather.7
  140.3 47.0 all-gather.11
  188.8 105.3 all-gather.13
  295.6 293.7 all-gather.15
  590.8 293.7 all-gather.17
  886.1 293.7 all-gather.19
  1397.8 61.0 reduce-scatter.7
  1461.8 119.8 reduce-scatter.11
  1584.4 374.1 reduce-scatter.13
  1961.5 358.7 reduce-scatter.9
  2327.1 431.1 reduce-scatter.15
  2765.3 430.5 reduce-scatter.17
  3202.8 430.5 reduce-scatter.19
where the time goes:
time: 3650 us; the launch traced here: 3640 us
  waiting for transfers between devices  3090 us (85%)
  matrix products  269 us (7%)
  local copies, waits for them, and re-layouts  89.9 us (2%)
  blocking collectives  83.6 us (2%)
  other arithmetic  50.2 us (1%)
    reduce_scatter x1, waiting for transfers between devices, on_device(): lax.psum_scatter(gate_grad, ('ctx', 'fsdp'), scatter_dimension=0, tiled=T...  438 us
    reduce_scatter x1, waiting for transfers between devices, on_device(): lax.psum_scatter(upward_grad, ('ctx', 'fsdp'), scatter_dimension=0, tiled...  438 us
    reduce_scatter x1, waiting for transfers between devices, on_device(): lax.psum_scatter(down_grad, ('ctx', 'fsdp'), scatter_dimension=0, tiled=T...  437 us
    reduce_scatter x1, waiting for transfers between devices, on_device(): lax.psum_scatter(query_grad, ('ctx', 'fsdp'), scatter_dimension=0, tiled=...  362 us
    reduce_scatter x1, waiting for transfers between devices, on_device(): lax.psum_scatter(out_grad, ('ctx', 'fsdp'), scatter_dimension=0, tiled=True)  307 us
    all_gather x1, waiting for transfers between devices, on_device(): lax.all_gather(shards[5], 'fsdp', axis=0, tiled=True)  288 us
    all_gather x1, waiting for transfers between devices, on_device(): lax.all_gather(shards[7], 'fsdp', axis=0, tiled=True)  279 us
    all_gather x1, waiting for transfers between devices, on_device(): lax.all_gather(shards[6], 'fsdp', axis=0, tiled=True)  278 us
  transfers between devices with their start and end apart: 17, of which 15 were waited for; matrix products, arithmetic and copies ran while one was open for 6% of the time, Pallas kernels for 0%

commit v1 on v0

v1 whole, which is shorter than its diff:
```python
import functools

import jax
import jax.numpy as jnp
from jax import lax
from jax.experimental import pallas as pl
from jax.experimental.pallas import tpu as pltpu
from jax.sharding import Mesh
from jax.sharding import PartitionSpec as P

H = 16
HD = 128
WINDOW = 1024
QBLK = 128
HEADS_STEP = 4
SPAN = WINDOW + QBLK
ROWS = HEADS_STEP * QBLK

epsilon = 1e-06
neg_large = -1e30
scale = HD ** (-0.5)
BF = jnp.bfloat16
F32 = jnp.float32
CTX = ("a", "b", "c")
ALL = ("a", "b", "c", "x")


def mm(left, right):
    return jnp.dot(left, right, preferred_element_type=F32)


def mm_tn(left, right):
    return lax.dot_general(left, right, (((0,), (0,)), ((), ())), preferred_element_type=F32)


def mm_nt(left, right):
    return lax.dot_general(left, right, (((1,), (1,)), ((), ())), preferred_element_type=F32)


def stack_heads(block):
    return jnp.concatenate([block[:, h * HD : (h + 1) * HD] for h in range(HEADS_STEP)], 0)


def unstack_heads(block_t):
    return jnp.concatenate(
        [block_t[:, h * QBLK : (h + 1) * QBLK].T for h in range(HEADS_STEP)], 1
    )


def bias_of(lo_ref, qb):
    key = lax.broadcasted_iota(jnp.int32, (SPAN, QBLK), 0) + qb * QBLK
    query = lax.broadcasted_iota(jnp.int32, (SPAN, QBLK), 1) + (WINDOW + qb * QBLK)
    allowed = (key >= lo_ref[...]) & (key <= query)
    bias = jnp.where(allowed, 0.0, neg_large).astype(F32)
    return jnp.concatenate([bias] * HEADS_STEP, 1)


def attend_kernel(lo_ref, q_ref, kv_ref, o_ref, lse_ref):
    qb = pl.program_id(0)
    rows = pl.ds(pl.multiple_of(qb * QBLK, QBLK), SPAN)
    keys = kv_ref[rows, :HD]
    values = kv_ref[rows, HD:]
    scores = mm_nt(keys, stack_heads(q_ref[...])) * scale + bias_of(lo_ref, qb)
    top = jnp.max(scores, axis=0, keepdims=True)
    raised = jnp.exp(scores - top)
    total = jnp.sum(raised, axis=0, keepdims=True)
    out_t = mm_tn(values, raised.astype(BF)) * (1.0 / total)
    o_ref[...] = unstack_heads(out_t).astype(BF)
    lse_ref[0] = top + jnp.log(total)


def attend_back_kernel(lo_ref, q_ref, kv_ref, do_ref, lse_ref, dq_ref, dkv_ref):
    qb = pl.program_id(0)

    @pl.when((qb == 0) & (pl.program_id(1) == 0))
    def _():
        dkv_ref[...] = jnp.zeros_like(dkv_ref)

    rows = pl.ds(pl.multiple_of(qb * QBLK, QBLK), SPAN)
    keys = kv_ref[rows, :HD]
    values = kv_ref[rows, HD:]
    queries = stack_heads(q_ref[...])
    d_out = stack_heads(do_ref[...])
    scores = mm_nt(keys, queries) * scale + bias_of(lo_ref, qb)
    probs = jnp.exp(scores - lse_ref[0])
    d_probs = mm_nt(values, d_out)
    delta = jnp.sum(probs * d_probs, axis=0, keepdims=True)
    d_scores = (probs * (d_probs - delta)).astype(BF)
    dq_ref[...] = unstack_heads(mm_tn(keys, d_scores) * scale).astype(BF)
    dkv_ref[rows, :HD] += mm(d_scores, queries) * scale
    dkv_ref[rows, HD:] += mm(probs.astype(BF), d_out)


def attend(queries, window, low):
    tok = queries.shape[0]
    groups = H // HEADS_STEP
    blocks = tok // QBLK
    return pl.pallas_call(
        attend_kernel,
        grid=(blocks, groups),
        in_specs=[
            pl.BlockSpec((1, QBLK), lambda i, j: (0, i)),
            pl.BlockSpec((QBLK, HEADS_STEP * HD), lambda i, j: (i, j)),
            pl.BlockSpec((WINDOW + tok, 2 * HD), lambda i, j: (0, 0)),
        ],
        out_specs=[
            pl.BlockSpec((QBLK, HEADS_STEP * HD), lambda i, j: (i, j)),
            pl.BlockSpec((1, 1, ROWS), lambda i, j: (i * groups + j, 0, 0)),
        ],
        out_shape=[
            jax.ShapeDtypeStruct((tok, H * HD), BF),
            jax.ShapeDtypeStruct((blocks * groups, 1, ROWS), F32),
        ],
        compiler_params=pltpu.CompilerParams(vmem_limit_bytes=48 * 1024 * 1024),
        cost_estimate=pl.CostEstimate(
            flops=4 * tok * H * HD * SPAN, bytes_accessed=4 * 1024 * 1024, transcendentals=0
        ),
        name="attend",
    )(low, queries, window)


def attend_back(queries, window, low, d_context, lse):
    tok = queries.shape[0]
    groups = H // HEADS_STEP
    blocks = tok // QBLK
    return pl.pallas_call(
        attend_back_kernel,
        grid=(blocks, groups),
        in_specs=[
            pl.BlockSpec((1, QBLK), lambda i, j: (0, i)),
            pl.BlockSpec((QBLK, HEADS_STEP * HD), lambda i, j: (i, j)),
            pl.BlockSpec((WINDOW + tok, 2 * HD), lambda i, j: (0, 0)),
            pl.BlockSpec((QBLK, HEADS_STEP * HD), lambda i, j: (i, j)),
            pl.BlockSpec((1, 1, ROWS), lambda i, j: (i * groups + j, 0, 0)),
        ],
        out_specs=[
            pl.BlockSpec((QBLK, HEADS_STEP * HD), lambda i, j: (i, j)),
            pl.BlockSpec((WINDOW + tok, 2 * HD), lambda i, j: (0, 0)),
        ],
        out_shape=[
            jax.ShapeDtypeStruct((tok, H * HD), BF),
            jax.ShapeDtypeStruct((WINDOW + tok, 2 * HD), F32),
        ],
        compiler_params=pltpu.CompilerParams(vmem_limit_bytes=48 * 1024 * 1024),
        cost_estimate=pl.CostEstimate(
            flops=10 * tok * H * HD * SPAN, bytes_accessed=6 * 1024 * 1024, transcendentals=0
        ),
        name="attend_back",
    )(low, queries, window, d_context, lse)


def ring_order(size_a, size_b):
    if size_b == 1:
        return [a for a in range(size_a)]
    order = [(a, 0) for a in range(size_a)]
    forward = True
    for a in reversed(range(size_a)):
        columns = range(1, size_b) if forward else reversed(range(1, size_b))
        order += [(a, b) for b in columns]
        forward = not forward
    return [a * size_b + b for a, b in order]


def norm_stats(values):
    inv = lax.rsqrt(jnp.mean(values * values, axis=-1, keepdims=True) + epsilon)
    return values * inv, inv


def norm_back(unit, inv, gain, grad):
    scaled = grad * gain
    inner = jnp.mean(scaled * unit, axis=-1, keepdims=True)
    return inv * (scaled - unit * inner), jnp.sum(grad * unit, axis=0)


def on_device(
    sizes,
    tokens,
    lengths,
    dealing,
    attn_gain,
    query_weight,
    kv_weight,
    out_weight,
    mlp_gain,
    gate_weight,
    up_weight,
    down_weight,
    cotangent,
):
    size_a, size_b, size_x = sizes
    chips = size_a * size_b
    n_ctx = chips * 2
    ranks = 2 * size_x
    ia, ib, ic, ix = (lax.axis_index(name) for name in ALL)
    chip = ia * size_b + ib
    own = chip * 2 + ic
    flat = own * size_x + ix
    rank = ix * 2 + ic
    tok = tokens.shape[1]
    width = tokens.shape[2]
    piece = tok // n_ctx
    halo = WINDOW // tok
    swap = [(0, 1), (1, 0)]

    def pick(array, index, axis=0):
        return lax.dynamic_index_in_dim(array, index, axis, keepdims=False)

    def put(array, part, index, axis=0):
        return lax.dynamic_update_index_in_dim(array, part, index, axis)

    def to_core(array):
        return lax.ppermute(array, "c", swap)

    def to_x(array, step):
        return lax.ppermute(array, "x", [(i, (i + step) % size_x) for i in range(size_x)])

    def shift_ctx(array, step):
        pairs = [(i, i + step) for i in range(n_ctx) if 0 <= i + step < n_ctx]
        return lax.ppermute(array, CTX, pairs)

    def from_x(step):
        return (ix + size_x - step) % size_x

    def whole_weight(shard):
        rows, cols = shard.shape
        halves = shard.reshape(2, rows // 2, cols)
        full = jnp.zeros((size_x, 2, rows // 2, cols), shard.dtype)
        full = lax.dynamic_update_slice(full, halves[None], (ix, 0, 0, 0))
        mine = pick(halves, ic)
        for step in range(1, size_x):
            got = to_x(mine, step)
            other = to_core(got)
            full = lax.dynamic_update_slice(full, got[None, None], (from_x(step), ic, 0, 0))
            full = lax.dynamic_update_slice(full, other[None, None], (from_x(step), 1 - ic, 0, 0))
        return full.reshape(size_x * rows, cols)

    def rank_columns(shard):
        rows, cols = shard.shape
        part = cols // ranks
        own_part = lax.dynamic_slice(shard, (0, rank * part), (rows, part))
        full = jnp.zeros((size_x, rows, part), shard.dtype)
        full = put(full, own_part, ix)
        for step in range(1, size_x):
            target = ((ix + step) % size_x) * 2 + ic
            got = to_x(lax.dynamic_slice(shard, (0, target * part), (rows, part)), step)
            full = put(full, got, from_x(step))
        return full.reshape(size_x * rows, part)

    def group_rows(array):
        parts = [array, to_core(array)]
        for step in range(1, size_x):
            got = to_x(array, step)
            parts += [got, to_core(got)]
        return jnp.concatenate(parts, 0)

    def group_columns(array):
        part = array.shape[1] // ranks
        view = array.reshape(tok, size_x, 2, part)
        kept = pick(view, ic, 2)
        got = to_core(pick(view, 1 - ic, 2))
        both = jnp.stack([kept, got])
        parts = [pick(both, ix, 2).reshape(2 * tok, part)]
        for step in range(1, size_x):
            sent = pick(both, (ix + step) % size_x, 2).reshape(2 * tok, part)
            parts.append(to_x(sent, step))
        return jnp.concatenate(parts, 0)

    def group_sum(part_of):
        total = None
        for step in list(range(1, size_x)) + [0]:
            both = part_of(step)
            summed = both[:tok] + to_core(both[tok:].astype(BF)).astype(F32)
            if step:
                summed = to_x(summed.astype(BF), size_x - step).astype(F32)
            total = summed if total is None else total + summed
        return total

    order = ring_order(size_a, size_b)
    place = [order.index(g) for g in range(chips)]
    position = jnp.asarray(place, jnp.int32)[chip]
    onward = [(order[p], order[(p + 1) % chips]) for p in range(chips)]
    backward = [(order[p], order[(p - 1) % chips]) for p in range(chips)]

    def ring_sum(chunks, slots):
        rows = chunks.shape[1]
        chunk_at = jnp.asarray([slots[g] for g in order], jnp.int32)
        half = rows // 2
        held_f = held_b = None
        for step in range(1, chips + 1):
            at_f = chunk_at[(position + 2 * chips - step) % chips]
            at_b = chunk_at[(position + step) % chips]
            part_f = lax.dynamic_slice(
                chunks, (at_f, 0, 0), (1, half, chunks.shape[2])
            )[0].astype(F32)
            part_b = lax.dynamic_slice(
                chunks, (at_b, half, 0), (1, rows - half, chunks.shape[2])
            )[0].astype(F32)
            if step > 1:
                part_f = part_f + held_f.astype(F32)
                part_b = part_b + held_b.astype(F32)
            if step == chips:
                return jnp.concatenate([part_f, part_b], 0)
            held_f = lax.ppermute(part_f.astype(BF), ("a", "b"), onward)
            held_b = lax.ppermute(part_b.astype(BF), ("a", "b"), backward)

    if (size_a, size_b, size_x) == (4, 2, 2):
        slot = [(g % 2) * 4 + ((g // 2) % 2) * 2 + (g // 2) // 2 for g in range(chips)]
    else:
        slot = list(range(chips))
    keep_pairs = []
    for g in range(chips):
        for c in range(2):
            for x in range(size_x):
                keep_pairs.append(((g * 2 + c) * size_x + x, (x * 2 + c) * chips + slot[g]))

    def sum_rows(grad):
        chunks = grad.astype(BF).reshape(chips, grad.shape[0] // chips, grad.shape[1])
        summed = ring_sum(chunks, slot)
        return lax.ppermute(summed.astype(BF), ALL, keep_pairs).astype(F32)

    def sum_columns(grad):
        rows, part = grad.shape
        chunks = grad.astype(BF).reshape(chips, rows // chips, part)
        summed = ring_sum(chunks, list(range(chips))).astype(BF).reshape(2, size_x, rows // (chips * ranks), part)
        both = jnp.zeros((2,) + summed.shape[1:], BF)
        both = put(both, pick(summed, ic), ic)
        both = put(both, to_core(pick(summed, 1 - ic)), 1 - ic)
        full = jnp.zeros((size_x, 2) + summed.shape[2:], BF)
        full = put(full, pick(both, ix, 1), ix)
        for step in range(1, size_x):
            full = put(full, to_x(pick(both, (ix + step) % size_x, 1), step), from_x(step))
        return full.transpose(2, 0, 1, 3).reshape(-1, ranks * part).astype(F32)

    def sum_gain(grad):
        for name, size in (("c", 2), ("x", size_x), ("b", size_b), ("a", size_a)):
            step = 1
            while step < size:
                grad = grad + lax.ppermute(grad, name, [(i, i ^ step) for i in range(size)])
                step *= 2
        part = grad.shape[0] // (n_ctx * size_x)
        return lax.dynamic_slice(grad, (flat * part,), (part,))

    own_deal = pick(dealing[0], own)
    deal = (own_deal[:, None] == jnp.arange(tok, dtype=jnp.int32)[None, :]).astype(BF)

    def to_stream(array):
        return lax.all_to_all(
            mm(deal, array).astype(BF), CTX, split_axis=0, concat_axis=0, tiled=True
        )

    def from_stream(array):
        dealt = lax.all_to_all(array, CTX, split_axis=0, concat_axis=0, tiled=True)
        return mm_tn(deal, dealt)

    gains = whole_weight(jnp.stack([attn_gain, mlp_gain], 1).reshape(-1, 2)).astype(F32)
    gain_one = gains[:, 0]
    gain_two = gains[:, 1]
    inputs_low = to_stream(tokens[0])
    w_query = whole_weight(query_weight)
    w_kv = whole_weight(kv_weight)
    w_out = whole_weight(out_weight)
    cot = to_stream(cotangent[0])
    w_gate = rank_columns(gate_weight)
    w_up = rank_columns(up_weight)
    down_part = down_weight.shape[0] // 2
    w_down = lax.dynamic_slice(down_weight, (ic * down_part, 0), (down_part, width))

    inputs = inputs_low.astype(F32)
    unit_one, inv_one = norm_stats(inputs)
    normed = (unit_one * gain_one).astype(BF)
    pairs = mm(normed, w_kv).astype(BF)
    window = jnp.concatenate([shift_ctx(pairs, halo - j) for j in range(halo)] + [pairs], 0)
    queries = mm(normed, w_query).astype(BF)
    stream = own * tok + jnp.arange(tok, dtype=jnp.int32)
    ends = jnp.cumsum(lengths[0])
    starts = jnp.max(jnp.where(stream[:, None] >= ends[None, :], ends[None, :], 0), axis=1)
    low = jnp.maximum(starts, stream - (WINDOW - 1)) - (own * tok - WINDOW)
    low = low.astype(jnp.int32)[None, :]
    context, lse = attend(queries, window, low)
    resid = inputs + mm(context, w_out)

    unit_two, inv_two = norm_stats(resid)
    normed_mlp = group_rows((unit_two * gain_two).astype(BF))
    cot_rows = group_rows(cot)
    gate = mm(normed_mlp, w_gate)
    upward = mm(normed_mlp, w_up)
    d_hidden = mm_nt(cot_rows, w_down)
    act, pull = jax.vjp(lambda v: jax.nn.gelu(v, approximate=True), gate)
    hidden = (act * upward).astype(BF)
    d_gate = pull(d_hidden * upward)[0].astype(BF)
    d_upward = (d_hidden * act).astype(BF)

    def rows_of(array, step):
        return array[2 * step * tok : 2 * (step + 1) * tok]

    d_normed_mlp = group_sum(
        lambda step: mm_nt(rows_of(d_gate, step), w_gate) + mm_nt(rows_of(d_upward, step), w_up)
    )
    down_grad = sum_rows(mm_tn(hidden, cot_rows))
    gate_grad = sum_columns(mm_tn(normed_mlp, d_gate))
    up_grad = sum_columns(mm_tn(normed_mlp, d_upward))
    branch_mlp = group_sum(lambda step: mm(rows_of(hidden, step), w_down))
    block_output = from_stream((resid + branch_mlp).astype(BF)).astype(BF)
    d_resid_part, mlp_gain_grad = norm_back(unit_two, inv_two, gain_two, d_normed_mlp)
    mlp_gain_grad = sum_gain(mlp_gain_grad)
    d_resid = cot.astype(F32) + d_resid_part
    d_branch = d_resid.astype(BF)

    d_context = mm_nt(d_branch, w_out).astype(BF)
    out_grad = sum_rows(mm_tn(group_columns(context), group_rows(d_branch)))
    d_queries, d_window = attend_back(queries, window, low, d_context, lse)
    d_pairs = d_window[halo * tok :]
    for j in range(halo):
        part = d_window[j * tok : (j + 1) * tok].astype(BF)
        d_pairs = d_pairs + shift_ctx(part, j - halo).astype(F32)
    d_pairs = d_pairs.astype(BF)
    normed_rows = group_rows(normed)
    query_grad = sum_columns(mm_tn(normed_rows, group_columns(d_queries)))
    kv_part = width // ranks
    normed_part = lax.dynamic_slice(normed_rows, (0, rank * kv_part), (ranks * tok, kv_part))
    kv_grad = sum_rows(mm_tn(normed_part, group_rows(d_pairs)))
    d_normed = mm_nt(d_queries, w_query) + mm_nt(d_pairs, w_kv)
    d_inputs, attn_gain_grad = norm_back(unit_one, inv_one, gain_one, d_normed)
    attn_gain_grad = sum_gain(attn_gain_grad)
    token_grad = from_stream((d_resid + d_inputs).astype(BF))
    return (
        block_output[None],
        token_grad[None],
        attn_gain_grad,
        query_grad,
        kv_grad,
        out_grad,
        mlp_gain_grad,
        gate_grad,
        up_grad,
        down_grad,
    )


def solution(mesh):
    n_ctx, size_x = mesh.shape["ctx"], mesh.shape["fsdp"]
    chips = n_ctx // 2
    size_a = 4 if chips % 4 == 0 else chips
    size_b = chips // size_a
    fine = Mesh(mesh.devices.reshape(size_a, size_b, 2, size_x), ALL)
    rows = P("x", CTX, None)
    split = P("x", None)
    every = P(ALL)
    matrix = P(ALL, None)
    return jax.shard_map(
        functools.partial(on_device, (size_a, size_b, size_x)),
        mesh=fine,
        in_specs=(
            rows,
            split,
            P("x", None, None),
            P("x"),
            split,
            split,
            split,
            P("x"),
            split,
            split,
            split,
            rows,
        ),
        out_specs=(rows, rows, every, matrix, matrix, matrix, every, matrix, matrix, matrix),
        check_vma=False,
    )
```

time: 3650 us -> 1100 us (0.30)
  waiting for transfers between devices: 3090 us -> 443 us
  starting transfers between devices: 19.7 us -> 219 us
  matrix products: 269 us -> 145 us
  blocking collectives: 83.6 us -> 0 us
  between operations: 14.5 us -> 70.9 us
    reduce_scatter x7 -> x0, waiting for transfers between devices: 2040 us -> none  [the longest x1 438 us: on_device(): lax.psum_scatter(gate_grad, ('ctx', 'fsdp'), scatter_dimension=0, tiled=T...]
    all_gather x7 -> x0, waiting for transfers between devices: 1010 us -> none  [the longest x1 288 us: on_device(): lax.all_gather(shards[5], 'fsdp', axis=0, tiled=True)]
    ppermute x0 -> x146, waiting for transfers between devices: none -> 429 us  [the longest x42 172 us: ring_sum(): held_f = lax.ppermute(part_f.astype(BF), ('a', 'b'), onward)]
    ppermute x0 -> x146, starting transfers between devices: none -> 194 us  [the longest x42 52.8 us: ring_sum(): held_b = lax.ppermute(part_b.astype(BF), ('a', 'b'), backward)]
    dot_general x32 -> x25, matrix products: 269 us -> 145 us  [the longest x9 54.2 us: mm(): return jnp.dot(left, right, preferred_element_type=F32)]
    unnamed x1 -> x0, blocking collectives: 46.1 us -> none
  transfers between devices with their start and end apart: 17 -> 150, of which waited for: 15 -> 65; matrix products, arithmetic and copies ran while one was open for 6% -> 21% of each run, Pallas kernels for 0% -> 3%
where the time goes in v1:
time: 1100 us; the launch traced here: 1080 us
  waiting for transfers between devices  443 us (40%)
  starting transfers between devices  219 us (20%)
  matrix products  145 us (13%)
  local copies, waits for them, and re-layouts  99.1 us (9%)
  other arithmetic  78.1 us (7%)
  between operations  70.9 us (6%)
  Pallas kernels  27.4 us (2%)
    ppermute x42, waiting for transfers between devices, ring_sum(): held_f = lax.ppermute(part_f.astype(BF), ('a', 'b'), onward)  172 us
    ppermute x18, waiting for transfers between devices, to_x(): lax.ppermute(array, 'x', [(i, (i + step) % size_x) for i in range(size_x)])  125 us
    ppermute x42, waiting for transfers between devices, ring_sum(): held_b = lax.ppermute(part_b.astype(BF), ('a', 'b'), backward)  110 us
    dot_general x9, matrix products, mm(): return jnp.dot(left, right, preferred_element_type=F32)  54.2 us
    ppermute x42, starting transfers between devices, ring_sum(): held_b = lax.ppermute(part_b.astype(BF), ('a', 'b'), backward)  52.8 us
    dot_general x8, matrix products, mm_nt(): lax.dot_general(left, right, (((1,), (1,)), ((), ())), preferred_element_...  51.6 us
    ppermute x42, starting transfers between devices, ring_sum(): held_f = lax.ppermute(part_f.astype(BF), ('a', 'b'), onward)  40.8 us
    dot_general x8, matrix products, mm_tn(): lax.dot_general(left, right, (((0,), (0,)), ((), ())), preferred_element_...  39.7 us
  transfers between devices with their start and end apart: 150, of which 65 were waited for; matrix products, arithmetic and copies ran while one was open for 21% of the time, Pallas kernels for 3%

profile of v1, /device:TPU:20, one launch (start us, length us, event | category | flops | bytes accessed | tf_op | source)
XLA Modules:
  0.0 1083.0 jit_solution(10190158207150194553)
XLA Ops:
  139.3 14.1 %all-to-all-done.2 = bf16[16,16,2048]{2,1,0:T(8,128)(2,1)} async-done(((bf16[16,16,2048]{2,1,0:T(8,128)(2,1)}), bf16[16,16,2048]{2,1,0:T(8,128)(2,1)}, u32[]{:S(2)}, u32[]{:S(2)}) %all-to-all-start.2) | async-done | bytes 1048608 | tf_op jit(solution)/shard_map/all_to_all | solution.py:347
  189.4 10.7 attend.1
  207.0 40.2 %collective-permute-done.16 = bf16[1024,1536]{1,0:T(8,128)(2,1)} collective-permute-done((bf16[1024,1536]{1,0:T(8,128)(2,1)}, bf16[1024,1536]{1,0:T(8,128)(2,1)}, u32[]{:S(2)}, u32[]{:S(2)}) %collective-permute-start.16) | collective-permute-done | bytes 3145760 | tf_op jit(solution)/shard_map/ppermute | solution.py:215
  250.9 63.7 %collective-permute-done.15 = bf16[1024,1536]{1,0:T(8,128)(2,1)} collective-permute-done((bf16[1024,1536]{1,0:T(8,128)(2,1)}, bf16[1024,1536]{1,0:T(8,128)(2,1)}, u32[]{:S(2)}, u32[]{:S(2)}) %collective-permute-start.15) | collective-permute-done | bytes 3145760 | tf_op jit(solution)/shard_map/ppermute | solution.py:215
  323.2 12.5 %collective-permute-done.13 = bf16[256,2048]{1,0:T(8,128)(2,1)} collective-permute-done((bf16[256,2048]{1,0:T(8,128)(2,1)}, bf16[256,2048]{1,0:T(8,128)(2,1)}, u32[]{:S(2)}, u32[]{:S(2)}) %collective-permute-start.13) | collective-permute-done | bytes 1048608 | tf_op jit(solution)/shard_map/ppermute | solution.py:215
  335.7 13.1 %fusion.7 = f32[1024,1536]{1,0:T(8,128)} fusion(bf16[3072,2048]{1,0:T(8,128)(2,1)} %param.29, s32[]{:T(128)S(6)} %select_n.787, bf16[256,2048]{1,0:T(8,128)(2,1)} %collective-permute-done.22, bf16[256,2048]{1,0:T(8,128)(2,1)} %collective-permute-done.21, bf16[256,2048]{1,0:T(8,128)(2,1)} %collective-permute-done.20, bf16[256,2048]{1,0:T(8,128)(2,1)} %bitcast.42), kind=kOutput, calls=%fused_computation.15 | convolution fusion | flops 6459228160 | bytes 16777220 | tf_op jit(solution)/shard_map/dot_general | solution.py:37
  350.1 14.3 %fusion.174 = f32[1024,1536]{1,0:T(8,128)} fusion(bf16[2048,1536]{1,0:T(8,128)(2,1)} %bitcast.36, bf16[256,2048]{1,0:T(8,128)(2,1)S(1)} %collective-permute-done.14, bf16[256,2048]{1,0:T(8,128)(2,1)} %collective-permute-done.13, bf16[256,2048]{1,0:T(8,128)(2,1)} %collective-permute-done.12, bf16[256,2048]{1,0:T(8,128)(2,1)} %multiply_convert_fusion.3), kind=kOutput, calls=%fused_computation.409 | convolution fusion | flops 6459228160 | bytes 16777216 | tf_op jit(solution)/shard_map/dot_general | solution.py:29
  364.4 17.9 %fusion.6 = (bf16[1024,1536]{1,0:T(8,128)(2,1)}, bf16[1024,1536]{1,0:T(8,128)(2,1)}, bf16[1024,1536]{1,0:T(8,128)(2,1)}) fusion(f32[1024,1536]{1,0:T(8,128)} %fusion.7, f32[1024,1536]{1,0:T(8,128)} %fusion.174, bf16[2048,1536]{1,0:T(8,128)(2,1)S(1)} %bitcast.553, bf16[256,2048]{1,0:T(8,128)(2,1)} %copy-done.61, ...), kind=kOutput, calls=%fused_computation.11 | convolution fusion | flops 6500122624 | bytes 32505856 | tf_op jit(solution)/shard_map/dot_general | solution.py:29
  382.4 8.9 fusion.34
  391.3 8.0 fusion.31
  409.5 8.7 convolution_convert_fusion
  423.6 8.5 convolution_convert_fusion.1
  434.9 8.7 convolution_convert_fusion.2
  467.0 9.8 collective-permute-done.116
  478.3 8.9 collective-permute-done.132
  500.4 16.7 %collective-permute-done.117 = bf16[128,1536]{1,0:T(8,128)(2,1)S(1)} collective-permute-done((bf16[128,1536]{1,0:T(8,128)(2,1)S(1)}, bf16[128,1536]{1,0:T(8,128)(2,1)S(1)}, u32[]{:S(2)}, u32[]{:S(2)}) %collective-permute-start.117) | collective-permute-done | bytes 393248 | tf_op jit(solution)/shard_map/ppermute | solution.py:303
  545.3 8.7 collective-permute-done.134
  578.2 16.7 %attend_back.1 = (bf16[256,2048]{1,0:T(8,128)(2,1)S(1)}, f32[1280,256]{1,0:T(8,128)S(1)}) custom-call(s32[1,256]{1,0:T(1,128)S(1)} %maximum_subtract_fusion.lo_ref, bf16[256,2048]{1,0:T(8,128)(2,1)S(1)} %copy-done.5, bf16[1280,256]{1,0:T(8,128)(2,1)S(1)} %copy-done.3, bf16[256,2048]{1,0:T(8,128)(2,1)S(1)} %convolution_convert_fusion.7.do_ref, ...), custom_call_target="tpu_custom_call" | custom-call | flops 6039797760 | bytes 6291456 | tf_op jit(solution)/shard_map/attend_back/pallas_call | solution.py:126
  652.9 15.6 %collective-permute-start.33 = (f32[2048]{0:T(1024)S(1)}, f32[2048]{0:T(1024)S(1)}, u32[]{:S(2)}, u32[]{:S(2)}) collective-permute-start(f32[2048]{0:T(1024)S(1)} %add.1287), channel_id=1, source_target_pairs={{0,8},{8,0},{16,24},{24,16},{1,9},{9,1},{17,25},{25,17},{2,10},{10... | collective-permute-start | bytes 24584 | tf_op jit(solution)/shard_map/ppermute | solution.py:338
  684.6 13.7 %collective-permute-done.104 = bf16[128,1536]{1,0:T(8,128)(2,1)S(1)} collective-permute-done((bf16[128,1536]{1,0:T(8,128)(2,1)S(1)}, bf16[128,1536]{1,0:T(8,128)(2,1)S(1)}, u32[]{:S(2)}, u32[]{:S(2)}) %collective-permute-start.104) | collective-permute-done | bytes 393248 | tf_op jit(solution)/shard_map/ppermute | solution.py:303
  762.1 8.4 collective-permute-done.124
  829.6 21.5 %collective-permute-done.61 = bf16[32,256]{1,0:T(8,128)(2,1)S(1)} collective-permute-done((bf16[32,256]{1,0:T(8,128)(2,1)S(1)}, bf16[32,256]{1,0:T(8,128)(2,1)S(1)}, u32[]{:S(2)}, u32[]{:S(2)}) %collective-permute-start.61) | collective-permute-done | bytes 16416 | tf_op jit(solution)/shard_map/ppermute | solution.py:303
  1007.2 12.8 %collective-permute-start.90 = (bf16[32,2048]{1,0:T(8,128)(2,1)S(1)}, bf16[32,2048]{1,0:T(8,128)(2,1)S(1)}, u32[]{:S(2)}, u32[]{:S(2)}) collective-permute-start(bf16[32,2048]{1,0:T(8,128)(2,1)S(1)} %fusion.104), channel_id=1, source_target_pairs={{0,4},{8,0},{16,8},{24,16},{28,24},{20,28},{12,20},{4,12},{1,5},{9... | collective-permute-start | bytes 393224 | tf_op jit(solution)/shard_map/ppermute | solution.py:304
  1023.1 11.8 %collective-permute-start.130 = (bf16[2,64,1536]{2,1,0:T(8,128)(2,1)S(1)}, bf16[2,64,1536]{2,1,0:T(8,128)(2,1)S(1)}, u32[]{:S(2)}, u32[]{:S(2)}) collective-permute-start(bf16[2,64,1536]{2,1,0:T(8,128)(2,1)S(1)} %dynamic-slice_bitcast_fusion.4), channel_id=1, source_target_pairs={{0,1},{1,0},{2,3},{3,2},{4,5},{5,4},{6,7},{7,6},{8,9},{9,8},{10,11... | collective-permute-start | bytes 1179656 | tf_op jit(solution)/shard_map/ppermute | solution.py:215
  (687 shorter events, 638.1 us)
Async XLA Ops:
  1.7 121.7 %collective-permute-start.4 = (bf16[512,256]{1,0:T(8,128)(2,1)S(1)}, bf16[512,256]{1,0:T(8,128)(2,1)}, u32[]{:S(2)}, u32[]{:S(2)}) collective-permute-start(bf16[512,256]{1,0:T(8,128)(2,1)S(1)} %dynamic-slice_bitcast_fusion.12), channel_id=1, source_target_pairs={{0,1},{1,0},{2,3},{3,2},{4,5},{5,4},{6,7},{7,6},{8,9},{9,8},{10,11... | collective-permute-start | bytes 786440 | tf_op jit(solution)/shard_map/ppermute | solution.py:215
  4.7 99.3 %collective-permute-start = (bf16[512,2]{0,1:T(2,128)(2,1)S(1)}, bf16[512,2]{0,1:T(2,128)(2,1)S(1)}, u32[]{:S(2)}, u32[]{:S(2)}) collective-permute-start(bf16[512,2]{0,1:T(2,128)(2,1)S(1)} %bitcast.674), channel_id=1, source_target_pairs={{0,1},{1,0},{2,3},{3,2},{4,5},{5,4},{6,7},{7,6},{8,9},{9,8},{10,11... | collective-permute-start | bytes 6152 | tf_op jit(solution)/shard_map/ppermute | solution.py:215
  7.5 116.5 %all-to-all-start = ((bf16[16,16,2048]{2,1,0:T(8,128)(2,1)}), bf16[16,16,2048]{2,1,0:T(8,128)(2,1)S(1)}, u32[]{:S(2)}, u32[]{:S(2)}) async-start(bf16[16,16,2048]{2,1,0:T(8,128)(2,1)} %bitcast.2), calls=%async_computation | async-start | bytes 2097152 | tf_op jit(solution)/shard_map/all_to_all | solution.py:347
  16.9 114.4 %collective-permute-start.2 = (bf16[512,2048]{1,0:T(8,128)(2,1)}, bf16[512,2048]{1,0:T(8,128)(2,1)}, u32[]{:S(2)}, u32[]{:S(2)}) collective-permute-start(bf16[512,2048]{1,0:T(8,128)(2,1)} %dynamic-slice_bitcast_fusion.1), channel_id=1, source_target_pairs={{0,1},{1,0},{2,3},{3,2},{4,5},{5,4},{6,7},{7,6},{8,9},{9,8},{10,11... | collective-permute-start | bytes 6291464 | tf_op jit(solution)/shard_map/ppermute | solution.py:215
  19.9 134.9 %collective-permute-start.10 = (bf16[512,2048]{1,0:T(8,128)(2,1)}, bf16[512,2048]{1,0:T(8,128)(2,1)}, u32[]{:S(2)}, u32[]{:S(2)}) collective-permute-start(bf16[512,2048]{1,0:T(8,128)(2,1)} %dynamic-slice_bitcast_fusion), channel_id=1, source_target_pairs={{0,1},{1,0},{2,3},{3,2},{4,5},{5,4},{6,7},{7,6},{8,9},{9,8},{10,11... | collective-permute-start | bytes 6291464 | tf_op jit(solution)/shard_map/ppermute | solution.py:215
  170.6 76.6 %collective-permute-start.16 = (bf16[1024,1536]{1,0:T(8,128)(2,1)}, bf16[1024,1536]{1,0:T(8,128)(2,1)}, u32[]{:S(2)}, u32[]{:S(2)}) collective-permute-start(bf16[1024,1536]{1,0:T(8,128)(2,1)} %constant_dynamic-slice_fusion.21), channel_id=1, source_target_pairs={{0,1},{1,0},{2,3},{3,2},{4,5},{5,4},{6,7},{7,6},{8,9},{9,8},{10,11... | collective-permute-start | bytes 9437192 | tf_op jit(solution)/shard_map/ppermute | solution.py:215
  171.6 143.0 %collective-permute-start.15 = (bf16[1024,1536]{1,0:T(8,128)(2,1)}, bf16[1024,1536]{1,0:T(8,128)(2,1)}, u32[]{:S(2)}, u32[]{:S(2)}) collective-permute-start(bf16[1024,1536]{1,0:T(8,128)(2,1)} %constant_dynamic-slice_fusion.22), channel_id=1, source_target_pairs={{0,1},{1,0},{2,3},{3,2},{4,5},{5,4},{6,7},{7,6},{8,9},{9,8},{10,11... | collective-permute-start | bytes 9437192 | tf_op jit(solution)/shard_map/ppermute | solution.py:215
  179.8 155.9 %collective-permute-start.20 = (bf16[256,2048]{1,0:T(8,128)(2,1)}, bf16[256,2048]{1,0:T(8,128)(2,1)}, u32[]{:S(2)}, u32[]{:S(2)}) collective-permute-start(bf16[256,2048]{1,0:T(8,128)(2,1)} %bitcast.42), channel_id=1, source_target_pairs={{0,2},{2,0},{1,3},{3,1},{4,6},{6,4},{5,7},{7,5},{8,10},{10,8},{9,1... | collective-permute-start | bytes 3145736 | tf_op jit(solution)/shard_map/ppermute | solution.py:212
  179.8 155.9 %collective-permute-start.22 = (bf16[256,2048]{1,0:T(8,128)(2,1)}, bf16[256,2048]{1,0:T(8,128)(2,1)}, u32[]{:S(2)}, u32[]{:S(2)}) collective-permute-start(bf16[256,2048]{1,0:T(8,128)(2,1)} %collective-permute-done.21), channel_id=1, source_target_pairs={{0,2},{2,0},{1,3},{3,1},{4,6},{6,4},{5,7},{7,5},{8,10},{10,8},{9,1... | collective-permute-start | bytes 3145736 | tf_op jit(solution)/shard_map/ppermute | solution.py:212
  205.5 130.2 %collective-permute-start.13 = (bf16[256,2048]{1,0:T(8,128)(2,1)}, bf16[256,2048]{1,0:T(8,128)(2,1)}, u32[]{:S(2)}, u32[]{:S(2)}) collective-permute-start(bf16[256,2048]{1,0:T(8,128)(2,1)} %multiply_convert_fusion.3), channel_id=1, source_target_pairs={{0,1},{1,0},{2,3},{3,2},{4,5},{5,4},{6,7},{7,6},{8,9},{9,8},{10,11... | collective-permute-start | bytes 3145736 | tf_op jit(solution)/shard_map/ppermute | solution.py:215
  459.6 109.2 %collective-permute-start.25 = (bf16[256,2048]{1,0:T(8,128)(2,1)S(1)}, bf16[256,2048]{1,0:T(8,128)(2,1)S(1)}, u32[]{:S(2)}, u32[]{:S(2)}) collective-permute-start(bf16[256,2048]{1,0:T(8,128)(2,1)S(1)} %slice.151), channel_id=1, source_target_pairs={{0,2},{2,0},{1,3},{3,1},{4,6},{6,4},{5,7},{7,5},{8,10},{10,8},{9,1... | collective-permute-start | bytes 3145736 | tf_op jit(solution)/shard_map/ppermute | solution.py:212
  465.0 104.8 %collective-permute-start.19 = (bf16[256,2048]{1,0:T(8,128)(2,1)S(1)}, bf16[256,2048]{1,0:T(8,128)(2,1)S(1)}, u32[]{:S(2)}, u32[]{:S(2)}) collective-permute-start(bf16[256,2048]{1,0:T(8,128)(2,1)S(1)} %slice.153), channel_id=1, source_target_pairs={{0,2},{2,0},{1,3},{3,1},{4,6},{6,4},{5,7},{7,5},{8,10},{10,8},{9,1... | collective-permute-start | bytes 3145736 | tf_op jit(solution)/shard_map/ppermute | solution.py:212
  614.2 236.9 %collective-permute-start.75 = (bf16[512,512]{1,0:T(8,128)(2,1)}, bf16[512,512]{1,0:T(8,128)(2,1)}, u32[]{:S(2)}, u32[]{:S(2)}) collective-permute-start(bf16[512,512]{1,0:T(8,128)(2,1)} %bitcast.143), channel_id=1, source_target_pairs={{0,1},{1,0},{2,3},{3,2},{4,5},{5,4},{6,7},{7,6},{8,9},{9,8},{10,11... | collective-permute-start | bytes 1572872 | tf_op jit(solution)/shard_map/ppermute | solution.py:215
  616.0 108.8 %collective-permute-start.138 = (bf16[96,2048]{1,0:T(8,128)(2,1)}, bf16[96,2048]{1,0:T(8,128)(2,1)}, u32[]{:S(2)}, u32[]{:S(2)}) collective-permute-start(bf16[96,2048]{1,0:T(8,128)(2,1)} %get-tuple-element.30), channel_id=1, source_target_pairs={{0,4},{8,0},{16,8},{24,16},{28,24},{20,28},{12,20},{4,12},{1,5},{9... | collective-permute-start | bytes 1179656 | tf_op jit(solution)/shard_map/ppermute | solution.py:304
  616.2 87.5 %collective-permute-start.122 = (bf16[128,1536]{1,0:T(8,128)(2,1)S(1)}, bf16[128,1536]{1,0:T(8,128)(2,1)}, u32[]{:S(2)}, u32[]{:S(2)}) collective-permute-start(bf16[128,1536]{1,0:T(8,128)(2,1)S(1)} %copy-done.40), channel_id=1, source_target_pairs={{0,4},{8,0},{16,8},{24,16},{28,24},{20,28},{12,20},{4,12},{1,5},{9... | collective-permute-start | bytes 1179656 | tf_op jit(solution)/shard_map/ppermute | solution.py:304
  639.7 182.4 %all-to-all-start.1 = ((bf16[16,16,2048]{2,1,0:T(8,128)(2,1)}), bf16[16,16,2048]{2,1,0:T(8,128)(2,1)S(1)}, u32[]{:S(2)}, u32[]{:S(2)}) async-start(bf16[16,16,2048]{2,1,0:T(8,128)(2,1)} %bitcast.603), calls=%async_computation.1 | async-start | bytes 2097152 | tf_op jit(solution)/shard_map/all_to_all | solution.py:352
  703.7 110.8 %collective-permute-start.77 = (bf16[256,2048]{1,0:T(8,128)(2,1)}, bf16[256,2048]{1,0:T(8,128)(2,1)}, u32[]{:S(2)}, u32[]{:S(2)}) collective-permute-start(bf16[256,2048]{1,0:T(8,128)(2,1)} %get-tuple-element.22), channel_id=1, source_target_pairs={{0,1},{1,0},{2,3},{3,2},{4,5},{5,4},{6,7},{7,6},{8,9},{9,8},{10,11... | collective-permute-start | bytes 3145736 | tf_op jit(solution)/shard_map/ppermute | solution.py:215
  713.5 59.4 %collective-permute-start.36 = (bf16[256,2048]{1,0:T(8,128)(2,1)S(1)}, bf16[256,2048]{1,0:T(8,128)(2,1)S(1)}, u32[]{:S(2)}, u32[]{:S(2)}) collective-permute-start(bf16[256,2048]{1,0:T(8,128)(2,1)S(1)} %copy-done.33), channel_id=1, source_target_pairs={{0,1},{1,0},{2,3},{3,2},{4,5},{5,4},{6,7},{7,6},{8,9},{9,8},{10,11... | collective-permute-start | bytes 3145736 | tf_op jit(solution)/shard_map/ppermute | solution.py:215
  724.8 73.2 %collective-permute-start.35 = (bf16[256,2048]{1,0:T(8,128)(2,1)S(1)}, bf16[256,2048]{1,0:T(8,128)(2,1)S(1)}, u32[]{:S(2)}, u32[]{:S(2)}) collective-permute-start(bf16[256,2048]{1,0:T(8,128)(2,1)S(1)} %copy-done.33), channel_id=1, source_target_pairs={{0,2},{2,0},{1,3},{3,1},{4,6},{6,4},{5,7},{7,5},{8,10},{10,8},{9,1... | collective-permute-start | bytes 3145736 | tf_op jit(solution)/shard_map/ppermute | solution.py:212
  814.5 57.8 %collective-permute-start.39 = (bf16[512,512]{1,0:T(8,128)(2,1)}, bf16[512,512]{1,0:T(8,128)(2,1)}, u32[]{:S(2)}, u32[]{:S(2)}) collective-permute-start(bf16[512,512]{1,0:T(8,128)(2,1)} %bitcast.50), channel_id=1, source_target_pairs={{0,1},{1,0},{2,3},{3,2},{4,5},{5,4},{6,7},{7,6},{8,9},{9,8},{10,11... | collective-permute-start | bytes 1572872 | tf_op jit(solution)/shard_map/ppermute | solution.py:215
  851.1 52.6 %collective-permute-start.142 = (bf16[96,2048]{1,0:T(8,128)(2,1)}, bf16[96,2048]{1,0:T(8,128)(2,1)}, u32[]{:S(2)}, u32[]{:S(2)}) collective-permute-start(bf16[96,2048]{1,0:T(8,128)(2,1)} %fusion.51), channel_id=1, source_target_pairs={{0,4},{8,0},{16,8},{24,16},{28,24},{20,28},{12,20},{4,12},{1,5},{9... | collective-permute-start | bytes 1179656 | tf_op jit(solution)/shard_map/ppermute | solution.py:304
  881.4 90.6 %collective-permute-start.86 = (bf16[32,2048]{1,0:T(8,128)(2,1)S(1)}, bf16[32,2048]{1,0:T(8,128)(2,1)S(1)}, u32[]{:S(2)}, u32[]{:S(2)}) collective-permute-start(bf16[32,2048]{1,0:T(8,128)(2,1)S(1)} %copy-done.48), channel_id=1, source_target_pairs={{0,4},{8,0},{16,8},{24,16},{28,24},{20,28},{12,20},{4,12},{1,5},{9... | collective-permute-start | bytes 393224 | tf_op jit(solution)/shard_map/ppermute | solution.py:304
  901.8 90.8 %collective-permute-start.47 = (bf16[128,512]{1,0:T(8,128)(2,1)S(1)}, bf16[128,512]{1,0:T(8,128)(2,1)S(1)}, u32[]{:S(2)}, u32[]{:S(2)}) collective-permute-start(bf16[128,512]{1,0:T(8,128)(2,1)S(1)} %get-tuple-element.46), channel_id=1, source_target_pairs={{0,4},{8,0},{16,8},{24,16},{28,24},{20,28},{12,20},{4,12},{1,5},{9... | collective-permute-start | bytes 393224 | tf_op jit(solution)/shard_map/ppermute | solution.py:304
  987.4 90.1 %collective-permute-start.145 = (bf16[192,2048]{1,0:T(8,128)(2,1)}, bf16[192,2048]{1,0:T(8,128)(2,1)}, u32[]{:S(2)}, u32[]{:S(2)}) collective-permute-start(bf16[192,2048]{1,0:T(8,128)(2,1)} %pad_maximum_fusion.5), channel_id=1, source_target_pairs={{0,0},{1,16},{2,8},{3,24},{4,4},{5,20},{6,12},{7,28},{8,2},{9,18},... | collective-permute-start | bytes 2359304 | tf_op jit(solution)/shard_map/ppermute | solution.py:319
  (207 other events, 4119.0 us)

commit v2 on v1

--- a/solution.py
+++ b/solution.py
@@ -23,6 +23,7 @@
 F32 = jnp.float32
 CTX = ("a", "b", "c")
 ALL = ("a", "b", "c", "x")
+MESH = pl.DeviceIdType.MESH
 
 
 def mm(left, right):
@@ -149,16 +150,241 @@
     )(low, queries, window, d_context, lse)
 
 
-def ring_order(size_a, size_b):
+def snake(pos, size_a, size_b):
     if size_b == 1:
-        return [a for a in range(size_a)]
-    order = [(a, 0) for a in range(size_a)]
-    forward = True
-    for a in reversed(range(size_a)):
-        columns = range(1, size_b) if forward else reversed(range(1, size_b))
-        order += [(a, b) for b in columns]
-        forward = not forward
-    return [a * size_b + b for a, b in order]
+        return pos, pos * 0
+    down = pos // size_a
+    first = 1 - (down + 7) // 8
+    q = (pos - size_a) * (1 - first)
+    a_up = size_a - 1 - q // (size_b - 1)
+    k = q % (size_b - 1)
+    odd = a_up % 2
+    b_up = odd * (1 + k) + (1 - odd) * (size_b - 1 - k)
+    return first * pos + (1 - first) * a_up, (1 - first) * b_up
+
+
+def snake_place(a, b, size_a, size_b):
+    if size_b == 1:
+        return a
+    moved = (b + size_b - 1) // size_b
+    odd = a % 2
+    along = odd * (b - 1) + (1 - odd) * (size_b - 1 - b)
+    return (1 - moved) * a + moved * (size_a + (size_a - 1 - a) * (size_b - 1) + along)
+
+
+def kept_slot(a, b, size_a, size_b):
+    half = size_a * size_b // 2
+    return (1 - b % 2) * half + a * (size_b // 2) + b // 2
+
+
+class Job:
+    def __init__(self, phase, left, right, rows, cols, by_rank):
+        self.phase, self.left, self.right = phase, left, right
+        self.rows, self.cols, self.by_rank = rows, cols, by_rank
+
+
+def grads_kernel(sizes, jobs, n_left, n_right, *refs):
+    size_a, size_b, size_x = sizes
+    chips = size_a * size_b
+    ranks = 2 * size_x
+    count = len(jobs)
+    lefts_in, refs = refs[:n_left], refs[n_left:]
+    rights_in, refs = refs[:n_right], refs[n_right:]
+    outs, refs = refs[:count], refs[count:]
+    lefts, refs = refs[:n_left], refs[n_left:]
+    rights, refs = refs[:n_right], refs[n_right:]
+    recv, refs = refs[:count], refs[count:]
+    send, refs = refs[:count], refs[count:]
+    done, refs = refs[:count], refs[count:]
+    load_sem, send_sem, recv_sem, done_send, done_recv, own_sem = refs
+    ia, ib, ic, ix = (lax.axis_index(name) for name in ALL)
+    rank = ix * 2 + ic
+    place = snake_place(ia, ib, size_a, size_b)
+
+    def on_ring(step):
+        return snake((place + 2 * chips + step) % chips, size_a, size_b)
+
+    def member(k):
+        return (ic + k // size_x) % 2, (ix + k % size_x) % size_x
+
+    kept = rank * chips + kept_slot(ia, ib, size_a, size_b)
+    kept_chip = kept // ranks
+    kept_id = (kept_chip // size_b, kept_chip % size_b, (kept // size_x) % 2, kept % size_x)
+    flat = ((ia * size_b + ib) * 2 + ic) * size_x + ix
+    from_rank = flat // chips
+    from_slot = flat % chips
+    half = chips // 2
+    from_id = (
+        (from_slot % half) // (size_b // 2),
+        ((from_slot % half) % (size_b // 2)) * 2 + 1 - from_slot // half,
+        from_rank % 2,
+        from_rank // 2,
+    )
+
+    loads = []
+    for i, (src, dst) in enumerate(zip(lefts_in + rights_in, lefts + rights)):
+        loads.append(pltpu.make_async_copy(src, dst, load_sem.at[i]))
+    for copy in loads:
+        copy.start()
+
+    barrier = pltpu.get_barrier_semaphore()
+    greeted = [on_ring(1) + (ic, ix), on_ring(-1) + (ic, ix), from_id]
+    greeted += [(ia, ib) + member(k) for k in range(1, ranks)]
+    for device in greeted:
+        pl.semaphore_signal(barrier, inc=1, device_id=device, device_id_type=MESH)
+    pl.semaphore_wait(barrier, len(greeted))
+
+    def ring_copy(j, way, step, parity):
+        neighbour = on_ring(1 - 2 * way) + (ic, ix)
+        return pltpu.make_async_remote_copy(
+            src_ref=send[j].at[way, parity],
+            dst_ref=recv[j].at[way, step],
+            send_sem=send_sem.at[j, way, parity],
+            recv_sem=recv_sem.at[j, way, step],
+            device_id=neighbour,
+            device_id_type=MESH,
+        )
+
+    def product(j, way, step):
+        job = jobs[j]
+        a, b = on_ring(step * (2 * way - 1))
+        part = job.rows // chips
+        if job.by_rank:
+            start = kept_slot(a, b, size_a, size_b) * part
+            if lefts[job.left].shape[0] != job.rows:
+                start = start + rank * job.rows
+        else:
+            start = (a * size_b + b) * part
+        cols = job.cols // 2
+        left = lefts[job.left][pl.ds(pl.multiple_of(start, part), part), :]
+        return jnp.dot(
+            left, rights[job.right][:, way * cols : (way + 1) * cols], preferred_element_type=F32
+        )
+
+    def deliver(j):
+        job = jobs[j]
+        if job.by_rank:
+            return [
+                pltpu.make_async_remote_copy(
+                    src_ref=done[j],
+                    dst_ref=outs[j],
+                    send_sem=done_send.at[j, 0],
+                    recv_sem=done_recv.at[j, 0],
+                    device_id=kept_id,
+                    device_id_type=MESH,
+                )
+            ]
+        part = job.rows // (chips * ranks)
+        copies = []
+        for k in range(1, ranks):
+            c, x = member(k)
+            start = pl.multiple_of((c * size_x + x) * part, part)
+            copies.append(
+                pltpu.make_async_remote_copy(
+                    src_ref=done[j].at[pl.ds(start, part), :],
+                    dst_ref=outs[j].at[rank],
+                    send_sem=done_send.at[j, k],
+                    recv_sem=done_recv.at[j, k],
+                    device_id=(ia, ib, c, x),
+                    device_id_type=MESH,
+                )
+            )
+        start = pl.multiple_of((ic * size_x + ix) * part, part)
+        copies.append(
+            pltpu.make_async_copy(done[j].at[pl.ds(start, part), :], outs[j].at[rank], own_sem.at[j])
+        )
+        return copies
+
+    loaded = set()
+    for phase in range(1 + max(job.phase for job in jobs)):
+        mine = [j for j in range(count) if jobs[j].phase == phase]
+        for j in mine:
+            for i in (jobs[j].left, n_left + jobs[j].right):
+                if i not in loaded:
+                    loaded.add(i)
+                    loads[i].wait()
+            for way in range(2):
+                send[j][way, 0] = product(j, way, 1).astype(BF)
+                ring_copy(j, way, 0, 0).start()
+
+        def step_of(step, carry):
+            parity = step % 2
+            for j in mine:
+                for way in range(2):
+                    part = product(j, way, step + 1)
+                    ring_copy(j, way, step - 1, 1 - parity).wait_recv()
+                    part = part + recv[j][way, step - 1].astype(F32)
+
+                    @pl.when(step >= 2)
+                    def _():
+                        ring_copy(j, way, step - 2, parity).wait_send()
+
+                    send[j][way, parity] = part.astype(BF)
+                    ring_copy(j, way, step, parity).start()
+            return carry
+
+        lax.fori_loop(1, chips - 1, step_of, 0)
+        last = chips - 2
+        for j in mine:
+            cols = jobs[j].cols // 2
+            for way in range(2):
+                part = product(j, way, chips)
+                ring_copy(j, way, last, last % 2).wait_recv()
+                part = part + recv[j][way, last].astype(F32)
+                done[j][:, way * cols : (way + 1) * cols] = part.astype(BF)
+            for copy in deliver(j):
+                copy.start()
+            for way in range(2):
+                ring_copy(j, way, last - 1, (last - 1) % 2).wait_send()
+                ring_copy(j, way, last, last % 2).wait_send()
+    for j in range(count):
+        for copy in deliver(j):
+            copy.wait()
+
+
+def sum_grads(sizes, jobs, lefts, rights):
+    size_a, size_b, size_x = sizes
+    chips = size_a * size_b
+    ranks = 2 * size_x
+    outs, recv, send, done = [], [], [], []
+    flops = 0
+    for job in jobs:
+        part = job.rows // chips
+        if job.by_rank:
+            outs.append(jax.ShapeDtypeStruct((part, job.cols), BF))
+        else:
+            outs.append(jax.ShapeDtypeStruct((ranks, part // ranks, job.cols), BF))
+        recv.append(pltpu.VMEM((2, chips - 1, part, job.cols // 2), BF))
+        send.append(pltpu.VMEM((2, 2, part, job.cols // 2), BF))
+        done.append(pltpu.VMEM((part, job.cols), BF))
+        flops += 2 * job.rows * job.cols * rights[job.right].shape[0]
+    count = len(jobs)
+    sem = pltpu.SemaphoreType.DMA
+    return pl.pallas_call(
+        functools.partial(grads_kernel, sizes, jobs, len(lefts), len(rights)),
+        in_specs=[pl.BlockSpec(memory_space=pl.ANY)] * (len(lefts) + len(rights)),
+        out_specs=[pl.BlockSpec(memory_space=pl.ANY)] * count,
+        out_shape=outs,
+        scratch_shapes=[pltpu.VMEM(a.shape, BF) for a in lefts + rights]
+        + recv
+        + send
+        + done
+        + [
+            sem((len(lefts) + len(rights),)),
+            sem((count, 2, 2)),
+            sem((count, 2, chips - 1)),
+            sem((count, ranks)),
+            sem((count, ranks)),
+            sem((count,)),
+        ],
+        compiler_params=pltpu.CompilerParams(
+            collective_id=0, has_side_effects=True, vmem_limit_bytes=60 * 1024 * 1024
+        ),
+        cost_estimate=pl.CostEstimate(
+            flops=flops, bytes_accessed=400 * 1024 * 1024, transcendentals=0
+        ),
+        name="sum_grads",
+    )(*lefts, *rights)
 
 
 def norm_stats(values):
@@ -275,61 +501,16 @@
             total = summed if total is None else total + summed
         return total
 
-    order = ring_order(size_a, size_b)
-    place = [order.index(g) for g in range(chips)]
-    position = jnp.asarray(place, jnp.int32)[chip]
-    onward = [(order[p], order[(p + 1) % chips]) for p in range(chips)]
-    backward = [(order[p], order[(p - 1) % chips]) for p in range(chips)]
-
-    def ring_sum(chunks, slots):
-        rows = chunks.shape[1]
-        chunk_at = jnp.asarray([slots[g] for g in order], jnp.int32)
-        half = rows // 2
-        held_f = held_b = None
-        for step in range(1, chips + 1):
-            at_f = chunk_at[(position + 2 * chips - step) % chips]
-            at_b = chunk_at[(position + step) % chips]
-            part_f = lax.dynamic_slice(
-                chunks, (at_f, 0, 0), (1, half, chunks.shape[2])
-            )[0].astype(F32)
-            part_b = lax.dynamic_slice(
-                chunks, (at_b, half, 0), (1, rows - half, chunks.shape[2])
-            )[0].astype(F32)
-            if step > 1:
-                part_f = part_f + held_f.astype(F32)
-                part_b = part_b + held_b.astype(F32)
-            if step == chips:
-                return jnp.concatenate([part_f, part_b], 0)
-            held_f = lax.ppermute(part_f.astype(BF), ("a", "b"), onward)
-            held_b = lax.ppermute(part_b.astype(BF), ("a", "b"), backward)
-
-    if (size_a, size_b, size_x) == (4, 2, 2):
-        slot = [(g % 2) * 4 + ((g // 2) % 2) * 2 + (g // 2) // 2 for g in range(chips)]
-    else:
-        slot = list(range(chips))
-    keep_pairs = []
-    for g in range(chips):
-        for c in range(2):
-            for x in range(size_x):
-                keep_pairs.append(((g * 2 + c) * size_x + x, (x * 2 + c) * chips + slot[g]))
-
     def sum_rows(grad):
-        chunks = grad.astype(BF).reshape(chips, grad.shape[0] // chips, grad.shape[1])
-        summed = ring_sum(chunks, slot)
-        return lax.ppermute(summed.astype(BF), ALL, keep_pairs).astype(F32)
-
-    def sum_columns(grad):
-        rows, part = grad.shape
-        chunks = grad.astype(BF).reshape(chips, rows // chips, part)
-        summed = ring_sum(chunks, list(range(chips))).astype(BF).reshape(2, size_x, rows // (chips * ranks), part)
-        both = jnp.zeros((2,) + summed.shape[1:], BF)
-        both = put(both, pick(summed, ic), ic)
-        both = put(both, to_core(pick(summed, 1 - ic)), 1 - ic)
-        full = jnp.zeros((size_x, 2) + summed.shape[2:], BF)
-        full = put(full, pick(both, ix, 1), ix)
-        for step in range(1, size_x):
-            full = put(full, to_x(pick(both, (ix + step) % size_x, 1), step), from_x(step))
-        return full.transpose(2, 0, 1, 3).reshape(-1, ranks * part).astype(F32)
+        summed = lax.psum_scatter(
+            grad.astype(BF), ("a", "b"), scatter_dimension=0, tiled=True
+        )
+        keep_pairs = []
+        for g in range(chips):
+            for c in range(2):
+                for x in range(size_x):
+                    keep_pairs.append(((g * 2 + c) * size_x + x, (x * 2 + c) * chips + g))
+        return lax.ppermute(summed, ALL, keep_pairs).astype(F32)
 
     def sum_gain(grad):
         for name, size in (("c", 2), ("x", size_x), ("b", size_b), ("a", size_a)):
@@ -397,8 +578,6 @@
         lambda step: mm_nt(rows_of(d_gate, step), w_gate) + mm_nt(rows_of(d_upward, step), w_up)
     )
     down_grad = sum_rows(mm_tn(hidden, cot_rows))
-    gate_grad = sum_columns(mm_tn(normed_mlp, d_gate))
-    up_grad = sum_columns(mm_tn(normed_mlp, d_upward))
     branch_mlp = group_sum(lambda step: mm(rows_of(hidden, step), w_down))
     block_output = from_stream((resid + branch_mlp).astype(BF)).astype(BF)
     d_resid_part, mlp_gain_grad = norm_back(unit_two, inv_two, gain_two, d_normed_mlp)
@@ -407,18 +586,31 @@
     d_branch = d_resid.astype(BF)
 
     d_context = mm_nt(d_branch, w_out).astype(BF)
-    out_grad = sum_rows(mm_tn(group_columns(context), group_rows(d_branch)))
+    context_cols = group_columns(context)
+    branch_rows = group_rows(d_branch)
     d_queries, d_window = attend_back(queries, window, low, d_context, lse)
     d_pairs = d_window[halo * tok :]
     for j in range(halo):
         part = d_window[j * tok : (j + 1) * tok].astype(BF)
         d_pairs = d_pairs + shift_ctx(part, j - halo).astype(F32)
     d_pairs = d_pairs.astype(BF)
-    normed_rows = group_rows(normed)
-    query_grad = sum_columns(mm_tn(normed_rows, group_columns(d_queries)))
-    kv_part = width // ranks
-    normed_part = lax.dynamic_slice(normed_rows, (0, rank * kv_part), (ranks * tok, kv_part))
-    kv_grad = sum_rows(mm_tn(normed_part, group_rows(d_pairs)))
+    jobs = [
+        Job(0, 0, 0, width, d_gate.shape[1], False),
+        Job(0, 0, 1, width, d_upward.shape[1], False),
+        Job(1, 1, 2, width, width // ranks, False),
+        Job(1, 2, 3, width // ranks, width, True),
+        Job(1, 1, 4, width // ranks, 2 * HD, True),
+    ]
+    sums = sum_grads(
+        sizes,
+        jobs,
+        [normed_mlp.T, group_rows(normed).T, context_cols.T],
+        [d_gate, d_upward, group_columns(d_queries), branch_rows, group_rows(d_pairs)],
+    )
+    gate_grad, up_grad, query_grad = (
+        v.transpose(1, 0, 2).reshape(v.shape[1], -1).astype(F32) for v in sums[:3]
+    )
+    out_grad, kv_grad = (v.astype(F32) for v in sums[3:])
     d_normed = mm_nt(d_queries, w_query) + mm_nt(d_pairs, w_kv)
     d_inputs, attn_gain_grad = norm_back(unit_one, inv_one, gain_one, d_normed)
     attn_gain_grad = sum_gain(attn_gain_grad)

time: 1100 us -> 857 us (0.78)
  Pallas kernels: 27.4 us -> 212 us
  waiting for transfers between devices: 443 us -> 260 us
  starting transfers between devices: 219 us -> 85.6 us
  between operations: 70.9 us -> 15.6 us
  other arithmetic: 78.1 us -> 46.6 us
  matrix products: 145 us -> 123 us
    ppermute x87 -> x1, waiting for transfers between devices: 284 us -> 30.4 us  [sum_rows(): return lax.ppermute(summed, ALL, keep_pairs).astype(F32)]
    pallas_call x0 -> x1, Pallas kernels: none -> 185 us  [sum_grads(): pl.pallas_call(functools.partial(grads_kernel, sizes, jobs, len(lefts), l...]
    ppermute x87 -> x1, starting transfers between devices: 105 us -> 3.14 us  [sum_rows(): return lax.ppermute(summed, ALL, keep_pairs).astype(F32)]
    ppermute x18 -> x15, waiting for transfers between devices: 125 us -> 177 us  [to_x(): lax.ppermute(array, 'x', [(i, (i + step) % size_x) for i in range(size_x)])]
    convert_element_type x72 -> x3, other arithmetic: 46.7 us -> 2.78 us  [the longest x2 1.47 us: on_device(): out_grad, kv_grad = (v.astype(F32) for v in sums[3:])]
    dot_general x8 -> x3, matrix products: 39.7 us -> 15.5 us  [mm_tn(): lax.dot_general(left, right, (((0,), (0,)), ((), ())), preferred_element_...]
    ppermute x18 -> x15, starting transfers between devices: 39.1 us -> 18.8 us  [to_x(): lax.ppermute(array, 'x', [(i, (i + step) % size_x) for i in range(size_x)])]
    all_to_all x2, waiting for transfers between devices: 0.01 us -> 19.8 us  [from_stream(): dealt = lax.all_to_all(array, CTX, split_axis=0, concat_axis=0, tiled=True)]
  transfers between devices with their start and end apart: 150 -> 59, of which waited for: 65 -> 24; matrix products, arithmetic and copies ran while one was open for 21% -> 31% of each run, Pallas kernels for 3% -> 25%
where the time goes in v2:
time: 857 us; the launch traced here: 848 us
  waiting for transfers between devices  260 us (30%)
  Pallas kernels  212 us (25%)
  matrix products  123 us (14%)
  local copies, waits for them, and re-layouts  104 us (12%)
  starting transfers between devices  85.6 us (10%)
  other arithmetic  46.6 us (5%)
  between operations  15.6 us (2%)
    pallas_call x1, Pallas kernels, sum_grads(): pl.pallas_call(functools.partial(grads_kernel, sizes, jobs, len(lefts), l...  185 us
    ppermute x15, waiting for transfers between devices, to_x(): lax.ppermute(array, 'x', [(i, (i + step) % size_x) for i in range(size_x)])  177 us
    dot_general x8, matrix products, mm_nt(): lax.dot_general(left, right, (((1,), (1,)), ((), ())), preferred_element_...  54.2 us
    dot_general x9, matrix products, mm(): return jnp.dot(left, right, preferred_element_type=F32)  52.9 us
    ppermute x1, waiting for transfers between devices, sum_rows(): return lax.ppermute(summed, ALL, keep_pairs).astype(F32)  30.4 us
    ppermute x8, starting transfers between devices, shift_ctx(): return lax.ppermute(array, CTX, pairs)  20.8 us
    all_to_all x2, waiting for transfers between devices, from_stream(): dealt = lax.all_to_all(array, CTX, split_axis=0, concat_axis=0, tiled=True)  19.8 us
    ppermute x15, starting transfers between devices, to_x(): lax.ppermute(array, 'x', [(i, (i + step) % size_x) for i in range(size_x)])  18.8 us
  transfers between devices with their start and end apart: 59, of which 24 were waited for; matrix products, arithmetic and copies ran while one was open for 31% of the time, Pallas kernels for 25%

profile of v2, /device:TPU:20, one launch (start us, length us, event | category | flops | bytes accessed | tf_op | source)
XLA Modules:
  0.0 847.5 jit_solution(17697480606125752304)
XLA Ops:
  79.3 13.7 %all-to-all-done.2 = bf16[16,16,2048]{2,1,0:T(8,128)(2,1)} async-done(((bf16[16,16,2048]{2,1,0:T(8,128)(2,1)}), bf16[16,16,2048]{2,1,0:T(8,128)(2,1)}, u32[]{:S(2)}, u32[]{:S(2)}) %all-to-all-start.2) | async-done | bytes 1048608 | tf_op jit(solution)/shard_map/all_to_all | solution.py:528
  94.6 22.6 %collective-permute-done.10 = bf16[512,2048]{1,0:T(8,128)(2,1)} collective-permute-done((bf16[512,2048]{1,0:T(8,128)(2,1)}, bf16[512,2048]{1,0:T(8,128)(2,1)}, u32[]{:S(2)}, u32[]{:S(2)}) %collective-permute-start.10) | collective-permute-done | bytes 2097184 | tf_op jit(solution)/shard_map/ppermute | solution.py:441
  149.4 10.6 %attend.1 = (bf16[256,2048]{1,0:T(8,128)(2,1)S(1)}, f32[8,1,512]{2,1,0:T(1,128)S(1)}) custom-call(s32[1,256]{1,0:T(1,128)S(1)} %maximum_subtract_fusion.lo_ref, bf16[256,2048]{1,0:T(8,128)(2,1)S(1)} %convolution_convert_fusion.5.q_ref, bf16[1280,256]{1,0:T(8,128)(2,1)S(1)} %constant_dynamic-update-slice_fusion.kv_ref), custom_call_target="tpu_custom_call" | custom-call | flops 2415919104 | bytes 4194304 | tf_op jit(solution)/shard_map/attend/pallas_call | solution.py:99
  167.6 39.5 %collective-permute-done.16 = bf16[1024,1536]{1,0:T(8,128)(2,1)} collective-permute-done((bf16[1024,1536]{1,0:T(8,128)(2,1)}, bf16[1024,1536]{1,0:T(8,128)(2,1)}, u32[]{:S(2)}, u32[]{:S(2)}) %collective-permute-start.16) | collective-permute-done | bytes 3145760 | tf_op jit(solution)/shard_map/ppermute | solution.py:441
  210.9 63.6 %collective-permute-done.15 = bf16[1024,1536]{1,0:T(8,128)(2,1)} collective-permute-done((bf16[1024,1536]{1,0:T(8,128)(2,1)}, bf16[1024,1536]{1,0:T(8,128)(2,1)}, u32[]{:S(2)}, u32[]{:S(2)}) %collective-permute-start.15) | collective-permute-done | bytes 3145760 | tf_op jit(solution)/shard_map/ppermute | solution.py:441
  278.2 17.9 %collective-permute-done.13 = bf16[256,2048]{1,0:T(8,128)(2,1)} collective-permute-done((bf16[256,2048]{1,0:T(8,128)(2,1)}, bf16[256,2048]{1,0:T(8,128)(2,1)}, u32[]{:S(2)}, u32[]{:S(2)}) %collective-permute-start.13) | collective-permute-done | bytes 1048608 | tf_op jit(solution)/shard_map/ppermute | solution.py:441
  296.2 13.0 %fusion.7 = f32[1024,1536]{1,0:T(8,128)} fusion(bf16[3072,2048]{1,0:T(8,128)(2,1)} %param.22, s32[]{:T(128)S(6)} %select_n.115, bf16[256,2048]{1,0:T(8,128)(2,1)} %collective-permute-done.22, bf16[256,2048]{1,0:T(8,128)(2,1)} %collective-permute-done.21, bf16[256,2048]{1,0:T(8,128)(2,1)} %collective-permute-done.20, bf16[256,2048]{1,0:T(8,128)(2,1)} %bitcast.42), kind=kOutput, calls=%fused_computation.13 | convolution fusion | flops 6459228160 | bytes 16777220 | tf_op jit(solution)/shard_map/dot_general | solution.py:38
  314.6 13.2 %fusion.46 = f32[1024,1536]{1,0:T(8,128)} fusion(bf16[2048,1536]{1,0:T(8,128)(2,1)} %bitcast.36, bf16[256,2048]{1,0:T(8,128)(2,1)} %collective-permute-done.14, bf16[256,2048]{1,0:T(8,128)(2,1)} %collective-permute-done.13, bf16[256,2048]{1,0:T(8,128)(2,1)} %collective-permute-done.12, bf16[256,2048]{1,0:T(8,128)(2,1)} %multiply_convert_fusion.3), kind=kOutput, calls=%fused_computation.149 | convolution fusion | flops 6459228160 | bytes 16777216 | tf_op jit(solution)/shard_map/dot_general | solution.py:30
  327.7 18.7 %fusion.6 = (bf16[1024,1536]{1,0:T(8,128)(2,1)S(1)}, bf16[1024,1536]{1,0:T(8,128)(2,1)S(1)}, bf16[1024,1536]{1,0:T(8,128)(2,1)}) fusion(f32[1024,1536]{1,0:T(8,128)} %fusion.7, f32[1024,1536]{1,0:T(8,128)} %fusion.46, bf16[2048,1536]{1,0:T(8,128)(2,1)} %bitcast.33, bf16[256,2048]{1,0:T(8,128)(2,1)} %collective-permute-done.14, ...), kind=kOutput, calls=%fused_computation.9 | convolution fusion | flops 6500122624 | bytes 32505856 | tf_op jit(solution)/shard_map/dot_general | solution.py:30
  346.5 7.9 fusion.23
  354.4 8.3 fusion.20
  377.6 10.9 %convolution_convert_fusion = bf16[1536,2048]{1,0:T(8,128)(2,1)} fusion(bf16[1024,1536]{1,0:T(8,128)(2,1)S(1)} %copy-done.47, bf16[256,2048]{1,0:T(8,128)(2,1)} %collective-permute-done.22, bf16[256,2048]{1,0:T(8,128)(2,1)} %collective-permute-done.21, bf16[256,2048]{1,0:T(8,128)(2,1)} %collective-permute-done.20, bf16[256,2048]{1,0:T(8,128)(2,1)} %bitcast.42), kind=kOutput, calls=%fused_computation.2 | convolution fusion | flops 6462373888 | bytes 13631488 | tf_op jit(solution)/shard_map/dot_general | solution.py:34
  388.5 8.0 convolution_add_fusion
  428.5 19.3 %collective-permute-done.18 = bf16[256,2048]{1,0:T(8,128)(2,1)} collective-permute-done((bf16[256,2048]{1,0:T(8,128)(2,1)}, bf16[256,2048]{1,0:T(8,128)(2,1)}, u32[]{:S(2)}, u32[]{:S(2)}) %collective-permute-start.18) | collective-permute-done | bytes 1048608 | tf_op jit(solution)/shard_map/ppermute | solution.py:441
  447.8 6.6 fusion.48
  456.8 16.7 %attend_back.1 = (bf16[256,2048]{1,0:T(8,128)(2,1)S(1)}, f32[1280,256]{1,0:T(8,128)S(1)}) custom-call(s32[1,256]{1,0:T(1,128)S(1)} %maximum_subtract_fusion.lo_ref, bf16[256,2048]{1,0:T(8,128)(2,1)S(1)} %copy-done.3, bf16[1280,256]{1,0:T(8,128)(2,1)S(1)} %constant_dynamic-update-slice_fusion.kv_ref, bf16[256,2048]{1,0:T(8,128)(2,1)S(1)} %convolution_convert_fusion.4.do_ref, ...), custom_call_target="tpu_custom_call" | custom-call | flops 6039797760 | bytes 6291456 | tf_op jit(solution)/shard_map/attend_back/pallas_call | solution.py:127
  489.4 7.3 all-to-all-start.1
  501.2 7.3 multiply_reduce_fusion.1
  510.8 19.8 %all-to-all-done.1 = bf16[16,16,2048]{2,1,0:T(8,128)(2,1)} async-done(((bf16[16,16,2048]{2,1,0:T(8,128)(2,1)}), bf16[16,16,2048]{2,1,0:T(8,128)(2,1)}, u32[]{:S(2)}, u32[]{:S(2)}) %all-to-all-start.1) | async-done | bytes 1048608 | tf_op jit(solution)/shard_map/all_to_all | solution.py:533
  530.6 9.4 %all-to-all-start.3 = ((bf16[16,16,2048]{2,1,0:T(8,128)(2,1)}), bf16[16,16,2048]{2,1,0:T(8,128)(2,1)S(1)}, u32[]{:S(2)}, u32[]{:S(2)}) async-start(bf16[16,16,2048]{2,1,0:T(8,128)(2,1)} %bitcast.43), calls=%async_computation.3 | async-start | bytes 2097152 | tf_op jit(solution)/shard_map/all_to_all | solution.py:533
  582.1 6.3 copy.65.refs_0_
  607.3 6.4 copy.66.refs_1_
  613.7 184.9 %sum_grads.1 = (bf16[4,64,1536]{2,1,0:T(8,128)(2,1)}, bf16[4,64,1536]{2,1,0:T(8,128)(2,1)}, bf16[4,64,512]{2,1,0:T(8,128)(2,1)}, bf16[64,2048]{1,0:T(8,128)(2,1)}, bf16[64,256]{1,0:T(8,128)(2,1)}) custom-call(bf16[2048,1024]{1,0:T(8,128)(2,1)} %copy.65.refs_0_, bf16[2048,1024]{1,0:T(8,128)(2,1)} %copy.66.refs_1_, ...), custom_call_target="tpu_custom_call" | custom-call | flops 17448304640 | bytes 419430400 | tf_op jit(solution)/shard_map/sum_grads/pallas_call | solution.py:363
  808.5 30.4 %collective-permute-done.53 = bf16[192,2048]{1,0:T(8,128)(2,1)S(1)} collective-permute-done((bf16[192,2048]{1,0:T(8,128)(2,1)}, bf16[192,2048]{1,0:T(8,128)(2,1)S(1)}, u32[]{:S(2)}, u32[]{:S(2)}) %collective-permute-start.53) | collective-permute-done | bytes 786464 | tf_op jit(solution)/shard_map/ppermute | solution.py:513
  (338 shorter events, 269.5 us)
Async XLA Ops:
  8.3 55.1 %collective-permute-start.4 = (bf16[512,256]{1,0:T(8,128)(2,1)S(1)}, bf16[512,256]{1,0:T(8,128)(2,1)}, u32[]{:S(2)}, u32[]{:S(2)}) collective-permute-start(bf16[512,256]{1,0:T(8,128)(2,1)S(1)} %dynamic-slice_bitcast_fusion.2), channel_id=1, source_target_pairs={{0,1},{1,0},{2,3},{3,2},{4,5},{5,4},{6,7},{7,6},{8,9},{9,8},{10,11... | collective-permute-start | bytes 786440 | tf_op jit(solution)/shard_map/ppermute | solution.py:441
  11.2 50.8 %collective-permute-start = (bf16[512,2]{0,1:T(2,128)(2,1)S(1)}, bf16[512,2]{0,1:T(2,128)(2,1)S(1)}, u32[]{:S(2)}, u32[]{:S(2)}) collective-permute-start(bf16[512,2]{0,1:T(2,128)(2,1)S(1)} %bitcast.186), channel_id=1, source_target_pairs={{0,1},{1,0},{2,3},{3,2},{4,5},{5,4},{6,7},{7,6},{8,9},{9,8},{10,11... | collective-permute-start | bytes 6152 | tf_op jit(solution)/shard_map/ppermute | solution.py:441
  14.0 49.6 %all-to-all-start = ((bf16[16,16,2048]{2,1,0:T(8,128)(2,1)}), bf16[16,16,2048]{2,1,0:T(8,128)(2,1)S(1)}, u32[]{:S(2)}, u32[]{:S(2)}) async-start(bf16[16,16,2048]{2,1,0:T(8,128)(2,1)} %bitcast.2), calls=%async_computation | async-start | bytes 2097152 | tf_op jit(solution)/shard_map/all_to_all | solution.py:528
  23.5 48.8 %collective-permute-start.2 = (bf16[512,2048]{1,0:T(8,128)(2,1)}, bf16[512,2048]{1,0:T(8,128)(2,1)}, u32[]{:S(2)}, u32[]{:S(2)}) collective-permute-start(bf16[512,2048]{1,0:T(8,128)(2,1)} %dynamic-slice_bitcast_fusion.1), channel_id=1, source_target_pairs={{0,1},{1,0},{2,3},{3,2},{4,5},{5,4},{6,7},{7,6},{8,9},{9,8},{10,11... | collective-permute-start | bytes 6291464 | tf_op jit(solution)/shard_map/ppermute | solution.py:441
  26.4 90.7 %collective-permute-start.10 = (bf16[512,2048]{1,0:T(8,128)(2,1)}, bf16[512,2048]{1,0:T(8,128)(2,1)}, u32[]{:S(2)}, u32[]{:S(2)}) collective-permute-start(bf16[512,2048]{1,0:T(8,128)(2,1)} %dynamic-slice_bitcast_fusion), channel_id=1, source_target_pairs={{0,1},{1,0},{2,3},{3,2},{4,5},{5,4},{6,7},{7,6},{8,9},{9,8},{10,11... | collective-permute-start | bytes 6291464 | tf_op jit(solution)/shard_map/ppermute | solution.py:441
  69.6 729.0 %reduce-scatter.2.cloned.1.call-start = ((), (), s32[]{:S(2)}) async-start(), calls=%async_computation.5 | async-start | bytes 7077888 | tf_op jit(solution)/shard_map/reduce_scatter | solution.py:505
  72.2 67.4 %collective-permute-start.3 = (bf16[512,2048]{1,0:T(8,128)(2,1)}, bf16[512,2048]{1,0:T(8,128)(2,1)}, u32[]{:S(2)}, u32[]{:S(2)}) collective-permute-start(bf16[512,2048]{1,0:T(8,128)(2,1)} %collective-permute-done.2), channel_id=1, source_target_pairs={{0,2},{2,0},{1,3},{3,1},{4,6},{6,4},{5,7},{7,5},{8,10},{10,8},{9,1... | collective-permute-start | bytes 6291464 | tf_op jit(solution)/shard_map/ppermute | solution.py:438
  74.0 49.6 %collective-permute-start.6 = (bf16[256,256]{1,0:T(8,128)(2,1)S(1)}, bf16[256,256]{1,0:T(8,128)(2,1)S(1)}, u32[]{:S(2)}, u32[]{:S(2)}) collective-permute-start(bf16[256,256]{1,0:T(8,128)(2,1)S(1)} %convolution_convert_fusion.6), channel_id=1, source_target_pairs={{0,8},{2,10},{4,12},{6,14},{8,16},{10,18},{12,20},{14,22},{16,24},... | collective-permute-start | bytes 393224 | tf_op jit(solution)/shard_map/ppermute | solution.py:445
  77.4 49.6 %collective-permute-start.7 = (bf16[256,256]{1,0:T(8,128)(2,1)S(1)}, bf16[256,256]{1,0:T(8,128)(2,1)S(1)}, u32[]{:S(2)}, u32[]{:S(2)}) collective-permute-start(bf16[256,256]{1,0:T(8,128)(2,1)S(1)} %convolution_convert_fusion.6), channel_id=1, source_target_pairs={{0,6},{2,8},{4,10},{6,12},{8,14},{10,16},{12,18},{14,20},{16,22},{... | collective-permute-start | bytes 393224 | tf_op jit(solution)/shard_map/ppermute | solution.py:445
  93.0 46.6 %collective-permute-start.21 = (bf16[256,2048]{1,0:T(8,128)(2,1)}, bf16[256,2048]{1,0:T(8,128)(2,1)}, u32[]{:S(2)}, u32[]{:S(2)}) collective-permute-start(bf16[256,2048]{1,0:T(8,128)(2,1)} %bitcast.42), channel_id=1, source_target_pairs={{0,1},{1,0},{2,3},{3,2},{4,5},{5,4},{6,7},{7,6},{8,9},{9,8},{10,11... | collective-permute-start | bytes 3145736 | tf_op jit(solution)/shard_map/ppermute | solution.py:441
  117.2 42.9 %collective-permute-start.11 = (bf16[512,2048]{1,0:T(8,128)(2,1)}, bf16[512,2048]{1,0:T(8,128)(2,1)S(1)}, u32[]{:S(2)}, u32[]{:S(2)}) collective-permute-start(bf16[512,2048]{1,0:T(8,128)(2,1)} %collective-permute-done.10), channel_id=1, source_target_pairs={{0,2},{2,0},{1,3},{3,1},{4,6},{6,4},{5,7},{7,5},{8,10},{10,8},{9,1... | collective-permute-start | bytes 6291464 | tf_op jit(solution)/shard_map/ppermute | solution.py:438
  131.4 75.6 %collective-permute-start.16 = (bf16[1024,1536]{1,0:T(8,128)(2,1)}, bf16[1024,1536]{1,0:T(8,128)(2,1)}, u32[]{:S(2)}, u32[]{:S(2)}) collective-permute-start(bf16[1024,1536]{1,0:T(8,128)(2,1)} %constant_dynamic-slice_fusion.5), channel_id=1, source_target_pairs={{0,1},{1,0},{2,3},{3,2},{4,5},{5,4},{6,7},{7,6},{8,9},{9,8},{10,11... | collective-permute-start | bytes 9437192 | tf_op jit(solution)/shard_map/ppermute | solution.py:441
  133.3 141.2 %collective-permute-start.15 = (bf16[1024,1536]{1,0:T(8,128)(2,1)}, bf16[1024,1536]{1,0:T(8,128)(2,1)}, u32[]{:S(2)}, u32[]{:S(2)}) collective-permute-start(bf16[1024,1536]{1,0:T(8,128)(2,1)} %constant_dynamic-slice_fusion.6), channel_id=1, source_target_pairs={{0,1},{1,0},{2,3},{3,2},{4,5},{5,4},{6,7},{7,6},{8,9},{9,8},{10,11... | collective-permute-start | bytes 9437192 | tf_op jit(solution)/shard_map/ppermute | solution.py:441
  139.7 156.5 %collective-permute-start.20 = (bf16[256,2048]{1,0:T(8,128)(2,1)}, bf16[256,2048]{1,0:T(8,128)(2,1)}, u32[]{:S(2)}, u32[]{:S(2)}) collective-permute-start(bf16[256,2048]{1,0:T(8,128)(2,1)} %bitcast.42), channel_id=1, source_target_pairs={{0,2},{2,0},{1,3},{3,1},{4,6},{6,4},{5,7},{7,5},{8,10},{10,8},{9,1... | collective-permute-start | bytes 3145736 | tf_op jit(solution)/shard_map/ppermute | solution.py:438
  139.7 156.5 %collective-permute-start.22 = (bf16[256,2048]{1,0:T(8,128)(2,1)}, bf16[256,2048]{1,0:T(8,128)(2,1)}, u32[]{:S(2)}, u32[]{:S(2)}) collective-permute-start(bf16[256,2048]{1,0:T(8,128)(2,1)} %collective-permute-done.21), channel_id=1, source_target_pairs={{0,2},{2,0},{1,3},{3,1},{4,6},{6,4},{5,7},{7,5},{8,10},{10,8},{9,1... | collective-permute-start | bytes 3145736 | tf_op jit(solution)/shard_map/ppermute | solution.py:438
  166.1 130.0 %collective-permute-start.13 = (bf16[256,2048]{1,0:T(8,128)(2,1)}, bf16[256,2048]{1,0:T(8,128)(2,1)}, u32[]{:S(2)}, u32[]{:S(2)}) collective-permute-start(bf16[256,2048]{1,0:T(8,128)(2,1)} %multiply_convert_fusion.3), channel_id=1, source_target_pairs={{0,1},{1,0},{2,3},{3,2},{4,5},{5,4},{6,7},{7,6},{8,9},{9,8},{10,11... | collective-permute-start | bytes 3145736 | tf_op jit(solution)/shard_map/ppermute | solution.py:441
  314.1 100.6 %collective-permute-start.38 = (bf16[256,2,512]{2,0,1:T(8,128)(2,1)}, bf16[256,2,512]{2,0,1:T(8,128)(2,1)}, u32[]{:S(2)}, u32[]{:S(2)}) collective-permute-start(bf16[256,2,512]{2,0,1:T(8,128)(2,1)} %bitcast.140), channel_id=1, source_target_pairs={{0,2},{2,0},{1,3},{3,1},{4,6},{6,4},{5,7},{7,5},{8,10},{10,8},{9,1... | collective-permute-start | bytes 1572872 | tf_op jit(solution)/shard_map/ppermute | solution.py:438
  418.8 148.5 %collective-permute-start.39 = (bf16[512,512]{0,1:T(8,128)(2,1)}, bf16[512,512]{0,1:T(8,128)(2,1)}, u32[]{:S(2)}, u32[]{:S(2)}) collective-permute-start(bf16[512,512]{0,1:T(8,128)(2,1)} %copy.71), channel_id=1, source_target_pairs={{0,1},{1,0},{2,3},{3,2},{4,5},{5,4},{6,7},{7,6},{8,9},{9,8},{10,11... | collective-permute-start | bytes 1572872 | tf_op jit(solution)/shard_map/ppermute | solution.py:441
  489.4 41.3 %all-to-all-start.1 = ((bf16[16,16,2048]{2,1,0:T(8,128)(2,1)}), bf16[16,16,2048]{2,1,0:T(8,128)(2,1)}, u32[]{:S(2)}, u32[]{:S(2)}) async-start(bf16[16,16,2048]{2,1,0:T(8,128)(2,1)} %bitcast.161), calls=%async_computation.1 | async-start | bytes 2097152 | tf_op jit(solution)/shard_map/all_to_all | solution.py:533
  496.7 76.8 %collective-permute-start.43 = (bf16[256,2048]{1,0:T(8,128)(2,1)}, bf16[256,2048]{1,0:T(8,128)(2,1)}, u32[]{:S(2)}, u32[]{:S(2)}) collective-permute-start(bf16[256,2048]{1,0:T(8,128)(2,1)} %copy-done.20), channel_id=1, source_target_pairs={{0,1},{1,0},{2,3},{3,2},{4,5},{5,4},{6,7},{7,6},{8,9},{9,8},{10,11... | collective-permute-start | bytes 3145736 | tf_op jit(solution)/shard_map/ppermute | solution.py:441
  498.2 75.2 %collective-permute-start.40 = (bf16[256,2,512]{2,0,1:T(8,128)(2,1)}, bf16[256,2,512]{2,0,1:T(8,128)(2,1)}, u32[]{:S(2)}, u32[]{:S(2)}) collective-permute-start(bf16[256,2,512]{2,0,1:T(8,128)(2,1)} %bitcast.171), channel_id=1, source_target_pairs={{0,2},{2,0},{1,3},{3,1},{4,6},{6,4},{5,7},{7,5},{8,10},{10,8},{9,1... | collective-permute-start | bytes 1572872 | tf_op jit(solution)/shard_map/ppermute | solution.py:438
  508.5 81.4 %collective-permute-start.36 = (bf16[256,2048]{1,0:T(8,128)(2,1)}, bf16[256,2048]{1,0:T(8,128)(2,1)}, u32[]{:S(2)}, u32[]{:S(2)}) collective-permute-start(bf16[256,2048]{1,0:T(8,128)(2,1)} %get-tuple-element.38), channel_id=1, source_target_pairs={{0,1},{1,0},{2,3},{3,2},{4,5},{5,4},{6,7},{7,6},{8,9},{9,8},{10,11... | collective-permute-start | bytes 3145736 | tf_op jit(solution)/shard_map/ppermute | solution.py:441
  530.6 71.0 %all-to-all-start.3 = ((bf16[16,16,2048]{2,1,0:T(8,128)(2,1)}), bf16[16,16,2048]{2,1,0:T(8,128)(2,1)S(1)}, u32[]{:S(2)}, u32[]{:S(2)}) async-start(bf16[16,16,2048]{2,1,0:T(8,128)(2,1)} %bitcast.43), calls=%async_computation.3 | async-start | bytes 2097152 | tf_op jit(solution)/shard_map/all_to_all | solution.py:533
  798.6 40.3 %collective-permute-start.53 = (bf16[192,2048]{1,0:T(8,128)(2,1)}, bf16[192,2048]{1,0:T(8,128)(2,1)S(1)}, u32[]{:S(2)}, u32[]{:S(2)}) collective-permute-start(bf16[192,2048]{1,0:T(8,128)(2,1)} %reduce-scatter.2.cloned.1.call-done), channel_id=1, source_target_pairs={{0,0},{1,16},{2,8},{3,24},{4,1},{5,17},{6,9},{7,25},{8,2},{9,18},{... | collective-permute-start | bytes 2359304 | tf_op jit(solution)/shard_map/ppermute | solution.py:513
  (91 other events, 1253.4 us)
Sparse Core Ops, SparseCore 0:
  388.7 129.7 reduce-scatter.1

commit v3 on v2

--- a/solution.py
+++ b/solution.py
@@ -175,6 +175,255 @@
 def kept_slot(a, b, size_a, size_b):
     half = size_a * size_b // 2
     return (1 - b % 2) * half + a * (size_b // 2) + b // 2
+
+
+class Piece:
+    def __init__(self, at, rows, square, shared, part, parts):
+        self.at, self.rows, self.square, self.shared = at, rows, square, shared
+        self.part, self.parts = part, parts
+        self.relays = [0, 1, 2, 3] if square else []
+        if shared:
+            self.relays += [4, 5, 6, 7, 8] if square else [4]
+
+
+def fetch_kernel(sizes, pieces, n_in, n_dealt, *refs):
+    size_a, size_b, size_x = sizes
+    n_ctx = size_a * size_b * 2
+    ins, refs = refs[:n_in], refs[n_in:]
+    outs, refs = refs[:n_in], refs[n_in:]
+    n_weights = n_in - n_dealt - 1
+    stages, refs = refs[:n_weights], refs[n_weights:]
+    keep_sem, own_sem, deal_send, deal_recv, gain_send, gain_recv = refs[:6]
+    x_send, x_recv, relay_send, relay_recv = refs[6:]
+    ia, ib, ic, ix = (lax.axis_index(name) for name in ALL)
+    own = (ia * size_b + ib) * 2 + ic
+    rank = ix * 2 + ic
+    pa, pb = ia % 2, ib % 2
+    other_a, other_b = ia + 1 - 2 * pa, ib + 1 - 2 * pb
+    corner = pa * 2 + pb
+    corner_a, corner_b, corner_d = (1 - pa) * 2 + pb, pa * 2 + 1 - pb, 3 - corner
+
+    barrier = pltpu.get_barrier_semaphore()
+    greeted = []
+    for k in range(1, n_ctx):
+        e = (own + k) % n_ctx
+        greeted.append((e // 2 // size_b, e // 2 % size_b, e % 2, ix))
+    for s in range(1, size_x):
+        greeted.append((ia, ib, ic, (ix + s) % size_x))
+    for device in greeted:
+        pl.semaphore_signal(barrier, inc=1, device_id=device, device_id_type=MESH)
+    pl.semaphore_wait(barrier, len(greeted))
+
+    def remote(src, dst, send, recv, device):
+        return pltpu.make_async_remote_copy(
+            src_ref=src,
+            dst_ref=dst,
+            send_sem=send,
+            recv_sem=recv,
+            device_id=device,
+            device_id_type=MESH,
+        )
+
+    def x_copy(i, s):
+        p = pieces[i]
+        shard, full = ins[p.at], outs[p.at]
+        target = (ix + s) % size_x
+        height = shard.shape[0]
+        rows, start = region(p, corner, ic)
+        if p.shared:
+            src = shard.at[pl.ds(start, rows), :]
+        else:
+            cols = full.shape[1]
+            at = pl.multiple_of((target * 2 + ic) * cols, cols)
+            src = shard.at[pl.ds(start, rows), pl.ds(at, cols)]
+        dst = full.at[pl.ds(pl.multiple_of(ix * height + start, rows), rows), :]
+        return remote(src, dst, x_send.at[i, s], x_recv.at[i, s], (ia, ib, ic, target))
+
+    def region(p, which, core):
+        owner = which if p.square else 0
+        owners = 4 if p.square else 1
+        if p.shared:
+            owner, owners = owner * 2 + core, owners * 2
+        rows = p.rows // (owners * p.parts)
+        return rows, pl.multiple_of((owner * p.parts + p.part) * rows, rows)
+
+    def landed(i, s, which, core, half=None):
+        p = pieces[i]
+        rows, start = region(p, which, core)
+        start = start + (ix + size_x - s) % size_x * p.rows
+        if half is not None:
+            rows = rows // 2
+            start = start + half * rows
+        return outs[p.at].at[pl.ds(pl.multiple_of(start, rows), rows), :]
+
+    def relay(i, s, kind, incoming=False):
+        sem = (relay_send.at[i, s, kind], relay_recv.at[i, s, kind])
+        if kind < 4:
+            device = (other_a, ib, ic, ix) if kind in (1, 2) else (ia, other_b, ic, ix)
+            sent = (
+                landed(i, s, corner, ic),
+                landed(i, s, corner, ic),
+                landed(i, s, corner_b, ic, 0),
+                landed(i, s, corner_a, ic, 1),
+            )[kind]
+            came = (
+                landed(i, s, corner_b, ic),
+                landed(i, s, corner_a, ic),
+                landed(i, s, corner_d, ic, 0),
+                landed(i, s, corner_d, ic, 1),
+            )[kind]
+        else:
+            device = (ia, ib, 1 - ic, ix)
+            which, half = ((corner, None), (corner_b, None), (corner_a, None), (corner_d, 0), (corner_d, 1))[
+                kind - 4
+            ]
+            sent = landed(i, s, which, ic, half)
+            came = landed(i, s, which, 1 - ic, half)
+        ref = came if incoming else sent
+        return remote(ref, ref, *sem, device)
+
+    rows = ins[0].shape[0] // n_ctx
+
+    def deal_copy(t, k):
+        e = (own + k) % n_ctx
+        src = ins[t].at[pl.ds(pl.multiple_of(e * rows, rows), rows), :]
+        dst = outs[t].at[pl.ds(pl.multiple_of(own * rows, rows), rows), :]
+        if k == 0:
+            return pltpu.make_async_copy(src, dst, own_sem.at[t])
+        device = (e // 2 // size_b, e // 2 % size_b, e % 2, ix)
+        return remote(src, dst, deal_send.at[t, k], deal_recv.at[t, k], device)
+
+    g = n_in - 1
+
+    def gain_copy(s):
+        if s == 0:
+            return pltpu.make_async_copy(ins[g], outs[g].at[ix], own_sem.at[g])
+        device = (ia, ib, ic, (ix + s) % size_x)
+        return remote(ins[g], outs[g].at[ix], gain_send.at[s], gain_recv.at[s], device)
+
+    def keep_copy(w, out):
+        shard, full = ins[w], outs[w]
+        stage = stages[w - n_dealt]
+        height = shard.shape[0]
+        sem = keep_sem.at[w, out]
+        if out:
+            dst = full.at[pl.ds(pl.multiple_of(ix * height, height), height), :]
+            return pltpu.make_async_copy(stage, dst, sem)
+        src = shard
+        if full.shape[1] != shard.shape[1]:
+            cols = full.shape[1]
+            src = shard.at[:, pl.ds(pl.multiple_of(rank * cols, cols), cols)]
+        return pltpu.make_async_copy(src, stage, sem)
+
+    ahead = 4
+    order = [(i, s) for i in range(len(pieces)) for s in range(1, size_x)]
+    for k in range(n_ctx):
+        deal_copy(0, k).start()
+    for s in range(size_x):
+        gain_copy(s).start()
+    for i, s in order[:ahead]:
+        x_copy(i, s).start()
+    for t in range(1, n_dealt):
+        for k in range(n_ctx):
+            deal_copy(t, k).start()
+    for w in range(n_dealt, n_dealt + n_weights):
+        keep_copy(w, 0).start()
+
+    for n in range(len(order) + 2):
+        if n < n_weights:
+            keep_copy(n_dealt + n, 0).wait()
+            keep_copy(n_dealt + n, 1).start()
+        if n < len(order):
+            i, s = order[n]
+            x_copy(i, s).wait_recv()
+            for kind in (0, 1, 4):
+                if kind in pieces[i].relays:
+                    relay(i, s, kind).start()
+            if n + ahead < len(order):
+                x_copy(i, s).wait_send()
+                x_copy(*order[n + ahead]).start()
+        if 1 <= n <= len(order) and pieces[order[n - 1][0]].square:
+            i, s = order[n - 1]
+            relay(i, s, 0, True).wait_recv()
+            relay(i, s, 2).start()
+            relay(i, s, 1, True).wait_recv()
+            relay(i, s, 3).start()
+            if pieces[i].shared:
+                relay(i, s, 5).start()
+                relay(i, s, 6).start()
+        if n >= 2 and pieces[order[n - 2][0]].square:
+            i, s = order[n - 2]
+            relay(i, s, 2, True).wait_recv()
+            relay(i, s, 3, True).wait_recv()
+            if pieces[i].shared:
+                relay(i, s, 7).start()
+                relay(i, s, 8).start()
+
+    for n, (i, s) in enumerate(order):
+        if n + ahead >= len(order):
+            x_copy(i, s).wait_send()
+        for kind in pieces[i].relays:
+            relay(i, s, kind).wait_send()
+            if kind >= 4:
+                relay(i, s, kind, True).wait_recv()
+    for t in range(n_dealt):
+        for k in range(n_ctx):
+            deal_copy(t, k).wait()
+    for s in range(size_x):
+        gain_copy(s).wait()
+    for w in range(n_dealt, n_dealt + n_weights):
+        keep_copy(w, 1).wait()
+
+
+def fetch(sizes, dealt, shared, split, gains):
+    size_a, size_b, size_x = sizes
+    n_ctx = size_a * size_b * 2
+    ins = dealt + shared + split + [gains]
+    outs = [jax.ShapeDtypeStruct(a.shape, BF) for a in dealt]
+    outs += [jax.ShapeDtypeStruct((size_x * a.shape[0], a.shape[1]), BF) for a in shared]
+    outs += [
+        jax.ShapeDtypeStruct((size_x * a.shape[0], a.shape[1] // (2 * size_x)), BF) for a in split
+    ]
+    outs.append(jax.ShapeDtypeStruct((size_x,) + gains.shape, BF))
+    pieces = []
+    first = len(dealt)
+    pieces.append(Piece(first, shared[0].shape[0], True, True, 0, 1))
+    for part in range(2):
+        for n, a in enumerate(split):
+            pieces.append(Piece(first + len(shared) + n, a.shape[0], True, False, part, 2))
+    for n, a in enumerate(shared[1:]):
+        pieces.append(Piece(first + 1 + n, a.shape[0], False, True, 0, 1))
+    count = len(pieces)
+    sem = pltpu.SemaphoreType.DMA
+    return pl.pallas_call(
+        functools.partial(fetch_kernel, sizes, pieces, len(ins), len(dealt)),
+        in_specs=[pl.BlockSpec(memory_space=pl.ANY)] * len(ins),
+        out_specs=[pl.BlockSpec(memory_space=pl.ANY)] * len(outs),
+        out_shape=outs,
+        scratch_shapes=[
+            pltpu.VMEM((a.shape[0], o.shape[1]), BF)
+            for a, o in zip(ins[len(dealt) : -1], outs[len(dealt) : -1])
+        ]
+        + [
+            sem((len(ins), 2)),
+            sem((len(ins),)),
+            sem((len(dealt), n_ctx)),
+            sem((len(dealt), n_ctx)),
+            sem((size_x,)),
+            sem((size_x,)),
+            sem((count, size_x)),
+            sem((count, size_x)),
+            sem((count, size_x, 9)),
+            sem((count, size_x, 9)),
+        ],
+        compiler_params=pltpu.CompilerParams(
+            collective_id=1, has_side_effects=True, vmem_limit_bytes=48 * 1024 * 1024
+        ),
+        cost_estimate=pl.CostEstimate(
+            flops=0, bytes_accessed=300 * 1024 * 1024, transcendentals=0
+        ),
+        name="fetch",
+    )(*ins)
 
 
 class Job:
@@ -447,31 +696,6 @@
     def from_x(step):
         return (ix + size_x - step) % size_x
 
-    def whole_weight(shard):
-        rows, cols = shard.shape
-        halves = shard.reshape(2, rows // 2, cols)
-        full = jnp.zeros((size_x, 2, rows // 2, cols), shard.dtype)
-        full = lax.dynamic_update_slice(full, halves[None], (ix, 0, 0, 0))
-        mine = pick(halves, ic)
-        for step in range(1, size_x):
-            got = to_x(mine, step)
-            other = to_core(got)
-            full = lax.dynamic_update_slice(full, got[None, None], (from_x(step), ic, 0, 0))
-            full = lax.dynamic_update_slice(full, other[None, None], (from_x(step), 1 - ic, 0, 0))
-        return full.reshape(size_x * rows, cols)
-
-    def rank_columns(shard):
-        rows, cols = shard.shape
-        part = cols // ranks
-        own_part = lax.dynamic_slice(shard, (0, rank * part), (rows, part))
-        full = jnp.zeros((size_x, rows, part), shard.dtype)
-        full = put(full, own_part, ix)
-        for step in range(1, size_x):
-            target = ((ix + step) % size_x) * 2 + ic
-            got = to_x(lax.dynamic_slice(shard, (0, target * part), (rows, part)), step)
-            full = put(full, got, from_x(step))
-        return full.reshape(size_x * rows, part)
-
     def group_rows(array):
         parts = [array, to_core(array)]
         for step in range(1, size_x):
@@ -524,25 +748,21 @@
     own_deal = pick(dealing[0], own)
     deal = (own_deal[:, None] == jnp.arange(tok, dtype=jnp.int32)[None, :]).astype(BF)
 
-    def to_stream(array):
-        return lax.all_to_all(
-            mm(deal, array).astype(BF), CTX, split_axis=0, concat_axis=0, tiled=True
-        )
-
     def from_stream(array):
         dealt = lax.all_to_all(array, CTX, split_axis=0, concat_axis=0, tiled=True)
         return mm_tn(deal, dealt)
 
-    gains = whole_weight(jnp.stack([attn_gain, mlp_gain], 1).reshape(-1, 2)).astype(F32)
-    gain_one = gains[:, 0]
-    gain_two = gains[:, 1]
-    inputs_low = to_stream(tokens[0])
-    w_query = whole_weight(query_weight)
-    w_kv = whole_weight(kv_weight)
-    w_out = whole_weight(out_weight)
-    cot = to_stream(cotangent[0])
-    w_gate = rank_columns(gate_weight)
-    w_up = rank_columns(up_weight)
+    gains = jnp.stack([attn_gain, mlp_gain]).reshape(-1, 128)
+    inputs_low, cot, w_query, w_kv, w_out, w_gate, w_up, gains = fetch(
+        sizes,
+        [mm(deal, tokens[0]).astype(BF), mm(deal, cotangent[0]).astype(BF)],
+        [query_weight, kv_weight, out_weight],
+        [gate_weight, up_weight],
+        gains,
+    )
+    gains = gains.reshape(size_x, 2, -1).astype(F32)
+    gain_one = gains[:, 0].reshape(-1)
+    gain_two = gains[:, 1].reshape(-1)
     down_part = down_weight.shape[0] // 2
     w_down = lax.dynamic_slice(down_weight, (ic * down_part, 0), (down_part, width))
 

time: 857 us -> 735 us (0.86)
  waiting for transfers between devices: 260 us -> 93.5 us
  Pallas kernels: 212 us -> 332 us
  local copies, waits for them, and re-layouts: 104 us -> 58.1 us
  starting transfers between devices: 85.6 us -> 59 us
    ppermute x15 -> x9, waiting for transfers between devices: 177 us -> 56.5 us  [to_x(): lax.ppermute(array, 'x', [(i, (i + step) % size_x) for i in range(size_x)])]
    pallas_call x0 -> x1, Pallas kernels: none -> 109 us  [fetch(): pl.pallas_call(functools.partial(fetch_kernel, sizes, pieces, len(ins), l...]
    dynamic_update_slice x15 -> x0, local copies, waits for them, and re-layouts: 29.2 us -> none  [the longest x4 15 us: put(): return lax.dynamic_update_index_in_dim(array, part, index, axis)]
    all_to_all x2, waiting for transfers between devices: 19.8 us -> 0.01 us  [from_stream(): dealt = lax.all_to_all(array, CTX, split_axis=0, concat_axis=0, tiled=True)]
    all_to_all x2 -> x0, waiting for transfers between devices: 13.7 us -> none  [to_stream(): lax.all_to_all(mm(deal, array).astype(BF), CTX, split_axis=0, concat_axis...]
    another operation x8 -> x2, local copies, waits for them, and re-layouts: 13.3 us -> 0.01 us  [on_device(): gains = jnp.stack([attn_gain, mlp_gain]).reshape(-1, 128)]
    all_to_all x2 -> x0, starting transfers between devices: 12.1 us -> none  [to_stream(): lax.all_to_all(mm(deal, array).astype(BF), CTX, split_axis=0, concat_axis...]
    pallas_call x1, Pallas kernels: 185 us -> 195 us  [sum_grads(): pl.pallas_call(functools.partial(grads_kernel, sizes, jobs, len(lefts), l...]
  transfers between devices with their start and end apart: 59 -> 47, of which waited for: 24 -> 9; matrix products, arithmetic and copies ran while one was open for 31% -> 29% of each run, Pallas kernels for 25% -> 31%
where the time goes in v3:
time: 735 us; the launch traced here: 729 us
  Pallas kernels  332 us (45%)
  matrix products  126 us (17%)
  waiting for transfers between devices  93.5 us (13%)
  starting transfers between devices  59 us (8%)
  local copies, waits for them, and re-layouts  58.1 us (8%)
  other arithmetic  45.3 us (6%)
  between operations  15.1 us (2%)
    pallas_call x1, Pallas kernels, sum_grads(): pl.pallas_call(functools.partial(grads_kernel, sizes, jobs, len(lefts), l...  195 us
    pallas_call x1, Pallas kernels, fetch(): pl.pallas_call(functools.partial(fetch_kernel, sizes, pieces, len(ins), l...  109 us
    dot_general x9, matrix products, mm(): return jnp.dot(left, right, preferred_element_type=F32)  57.2 us
    ppermute x9, waiting for transfers between devices, to_x(): lax.ppermute(array, 'x', [(i, (i + step) % size_x) for i in range(size_x)])  56.5 us
    dot_general x8, matrix products, mm_nt(): lax.dot_general(left, right, (((1,), (1,)), ((), ())), preferred_element_...  55.3 us
    ppermute x1, waiting for transfers between devices, sum_rows(): return lax.ppermute(summed, ALL, keep_pairs).astype(F32)  29.7 us
    ppermute x8, starting transfers between devices, shift_ctx(): return lax.ppermute(array, CTX, pairs)  23.5 us
    pallas_call x1, Pallas kernels, attend_back(): pl.pallas_call(attend_back_kernel, grid=(blocks, groups), in_specs=[pl.Bl...  17 us
  transfers between devices with their start and end apart: 47, of which 9 were waited for; matrix products, arithmetic and copies ran while one was open for 29% of the time, Pallas kernels for 31%

profile of v3, /device:TPU:20, one launch (start us, length us, event | category | flops | bytes accessed | tf_op | source)
XLA Modules:
  0.0 728.9 jit_solution(4142818256476207651)
XLA Ops:
  13.9 109.4 %fetch.1 = (bf16[256,2048]{1,0:T(8,128)(2,1)S(1)}, bf16[256,2048]{1,0:T(8,128)(2,1)S(1)}, bf16[2048,2048]{1,0:T(8,128)(2,1)}, bf16[2048,256]{1,0:T(8,128)(2,1)S(...) custom-call(bf16[256,2048]{1,0:T(8,128)(2,1)S(1)} %copy-done.4, ...), custom_call_target="tpu_custom_call" | custom-call | bytes 314572800 | tf_op jit(solution)/shard_map/fetch/pallas_call | solution.py:398
  138.6 7.0 convolution_convert_fusion.5.q_ref
  149.1 10.6 %attend.1 = (bf16[256,2048]{1,0:T(8,128)(2,1)S(1)}, f32[8,1,512]{2,1,0:T(1,128)S(1)}) custom-call(s32[1,256]{1,0:T(1,128)S(1)} %maximum_subtract_fusion.lo_ref, bf16[256,2048]{1,0:T(8,128)(2,1)S(1)} %copy-done.12, bf16[1280,256]{1,0:T(8,128)(2,1)S(1)} %constant_dynamic-update-slice_fusion.kv_ref), custom_call_target="tpu_custom_call" | custom-call | flops 2415919104 | bytes 4194304 | tf_op jit(solution)/shard_map/attend/pallas_call | solution.py:99
  175.1 17.4 %collective-permute-done.5 = bf16[256,2048]{1,0:T(8,128)(2,1)} collective-permute-done((bf16[256,2048]{1,0:T(8,128)(2,1)}, bf16[256,2048]{1,0:T(8,128)(2,1)}, u32[]{:S(2)}, u32[]{:S(2)}) %collective-permute-start.5) | collective-permute-done | bytes 1048608 | tf_op jit(solution)/shard_map/ppermute | solution.py:690
  205.9 13.1 %fusion.55 = f32[1024,1536]{1,0:T(8,128)} fusion(bf16[2048,1536]{1,0:T(8,128)(2,1)} %get-tuple-element.34, bf16[256,2048]{1,0:T(8,128)(2,1)} %collective-permute-done.6, bf16[256,2048]{1,0:T(8,128)(2,1)} %collective-permute-done.5, bf16[256,2048]{1,0:T(8,128)(2,1)} %collective-permute-done.4, bf16[256,2048]{1,0:T(8,128)(2,1)} %multiply_convert_fusion.2), kind=kOutput, calls=%fused_computation.134 | convolution fusion | flops 6459228160 | bytes 16777216 | tf_op jit(solution)/shard_map/dot_general | solution.py:30
  219.0 11.9 %fusion.56 = f32[1024,1536]{1,0:T(8,128)} fusion(bf16[2048,1536]{1,0:T(8,128)(2,1)S(1)} %bitcast.104, bf16[256,2048]{1,0:T(8,128)(2,1)} %collective-permute-done.6, bf16[256,2048]{1,0:T(8,128)(2,1)} %collective-permute-done.5, bf16[256,2048]{1,0:T(8,128)(2,1)} %collective-permute-done.4, bf16[256,2048]{1,0:T(8,128)(2,1)} %multiply_convert_fusion.2), kind=kOutput, calls=%fused_computation.135 | convolution fusion | flops 6459228160 | bytes 16777216 | tf_op jit(solution)/shard_map/dot_general | solution.py:30
  230.9 16.9 %multiply_convert_fusion = (bf16[1024,1536]{1,0:T(8,128)(2,1)}, bf16[1024,1536]{1,0:T(8,128)(2,1)}, bf16[1024,1536]{1,0:T(8,128)(2,1)S(1)}) fusion(f32[1024,1536]{1,0:T(8,128)} %fusion.56, f32[1024,1536]{1,0:T(8,128)} %fusion.55, bf16[1024,2048]{1,0:T(8,128)(2,1)S(1)} %copy-done.31, bf16[3072,2048]{1,0:T(8,128)(2,1)} %param.22, s32[]{:T(128)S(6)} %select_n.44), kind=kOutput, calls=%fused_computation.10 | convolution fusion | flops 6483345408 | bytes 32505860 | tf_op jit(solution)/shard_map/dot_general | solution.py:38
  247.8 8.8 %fusion.11 = f32[512,2048]{1,0:T(8,128)} fusion(bf16[3072,2048]{1,0:T(8,128)(2,1)} %param.22, s32[]{:T(128)S(6)} %select_n.44, bf16[1024,1536]{1,0:T(8,128)(2,1)S(1)} %get-tuple-element.52), kind=kOutput, calls=%fused_computation.17 | convolution fusion | flops 3221225472 | bytes 12058628 | tf_op jit(solution)/shard_map/dot_general | solution.py:30
  256.6 8.6 %convolution_convert_fusion = bf16[1536,2048]{1,0:T(8,128)(2,1)} fusion(bf16[1024,1536]{1,0:T(8,128)(2,1)S(1)} %get-tuple-element.52, bf16[1024,2048]{1,0:T(8,128)(2,1)S(1)} %copy-done.31), kind=kOutput, calls=%fused_computation.2 | convolution fusion | flops 6445596672 | bytes 13631488 | tf_op jit(solution)/shard_map/dot_general | solution.py:34
  265.2 6.2 fusion.36
  280.3 6.2 fusion.33
  314.0 10.9 %collective-permute-done.14 = bf16[256,2048]{1,0:T(8,128)(2,1)} collective-permute-done((bf16[256,2048]{1,0:T(8,128)(2,1)}, bf16[256,2048]{1,0:T(8,128)(2,1)}, u32[]{:S(2)}, u32[]{:S(2)}) %collective-permute-start.14) | collective-permute-done | bytes 1048608 | tf_op jit(solution)/shard_map/ppermute | solution.py:690
  328.3 17.9 %collective-permute-done.8 = bf16[256,2048]{1,0:T(8,128)(2,1)} collective-permute-done((bf16[256,2048]{1,0:T(8,128)(2,1)}, bf16[256,2048]{1,0:T(8,128)(2,1)}, u32[]{:S(2)}, u32[]{:S(2)}) %collective-permute-start.8) | collective-permute-done | bytes 1048608 | tf_op jit(solution)/shard_map/ppermute | solution.py:690
  346.2 6.0 fusion.57
  352.2 6.2 convolution_convert_fusion.4.do_ref
  358.5 17.0 %attend_back.1 = (bf16[256,2048]{1,0:T(8,128)(2,1)S(1)}, f32[1280,256]{1,0:T(8,128)S(1)}) custom-call(s32[1,256]{1,0:T(1,128)S(1)} %maximum_subtract_fusion.lo_ref, bf16[256,2048]{1,0:T(8,128)(2,1)S(1)} %copy-done.13, bf16[1280,256]{1,0:T(8,128)(2,1)S(1)} %copy-done.11, bf16[256,2048]{1,0:T(8,128)(2,1)S(1)} %convolution_convert_fusion.4.do_ref, ...), custom_call_target="tpu_custom_call" | custom-call | flops 6039797760 | bytes 6291456 | tf_op jit(solution)/shard_map/attend_back/pallas_call | solution.py:127
  396.1 6.4 copy.46.refs_1_
  405.2 7.2 all-to-all-start
  417.8 7.7 %fusion.24 = (f32[2048]{0:T(1024)S(1)}, f32[256]{0:T(256)S(1)}, f32[256,2048]{1,0:T(8,128)}) fusion(bf16[256,2048]{1,0:T(8,128)(2,1)S(1)} %get-tuple-element.27, f32[256]{0:T(256)S(1)} %copy-done.38, f32[2048]{0:T(1024)S(1)} %bitcast.95, f32[256,2048]{1,0:T(8,128)S(1)} %fusion.60, bf16[256,2048]{1,0:T(8,128)(2,1)S(1)} %copy-done.8, ...), kind=kOutput, calls=%fused_computation.45 | convolution fusion | flops 2151675648 | bytes 14698496 | tf_op jit(solution)/shard_map/dot_general | solution.py:38
  437.6 6.6 copy.45.refs_0_
  461.3 10.2 %collective-permute-done.31 = bf16[512,512]{1,0:T(8,128)(2,1)S(1)} collective-permute-done((bf16[512,512]{1,0:T(8,128)(2,1)S(1)}, bf16[512,512]{1,0:T(8,128)(2,1)S(1)}, u32[]{:S(2)}, u32[]{:S(2)}) %collective-permute-start.31) | collective-permute-done | bytes 524320 | tf_op jit(solution)/shard_map/ppermute | solution.py:690
  472.6 6.2 all-to-all-start.1
  485.2 195.1 %sum_grads.1 = (bf16[4,64,1536]{2,1,0:T(8,128)(2,1)}, bf16[4,64,1536]{2,1,0:T(8,128)(2,1)}, bf16[4,64,512]{2,1,0:T(8,128)(2,1)}, bf16[64,2048]{1,0:T(8,128)(2,1)}, bf16[64,256]{1,0:T(8,128)(2,1)}) custom-call(bf16[2048,1024]{1,0:T(8,128)(2,1)} %copy.45.refs_0_, bf16[2048,1024]{1,0:T(8,128)(2,1)} %copy.46.refs_1_, ...), custom_call_target="tpu_custom_call" | custom-call | flops 17448304640 | bytes 419430400 | tf_op jit(solution)/shard_map/sum_grads/pallas_call | solution.py:612
  690.8 29.7 %collective-permute-done.43 = bf16[192,2048]{1,0:T(8,128)(2,1)S(1)} collective-permute-done((bf16[192,2048]{1,0:T(8,128)(2,1)}, bf16[192,2048]{1,0:T(8,128)(2,1)S(1)}, u32[]{:S(2)}, u32[]{:S(2)}) %collective-permute-start.43) | collective-permute-done | bytes 786464 | tf_op jit(solution)/shard_map/ppermute | solution.py:737
  (269 shorter events, 170.6 us)
Async XLA Ops:
  7.2 673.1 %reduce-scatter.2.cloned.1.call-start = ((), (), s32[]{:S(2)}) async-start(), calls=%async_computation.3 | async-start | bytes 7077888 | tf_op jit(solution)/shard_map/reduce_scatter | solution.py:729
  137.0 37.6 %collective-permute-start.11 = (bf16[256,2048]{1,0:T(8,128)(2,1)S(1)}, bf16[256,2048]{1,0:T(8,128)(2,1)}, u32[]{:S(2)}, u32[]{:S(2)}) collective-permute-start(bf16[256,2048]{1,0:T(8,128)(2,1)S(1)} %copy-done.6), channel_id=1, source_target_pairs={{0,1},{1,0},{2,3},{3,2},{4,5},{5,4},{6,7},{7,6},{8,9},{9,8},{10,11... | collective-permute-start | bytes 3145736 | tf_op jit(solution)/shard_map/ppermute | solution.py:690
  167.3 25.2 %collective-permute-start.5 = (bf16[256,2048]{1,0:T(8,128)(2,1)}, bf16[256,2048]{1,0:T(8,128)(2,1)}, u32[]{:S(2)}, u32[]{:S(2)}) collective-permute-start(bf16[256,2048]{1,0:T(8,128)(2,1)} %multiply_convert_fusion.2), channel_id=1, source_target_pairs={{0,1},{1,0},{2,3},{3,2},{4,5},{5,4},{6,7},{7,6},{8,9},{9,8},{10,11... | collective-permute-start | bytes 3145736 | tf_op jit(solution)/shard_map/ppermute | solution.py:690
  167.8 29.5 %collective-permute-start.10 = (bf16[256,2048]{1,0:T(8,128)(2,1)S(1)}, bf16[256,2048]{1,0:T(8,128)(2,1)}, u32[]{:S(2)}, u32[]{:S(2)}) collective-permute-start(bf16[256,2048]{1,0:T(8,128)(2,1)S(1)} %copy-done.6), channel_id=1, source_target_pairs={{0,2},{2,0},{1,3},{3,1},{4,6},{6,4},{5,7},{7,5},{8,10},{10,8},{9,1... | collective-permute-start | bytes 3145736 | tf_op jit(solution)/shard_map/ppermute | solution.py:687
  174.6 28.8 %collective-permute-start.12 = (bf16[256,2048]{1,0:T(8,128)(2,1)}, bf16[256,2048]{1,0:T(8,128)(2,1)}, u32[]{:S(2)}, u32[]{:S(2)}) collective-permute-start(bf16[256,2048]{1,0:T(8,128)(2,1)} %collective-permute-done.11), channel_id=1, source_target_pairs={{0,2},{2,0},{1,3},{3,1},{4,6},{6,4},{5,7},{7,5},{8,10},{10,8},{9,1... | collective-permute-start | bytes 3145736 | tf_op jit(solution)/shard_map/ppermute | solution.py:687
  174.6 31.3 %collective-permute-start.4 = (bf16[256,2048]{1,0:T(8,128)(2,1)}, bf16[256,2048]{1,0:T(8,128)(2,1)}, u32[]{:S(2)}, u32[]{:S(2)}) collective-permute-start(bf16[256,2048]{1,0:T(8,128)(2,1)} %multiply_convert_fusion.2), channel_id=1, source_target_pairs={{0,2},{2,0},{1,3},{3,1},{4,6},{6,4},{5,7},{7,5},{8,10},{10,8},{9,1... | collective-permute-start | bytes 3145736 | tf_op jit(solution)/shard_map/ppermute | solution.py:687
  193.8 119.7 %collective-permute-start.26 = (bf16[256,2048]{1,0:T(8,128)(2,1)}, bf16[256,2048]{1,0:T(8,128)(2,1)}, u32[]{:S(2)}, u32[]{:S(2)}) collective-permute-start(bf16[256,2048]{1,0:T(8,128)(2,1)} %fusion.18), channel_id=1, source_target_pairs={{0,1},{1,0},{2,3},{3,2},{4,5},{5,4},{6,7},{7,6},{8,9},{9,8},{10,11... | collective-permute-start | bytes 3145736 | tf_op jit(solution)/shard_map/ppermute | solution.py:690
  197.3 110.0 %collective-permute-start.29 = (bf16[512,512]{0,1:T(8,128)(2,1)}, bf16[512,512]{0,1:T(8,128)(2,1)}, u32[]{:S(2)}, u32[]{:S(2)}) collective-permute-start(bf16[512,512]{0,1:T(8,128)(2,1)} %copy.51), channel_id=1, source_target_pairs={{0,1},{1,0},{2,3},{3,2},{4,5},{5,4},{6,7},{7,6},{8,9},{9,8},{10,11... | collective-permute-start | bytes 1572872 | tf_op jit(solution)/shard_map/ppermute | solution.py:690
  298.5 26.4 %collective-permute-start.14 = (bf16[256,2048]{1,0:T(8,128)(2,1)}, bf16[256,2048]{1,0:T(8,128)(2,1)}, u32[]{:S(2)}, u32[]{:S(2)}) collective-permute-start(bf16[256,2048]{1,0:T(8,128)(2,1)} %fusion.27), channel_id=1, source_target_pairs={{0,1},{1,0},{2,3},{3,2},{4,5},{5,4},{6,7},{7,6},{8,9},{9,8},{10,11... | collective-permute-start | bytes 3145736 | tf_op jit(solution)/shard_map/ppermute | solution.py:690
  305.8 22.5 %collective-permute-start.9 = (bf16[256,2048]{1,0:T(8,128)(2,1)}, bf16[256,2048]{1,0:T(8,128)(2,1)}, u32[]{:S(2)}, u32[]{:S(2)}) collective-permute-start(bf16[256,2048]{1,0:T(8,128)(2,1)} %slice.153), channel_id=1, source_target_pairs={{0,2},{2,0},{1,3},{3,1},{4,6},{6,4},{5,7},{7,5},{8,10},{10,8},{9,1... | collective-permute-start | bytes 3145736 | tf_op jit(solution)/shard_map/ppermute | solution.py:687
  307.2 39.0 %collective-permute-start.8 = (bf16[256,2048]{1,0:T(8,128)(2,1)}, bf16[256,2048]{1,0:T(8,128)(2,1)}, u32[]{:S(2)}, u32[]{:S(2)}) collective-permute-start(bf16[256,2048]{1,0:T(8,128)(2,1)} %fusion.31), channel_id=1, source_target_pairs={{0,1},{1,0},{2,3},{3,2},{4,5},{5,4},{6,7},{7,6},{8,9},{9,8},{10,11... | collective-permute-start | bytes 3145736 | tf_op jit(solution)/shard_map/ppermute | solution.py:690
  313.4 75.3 %collective-permute-start.25 = (bf16[256,2048]{1,0:T(8,128)(2,1)}, bf16[256,2048]{1,0:T(8,128)(2,1)S(1)}, u32[]{:S(2)}, u32[]{:S(2)}) collective-permute-start(bf16[256,2048]{1,0:T(8,128)(2,1)} %fusion.18), channel_id=1, source_target_pairs={{0,2},{2,0},{1,3},{3,1},{4,6},{6,4},{5,7},{7,5},{8,10},{10,8},{9,1... | collective-permute-start | bytes 3145736 | tf_op jit(solution)/shard_map/ppermute | solution.py:687
  313.5 78.6 %collective-permute-start.27 = (bf16[256,2048]{1,0:T(8,128)(2,1)}, bf16[256,2048]{1,0:T(8,128)(2,1)S(1)}, u32[]{:S(2)}, u32[]{:S(2)}) collective-permute-start(bf16[256,2048]{1,0:T(8,128)(2,1)} %collective-permute-done.26), channel_id=1, source_target_pairs={{0,2},{2,0},{1,3},{3,1},{4,6},{6,4},{5,7},{7,5},{8,10},{10,8},{9,1... | collective-permute-start | bytes 3145736 | tf_op jit(solution)/shard_map/ppermute | solution.py:687
  377.9 36.1 %collective-permute-start.16 = (bf16[256,256]{1,0:T(8,128)(2,1)}, bf16[256,256]{1,0:T(8,128)(2,1)}, u32[]{:S(2)}, u32[]{:S(2)}) collective-permute-start(bf16[256,256]{1,0:T(8,128)(2,1)} %get-tuple-element.62), channel_id=1, source_target_pairs={{8,0},{10,2},{12,4},{14,6},{16,8},{18,10},{20,12},{22,14},{24,16},... | collective-permute-start | bytes 393224 | tf_op jit(solution)/shard_map/ppermute | solution.py:694
  383.3 32.2 %collective-permute-start.17 = (bf16[256,256]{1,0:T(8,128)(2,1)}, bf16[256,256]{1,0:T(8,128)(2,1)}, u32[]{:S(2)}, u32[]{:S(2)}) collective-permute-start(bf16[256,256]{1,0:T(8,128)(2,1)} %get-tuple-element.65), channel_id=1, source_target_pairs={{6,0},{8,2},{10,4},{12,6},{14,8},{16,10},{18,12},{20,14},{22,16},{... | collective-permute-start | bytes 393224 | tf_op jit(solution)/shard_map/ppermute | solution.py:694
  386.5 29.0 %collective-permute-start.18 = (bf16[256,256]{1,0:T(8,128)(2,1)}, bf16[256,256]{1,0:T(8,128)(2,1)}, u32[]{:S(2)}, u32[]{:S(2)}) collective-permute-start(bf16[256,256]{1,0:T(8,128)(2,1)} %get-tuple-element.64), channel_id=1, source_target_pairs={{4,0},{6,2},{8,4},{10,6},{12,8},{14,10},{16,12},{18,14},{20,16},{2... | collective-permute-start | bytes 393224 | tf_op jit(solution)/shard_map/ppermute | solution.py:694
  388.8 26.7 %collective-permute-start.19 = (bf16[256,256]{1,0:T(8,128)(2,1)}, bf16[256,256]{1,0:T(8,128)(2,1)}, u32[]{:S(2)}, u32[]{:S(2)}) collective-permute-start(bf16[256,256]{1,0:T(8,128)(2,1)} %get-tuple-element.63), channel_id=1, source_target_pairs={{2,0},{4,2},{6,4},{8,6},{10,8},{12,10},{14,12},{16,14},{18,16},{20... | collective-permute-start | bytes 393224 | tf_op jit(solution)/shard_map/ppermute | solution.py:694
  405.2 67.4 %all-to-all-start = ((bf16[16,16,2048]{2,1,0:T(8,128)(2,1)}), bf16[16,16,2048]{2,1,0:T(8,128)(2,1)}, u32[]{:S(2)}, u32[]{:S(2)}) async-start(bf16[16,16,2048]{2,1,0:T(8,128)(2,1)} %bitcast.81), calls=%async_computation | async-start | bytes 2097152 | tf_op jit(solution)/shard_map/all_to_all | solution.py:752
  412.4 45.9 %collective-permute-start.33 = (bf16[256,2048]{1,0:T(8,128)(2,1)}, bf16[256,2048]{1,0:T(8,128)(2,1)}, u32[]{:S(2)}, u32[]{:S(2)}) collective-permute-start(bf16[256,2048]{1,0:T(8,128)(2,1)} %copy-done.20), channel_id=1, source_target_pairs={{0,1},{1,0},{2,3},{3,2},{4,5},{5,4},{6,7},{7,6},{8,9},{9,8},{10,11... | collective-permute-start | bytes 3145736 | tf_op jit(solution)/shard_map/ppermute | solution.py:690
  429.6 26.4 %collective-permute-start.30 = (bf16[256,2,512]{2,0,1:T(8,128)(2,1)}, bf16[256,2,512]{2,0,1:T(8,128)(2,1)}, u32[]{:S(2)}, u32[]{:S(2)}) collective-permute-start(bf16[256,2,512]{2,0,1:T(8,128)(2,1)} %bitcast.76), channel_id=1, source_target_pairs={{0,2},{2,0},{1,3},{3,1},{4,6},{6,4},{5,7},{7,5},{8,10},{10,8},{9,1... | collective-permute-start | bytes 1572872 | tf_op jit(solution)/shard_map/ppermute | solution.py:687
  444.2 37.4 %collective-permute-start.32 = (bf16[256,2048]{1,0:T(8,128)(2,1)}, bf16[256,2048]{1,0:T(8,128)(2,1)}, u32[]{:S(2)}, u32[]{:S(2)}) collective-permute-start(bf16[256,2048]{1,0:T(8,128)(2,1)} %copy-done.20), channel_id=1, source_target_pairs={{0,2},{2,0},{1,3},{3,1},{4,6},{6,4},{5,7},{7,5},{8,10},{10,8},{9,1... | collective-permute-start | bytes 3145736 | tf_op jit(solution)/shard_map/ppermute | solution.py:687
  458.3 23.3 %collective-permute-start.34 = (bf16[256,2048]{1,0:T(8,128)(2,1)}, bf16[256,2048]{1,0:T(8,128)(2,1)}, u32[]{:S(2)}, u32[]{:S(2)}) collective-permute-start(bf16[256,2048]{1,0:T(8,128)(2,1)} %collective-permute-done.33), channel_id=1, source_target_pairs={{0,2},{2,0},{1,3},{3,1},{4,6},{6,4},{5,7},{7,5},{8,10},{10,8},{9,1... | collective-permute-start | bytes 3145736 | tf_op jit(solution)/shard_map/ppermute | solution.py:687
  472.6 216.3 %all-to-all-start.1 = ((bf16[16,16,2048]{2,1,0:T(8,128)(2,1)}), bf16[16,16,2048]{2,1,0:T(8,128)(2,1)S(1)}, u32[]{:S(2)}, u32[]{:S(2)}) async-start(bf16[16,16,2048]{2,1,0:T(8,128)(2,1)} %bitcast.80), calls=%async_computation.1 | async-start | bytes 2097152 | tf_op jit(solution)/shard_map/all_to_all | solution.py:752
  680.3 40.3 %collective-permute-start.43 = (bf16[192,2048]{1,0:T(8,128)(2,1)}, bf16[192,2048]{1,0:T(8,128)(2,1)S(1)}, u32[]{:S(2)}, u32[]{:S(2)}) collective-permute-start(bf16[192,2048]{1,0:T(8,128)(2,1)} %reduce-scatter.2.cloned.1.call-done), channel_id=1, source_target_pairs={{0,0},{1,16},{2,8},{3,24},{4,1},{5,17},{6,9},{7,25},{8,2},{9,18},{... | collective-permute-start | bytes 2359304 | tf_op jit(solution)/shard_map/ppermute | solution.py:737
  (71 other events, 746.0 us)
Sparse Core Ops, SparseCore 0:
  280.4 122.7 reduce-scatter.1

commit v4 on v3

--- a/solution.py
+++ b/solution.py
@@ -432,21 +432,25 @@
         self.rows, self.cols, self.by_rank = rows, cols, by_rank
 
 
-def grads_kernel(sizes, jobs, n_left, n_right, *refs):
+def grads_kernel(sizes, jobs, *refs):
     size_a, size_b, size_x = sizes
     chips = size_a * size_b
+    n_ctx = 2 * chips
     ranks = 2 * size_x
     count = len(jobs)
-    lefts_in, refs = refs[:n_left], refs[n_left:]
-    rights_in, refs = refs[:n_right], refs[n_right:]
+    ins, refs = refs[:11], refs[11:]
     outs, refs = refs[:count], refs[count:]
-    lefts, refs = refs[:n_left], refs[n_left:]
-    rights, refs = refs[:n_right], refs[n_right:]
+    dealt, refs = refs[:2], refs[2:]
+    gain_out, refs = refs[0], refs[1:]
+    held, refs = refs[:8], refs[8:]
+    gain_ctx, gain_x, refs = refs[0], refs[1], refs[2:]
     recv, refs = refs[:count], refs[count:]
     send, refs = refs[:count], refs[count:]
     done, refs = refs[:count], refs[count:]
-    load_sem, send_sem, recv_sem, done_send, done_recv, own_sem = refs
+    load_sem, group_send, group_recv, deal_send, deal_recv = refs[:5]
+    gain_send, gain_recv, send_sem, recv_sem, done_send, done_recv, own_sem = refs[5:]
     ia, ib, ic, ix = (lax.axis_index(name) for name in ALL)
+    own = (ia * size_b + ib) * 2 + ic
     rank = ix * 2 + ic
     place = snake_place(ia, ib, size_a, size_b)
 
@@ -455,11 +459,15 @@
 
     def member(k):
         return (ic + k // size_x) % 2, (ix + k % size_x) % size_x
+
+    def ctx_device(k):
+        e = (own + k) % n_ctx
+        return e // 2 // size_b, e // 2 % size_b, e % 2, ix
 
     kept = rank * chips + kept_slot(ia, ib, size_a, size_b)
     kept_chip = kept // ranks
     kept_id = (kept_chip // size_b, kept_chip % size_b, (kept // size_x) % 2, kept % size_x)
-    flat = ((ia * size_b + ib) * 2 + ic) * size_x + ix
+    flat = own * size_x + ix
     from_rank = flat // chips
     from_slot = flat % chips
     half = chips // 2
@@ -470,91 +478,126 @@
         from_rank // 2,
     )
 
-    loads = []
-    for i, (src, dst) in enumerate(zip(lefts_in + rights_in, lefts + rights)):
-        loads.append(pltpu.make_async_copy(src, dst, load_sem.at[i]))
+    def remote(src, dst, sent, came, device):
+        return pltpu.make_async_remote_copy(
+            src_ref=src,
+            dst_ref=dst,
+            send_sem=sent,
+            recv_sem=came,
+            device_id=device,
+            device_id_type=MESH,
+        )
+
+    loads = [pltpu.make_async_copy(ins[i], held[i], load_sem.at[i]) for i in range(3)]
     for copy in loads:
         copy.start()
 
     barrier = pltpu.get_barrier_semaphore()
-    greeted = [on_ring(1) + (ic, ix), on_ring(-1) + (ic, ix), from_id]
-    greeted += [(ia, ib) + member(k) for k in range(1, ranks)]
+    greeted = [ctx_device(k) for k in range(1, n_ctx)] + [from_id]
+    greeted += [(ia, ib) + member(k) for k in range(ranks) if k % size_x]
     for device in greeted:
         pl.semaphore_signal(barrier, inc=1, device_id=device, device_id_type=MESH)
     pl.semaphore_wait(barrier, len(greeted))
 
+    def group_copy(i, k):
+        c, x = member(k)
+        src, dst = ins[i], held[i].at[k]
+        target = x * 2 + c
+        if i == 4:
+            rows = held[i].shape[1]
+            src = src.at[pl.ds(pl.multiple_of(target * rows, rows), rows), :]
+        if i == 6:
+            cols = held[i].shape[2]
+            src = src.at[:, pl.ds(pl.multiple_of(target * cols, cols), cols)]
+        if k == 0:
+            return pltpu.make_async_copy(src, dst, load_sem.at[i])
+        return remote(src, dst, group_send.at[i, k], group_recv.at[i, k], (ia, ib, c, x))
+
+    def deal_copy(t, k):
+        e = (own + k) % n_ctx
+        rows = ins[8 + t].shape[0] // n_ctx
+        src = ins[8 + t].at[pl.ds(pl.multiple_of(e * rows, rows), rows), :]
+        dst = dealt[t].at[pl.ds(pl.multiple_of(own * rows, rows), rows), :]
+        if k == 0:
+            return pltpu.make_async_copy(src, dst, load_sem.at[8 + t])
+        return remote(src, dst, deal_send.at[t, k], deal_recv.at[t, k], ctx_device(k))
+
+    def gain_copy(k):
+        src, dst = ins[10].at[(own + k) % n_ctx], gain_ctx.at[k]
+        if k == 0:
+            return pltpu.make_async_copy(src, dst, load_sem.at[10])
+        return remote(src, dst, deal_send.at[2, k], deal_recv.at[2, k], ctx_device(k))
+
+    def gain_copy_x(s):
+        device = (ia, ib, ic, (ix + s) % size_x)
+        return remote(gain_x.at[0], gain_x.at[s], gain_send.at[s], gain_recv.at[s], device)
+
     def ring_copy(j, way, step, parity):
         neighbour = on_ring(1 - 2 * way) + (ic, ix)
-        return pltpu.make_async_remote_copy(
-            src_ref=send[j].at[way, parity],
-            dst_ref=recv[j].at[way, step],
-            send_sem=send_sem.at[j, way, parity],
-            recv_sem=recv_sem.at[j, way, step],
-            device_id=neighbour,
-            device_id_type=MESH,
+        return remote(
+            send[j].at[way, parity],
+            recv[j].at[way, step],
+            send_sem.at[j, way, parity],
+            recv_sem.at[j, way, step],
+            neighbour,
         )
 
     def product(j, way, step):
         job = jobs[j]
         a, b = on_ring(step * (2 * way - 1))
         part = job.rows // chips
+        cols = slice(way * job.cols // 2, (way + 1) * job.cols // 2)
+        left, right = held[job.left], held[job.right]
+        if job.phase == 0:
+            start = pl.multiple_of((a * size_b + b) * part, part)
+            return mm_tn(left[:, pl.ds(start, part)], right[:, cols])
         if job.by_rank:
             start = kept_slot(a, b, size_a, size_b) * part
-            if lefts[job.left].shape[0] != job.rows:
+            if left.shape[1] != job.rows:
                 start = start + rank * job.rows
         else:
             start = (a * size_b + b) * part
-        cols = job.cols // 2
-        left = lefts[job.left][pl.ds(pl.multiple_of(start, part), part), :]
-        return jnp.dot(
-            left, rights[job.right][:, way * cols : (way + 1) * cols], preferred_element_type=F32
-        )
+        rows = pl.ds(pl.multiple_of(start, part), part)
+        total = mm(left[0, rows, :], right[0, :, cols])
+        for k in range(1, ranks):
+            total = total + mm(left[k, rows, :], right[k, :, cols])
+        return total
 
     def deliver(j):
         job = jobs[j]
         if job.by_rank:
-            return [
-                pltpu.make_async_remote_copy(
-                    src_ref=done[j],
-                    dst_ref=outs[j],
-                    send_sem=done_send.at[j, 0],
-                    recv_sem=done_recv.at[j, 0],
-                    device_id=kept_id,
-                    device_id_type=MESH,
-                )
-            ]
+            return [remote(done[j], outs[j], done_send.at[j, 0], done_recv.at[j, 0], kept_id)]
         part = job.rows // (chips * ranks)
         copies = []
-        for k in range(1, ranks):
+        for k in range(ranks):
             c, x = member(k)
             start = pl.multiple_of((c * size_x + x) * part, part)
-            copies.append(
-                pltpu.make_async_remote_copy(
-                    src_ref=done[j].at[pl.ds(start, part), :],
-                    dst_ref=outs[j].at[rank],
-                    send_sem=done_send.at[j, k],
-                    recv_sem=done_recv.at[j, k],
-                    device_id=(ia, ib, c, x),
-                    device_id_type=MESH,
+            src, dst = done[j].at[pl.ds(start, part), :], outs[j].at[rank]
+            if k == 0:
+                copies.append(pltpu.make_async_copy(src, dst, own_sem.at[j]))
+            else:
+                copies.append(
+                    remote(src, dst, done_send.at[j, k], done_recv.at[j, k], (ia, ib, c, x))
                 )
-            )
-        start = pl.multiple_of((ic * size_x + ix) * part, part)
-        copies.append(
-            pltpu.make_async_copy(done[j].at[pl.ds(start, part), :], outs[j].at[rank], own_sem.at[j])
-        )
         return copies
 
-    loaded = set()
-    for phase in range(1 + max(job.phase for job in jobs)):
+    for copy in loads:
+        copy.wait()
+    for phase in range(2):
         mine = [j for j in range(count) if jobs[j].phase == phase]
         for j in mine:
-            for i in (jobs[j].left, n_left + jobs[j].right):
-                if i not in loaded:
-                    loaded.add(i)
-                    loads[i].wait()
             for way in range(2):
                 send[j][way, 0] = product(j, way, 1).astype(BF)
                 ring_copy(j, way, 0, 0).start()
+        if phase == 0:
+            for k in range(n_ctx):
+                gain_copy(k).start()
+            for i in range(3, 8):
+                for k in range(ranks):
+                    group_copy(i, k).start()
+            for t in range(2):
+                for k in range(n_ctx):
+                    deal_copy(t, k).start()
 
         def step_of(step, carry):
             parity = step % 2
@@ -573,6 +616,12 @@
             return carry
 
         lax.fori_loop(1, chips - 1, step_of, 0)
+        if phase == 0:
+            for k in range(n_ctx):
+                gain_copy(k).wait()
+            gain_x[0] = jnp.sum(gain_ctx[...], axis=0)
+            for s in range(1, size_x):
+                gain_copy_x(s).start()
         last = chips - 2
         for j in mine:
             cols = jobs[j].cols // 2
@@ -586,15 +635,47 @@
             for way in range(2):
                 ring_copy(j, way, last - 1, (last - 1) % 2).wait_send()
                 ring_copy(j, way, last, last % 2).wait_send()
+        if phase == 0:
+            for i in range(3, 8):
+                for k in range(ranks):
+                    group_copy(i, k).wait()
+    for s in range(1, size_x):
+        gain_copy_x(s).wait()
+    gain_out[...] = jnp.sum(gain_x[...], axis=0)
+    for t in range(2):
+        for k in range(n_ctx):
+            deal_copy(t, k).wait()
     for j in range(count):
         for copy in deliver(j):
             copy.wait()
 
 
-def sum_grads(sizes, jobs, lefts, rights):
+def sum_grads(sizes, ins):
     size_a, size_b, size_x = sizes
     chips = size_a * size_b
     ranks = 2 * size_x
+    normed_mlp, d_gate, d_upward = ins[:3]
+    width = normed_mlp.shape[1]
+    tok = ins[5].shape[0]
+    part_width = width // ranks
+    jobs = [
+        Job(0, 0, 1, width, d_gate.shape[1], False),
+        Job(0, 0, 2, width, d_upward.shape[1], False),
+        Job(1, 3, 6, width, part_width, False),
+        Job(1, 4, 5, part_width, width, True),
+        Job(1, 3, 7, part_width, 2 * HD, True),
+    ]
+    held = [pltpu.VMEM(a.shape, BF) for a in ins[:3]]
+    held += [
+        pltpu.VMEM((ranks,) + shape, BF)
+        for shape in (
+            (width, tok),
+            (part_width, tok),
+            (tok, width),
+            (tok, part_width),
+            (tok, 2 * HD),
+        )
+    ]
     outs, recv, send, done = [], [], [], []
     flops = 0
     for job in jobs:
@@ -606,20 +687,31 @@
         recv.append(pltpu.VMEM((2, chips - 1, part, job.cols // 2), BF))
         send.append(pltpu.VMEM((2, 2, part, job.cols // 2), BF))
         done.append(pltpu.VMEM((part, job.cols), BF))
-        flops += 2 * job.rows * job.cols * rights[job.right].shape[0]
+        flops += 2 * job.rows * job.cols * normed_mlp.shape[0]
     count = len(jobs)
+    outs += [jax.ShapeDtypeStruct((tok, width), BF)] * 2
+    gain_shape = ins[10].shape[1:]
+    outs.append(jax.ShapeDtypeStruct(gain_shape, F32))
     sem = pltpu.SemaphoreType.DMA
     return pl.pallas_call(
-        functools.partial(grads_kernel, sizes, jobs, len(lefts), len(rights)),
-        in_specs=[pl.BlockSpec(memory_space=pl.ANY)] * (len(lefts) + len(rights)),
-        out_specs=[pl.BlockSpec(memory_space=pl.ANY)] * count,
+        functools.partial(grads_kernel, sizes, jobs),
+        in_specs=[pl.BlockSpec(memory_space=pl.ANY)] * len(ins),
+        out_specs=[pl.BlockSpec(memory_space=pl.ANY)] * (count + 2)
+        + [pl.BlockSpec(memory_space=pltpu.VMEM)],
         out_shape=outs,
-        scratch_shapes=[pltpu.VMEM(a.shape, BF) for a in lefts + rights]
+        scratch_shapes=held
+        + [pltpu.VMEM((2 * chips,) + gain_shape, F32), pltpu.VMEM((size_x,) + gain_shape, F32)]
         + recv
         + send
         + done
         + [
-            sem((len(lefts) + len(rights),)),
+            sem((len(ins),)),
+            sem((8, ranks)),
+            sem((8, ranks)),
+            sem((3, 2 * chips)),
+            sem((3, 2 * chips)),
+            sem((size_x,)),
+            sem((size_x,)),
             sem((count, 2, 2)),
             sem((count, 2, chips - 1)),
             sem((count, ranks)),
@@ -633,7 +725,7 @@
             flops=flops, bytes_accessed=400 * 1024 * 1024, transcendentals=0
         ),
         name="sum_grads",
-    )(*lefts, *rights)
+    )(*ins)
 
 
 def norm_stats(values):
@@ -703,18 +795,6 @@
             parts += [got, to_core(got)]
         return jnp.concatenate(parts, 0)
 
-    def group_columns(array):
-        part = array.shape[1] // ranks
-        view = array.reshape(tok, size_x, 2, part)
-        kept = pick(view, ic, 2)
-        got = to_core(pick(view, 1 - ic, 2))
-        both = jnp.stack([kept, got])
-        parts = [pick(both, ix, 2).reshape(2 * tok, part)]
-        for step in range(1, size_x):
-            sent = pick(both, (ix + step) % size_x, 2).reshape(2 * tok, part)
-            parts.append(to_x(sent, step))
-        return jnp.concatenate(parts, 0)
-
     def group_sum(part_of):
         total = None
         for step in list(range(1, size_x)) + [0]:
@@ -736,21 +816,8 @@
                     keep_pairs.append(((g * 2 + c) * size_x + x, (x * 2 + c) * chips + g))
         return lax.ppermute(summed, ALL, keep_pairs).astype(F32)
 
-    def sum_gain(grad):
-        for name, size in (("c", 2), ("x", size_x), ("b", size_b), ("a", size_a)):
-            step = 1
-            while step < size:
-                grad = grad + lax.ppermute(grad, name, [(i, i ^ step) for i in range(size)])
-                step *= 2
-        part = grad.shape[0] // (n_ctx * size_x)
-        return lax.dynamic_slice(grad, (flat * part,), (part,))
-
     own_deal = pick(dealing[0], own)
     deal = (own_deal[:, None] == jnp.arange(tok, dtype=jnp.int32)[None, :]).astype(BF)
-
-    def from_stream(array):
-        dealt = lax.all_to_all(array, CTX, split_axis=0, concat_axis=0, tiled=True)
-        return mm_tn(deal, dealt)
 
     gains = jnp.stack([attn_gain, mlp_gain]).reshape(-1, 128)
     inputs_low, cot, w_query, w_kv, w_out, w_gate, w_up, gains = fetch(
@@ -799,42 +866,48 @@
     )
     down_grad = sum_rows(mm_tn(hidden, cot_rows))
     branch_mlp = group_sum(lambda step: mm(rows_of(hidden, step), w_down))
-    block_output = from_stream((resid + branch_mlp).astype(BF)).astype(BF)
+    block_output = (resid + branch_mlp).astype(BF)
     d_resid_part, mlp_gain_grad = norm_back(unit_two, inv_two, gain_two, d_normed_mlp)
-    mlp_gain_grad = sum_gain(mlp_gain_grad)
     d_resid = cot.astype(F32) + d_resid_part
     d_branch = d_resid.astype(BF)
 
     d_context = mm_nt(d_branch, w_out).astype(BF)
-    context_cols = group_columns(context)
-    branch_rows = group_rows(d_branch)
     d_queries, d_window = attend_back(queries, window, low, d_context, lse)
     d_pairs = d_window[halo * tok :]
     for j in range(halo):
         part = d_window[j * tok : (j + 1) * tok].astype(BF)
         d_pairs = d_pairs + shift_ctx(part, j - halo).astype(F32)
     d_pairs = d_pairs.astype(BF)
-    jobs = [
-        Job(0, 0, 0, width, d_gate.shape[1], False),
-        Job(0, 0, 1, width, d_upward.shape[1], False),
-        Job(1, 1, 2, width, width // ranks, False),
-        Job(1, 2, 3, width // ranks, width, True),
-        Job(1, 1, 4, width // ranks, 2 * HD, True),
-    ]
+    d_normed = mm_nt(d_queries, w_query) + mm_nt(d_pairs, w_kv)
+    d_inputs, attn_gain_grad = norm_back(unit_one, inv_one, gain_one, d_normed)
+    gain_part = width // (n_ctx * size_x)
+    gain_grads = jnp.stack([attn_gain_grad, mlp_gain_grad]).reshape(2, n_ctx, size_x, gain_part)
+    gain_grads = gain_grads.transpose(1, 2, 0, 3).reshape(n_ctx, -1)
+    gain_grads = jnp.pad(gain_grads, ((0, 0), (0, 1024 - gain_grads.shape[1])))
     sums = sum_grads(
         sizes,
-        jobs,
-        [normed_mlp.T, group_rows(normed).T, context_cols.T],
-        [d_gate, d_upward, group_columns(d_queries), branch_rows, group_rows(d_pairs)],
+        [
+            normed_mlp,
+            d_gate,
+            d_upward,
+            normed.T,
+            context.T,
+            d_branch,
+            d_queries,
+            d_pairs,
+            block_output,
+            (d_resid + d_inputs).astype(BF),
+            gain_grads.reshape(n_ctx, 8, 128),
+        ],
     )
     gate_grad, up_grad, query_grad = (
         v.transpose(1, 0, 2).reshape(v.shape[1], -1).astype(F32) for v in sums[:3]
     )
-    out_grad, kv_grad = (v.astype(F32) for v in sums[3:])
-    d_normed = mm_nt(d_queries, w_query) + mm_nt(d_pairs, w_kv)
-    d_inputs, attn_gain_grad = norm_back(unit_one, inv_one, gain_one, d_normed)
-    attn_gain_grad = sum_gain(attn_gain_grad)
-    token_grad = from_stream((d_resid + d_inputs).astype(BF))
+    out_grad, kv_grad = (v.astype(F32) for v in sums[3:5])
+    block_output = mm_tn(deal, sums[5]).astype(BF)
+    token_grad = mm_tn(deal, sums[6])
+    gain_grads = lax.dynamic_slice(sums[7].reshape(-1), (ix * 2 * gain_part,), (2 * gain_part,))
+    attn_gain_grad, mlp_gain_grad = gain_grads[:gain_part], gain_grads[gain_part:]
     return (
         block_output[None],
         token_grad[None],

time: 735 us -> 684 us (0.931)
  Pallas kernels: 332 us -> 370 us
  local copies, waits for them, and re-layouts: 58.1 us -> 24.8 us
  starting transfers between devices: 59 us -> 30.6 us
  other arithmetic: 45.3 us -> 30.4 us
  waiting for transfers between devices: 93.5 us -> 85.7 us
    pallas_call x1, Pallas kernels: 195 us -> 233 us  [sum_grads(): pl.pallas_call(functools.partial(grads_kernel, sizes, jobs), in_specs=[pl...]
    all_to_all x2 -> x0, starting transfers between devices: 13.3 us -> none  [from_stream(): dealt = lax.all_to_all(array, CTX, split_axis=0, concat_axis=0, tiled=True)]
    transpose x2 -> x1, local copies, waits for them, and re-layouts: 13 us -> 2.26 us  [on_device(): sums = sum_grads(sizes, [normed_mlp, d_gate, d_upward, normed.T, context....]
    dynamic_slice x6 -> x1, local copies, waits for them, and re-layouts: 11.1 us -> 0.78 us  [pick(): return lax.dynamic_index_in_dim(array, index, axis, keepdims=False)]
    dot_general x8, matrix products: 55.3 us -> 45.6 us  [mm_nt(): lax.dot_general(left, right, (((1,), (1,)), ((), ())), preferred_element_...]
    transpose x3 -> x1, other arithmetic: 9.69 us -> 0.04 us  [on_device(): gain_grads = gain_grads.transpose(1, 2, 0, 3).reshape(n_ctx, -1)]
    ppermute x10 -> x0, starting transfers between devices: 8.61 us -> none  [sum_gain(): grad = grad + lax.ppermute(grad, name, [(i, i ^ step) for i in range(size)])]
    unnamed x104 -> x101, local copies, waits for them, and re-layouts: 16.4 us -> 9.76 us
  transfers between devices with their start and end apart: 47 -> 22, of which waited for: 9 -> 5; matrix products, arithmetic and copies ran while one was open for 29% -> 18% of each run, Pallas kernels for 31% -> 38%
where the time goes in v4:
time: 684 us; the launch traced here: 679 us
  Pallas kernels  370 us (54%)
  matrix products  122 us (18%)
  waiting for transfers between devices  85.7 us (13%)
  starting transfers between devices  30.6 us (4%)
  other arithmetic  30.4 us (4%)
  local copies, waits for them, and re-layouts  24.8 us (4%)
  between operations  15.4 us (2%)
    pallas_call x1, Pallas kernels, sum_grads(): pl.pallas_call(functools.partial(grads_kernel, sizes, jobs), in_specs=[pl...  233 us
    pallas_call x1, Pallas kernels, fetch(): pl.pallas_call(functools.partial(fetch_kernel, sizes, pieces, len(ins), l...  109 us
    dot_general x9, matrix products, mm(): return jnp.dot(left, right, preferred_element_type=F32)  61.7 us
    ppermute x4, waiting for transfers between devices, to_x(): lax.ppermute(array, 'x', [(i, (i + step) % size_x) for i in range(size_x)])  50 us
    dot_general x8, matrix products, mm_nt(): lax.dot_general(left, right, (((1,), (1,)), ((), ())), preferred_element_...  45.6 us
    ppermute x1, waiting for transfers between devices, sum_rows(): return lax.ppermute(summed, ALL, keep_pairs).astype(F32)  31.5 us
    ppermute x8, starting transfers between devices, shift_ctx(): return lax.ppermute(array, CTX, pairs)  24.1 us
    pallas_call x1, Pallas kernels, attend_back(): pl.pallas_call(attend_back_kernel, grid=(blocks, groups), in_specs=[pl.Bl...  16.9 us
  transfers between devices with their start and end apart: 22, of which 5 were waited for; matrix products, arithmetic and copies ran while one was open for 18% of the time, Pallas kernels for 38%

profile of v4, /device:TPU:20, one launch (start us, length us, event | category | flops | bytes accessed | tf_op | source)
XLA Modules:
  0.0 678.6 jit_solution(2101744411744289882)
XLA Ops:
  11.8 109.4 %fetch.1 = (bf16[256,2048]{1,0:T(8,128)(2,1)S(1)}, bf16[256,2048]{1,0:T(8,128)(2,1)}, bf16[2048,2048]{1,0:T(8,128)(2,1)}, bf16[2048,256]{1,0:T(8,128)(2,1)S(1)},...) custom-call(bf16[256,2048]{1,0:T(8,128)(2,1)S(1)} %convolution_conve, ...), custom_call_target="tpu_custom_call" | custom-call | bytes 314572800 | tf_op jit(solution)/shard_map/fetch/pallas_call | solution.py:398
  133.1 6.7 convolution_convert_fusion.5.q_ref
  147.7 10.3 %attend.1 = (bf16[256,2048]{1,0:T(8,128)(2,1)S(1)}, f32[8,1,512]{2,1,0:T(1,128)S(1)}) custom-call(s32[1,256]{1,0:T(1,128)S(1)} %maximum_subtract_fusion.lo_ref, bf16[256,2048]{1,0:T(8,128)(2,1)S(1)} %copy-done.7, bf16[1280,256]{1,0:T(8,128)(2,1)S(1)} %constant_dynamic-update-slice_fusion.kv_ref), custom_call_target="tpu_custom_call" | custom-call | flops 2415919104 | bytes 4194304 | tf_op jit(solution)/shard_map/attend/pallas_call | solution.py:99
  158.0 7.1 %multiply_reduce_fusion.2 = (f32[256]{0:T(256)S(1)}, f32[256,2048]{1,0:T(8,128)}) fusion(bf16[256,2048]{1,0:T(8,128)(2,1)S(1)} %get-tuple-element.34, bf16[2048,2048]{1,0:T(8,128)(2,1)} %get-tuple-element.35, bf16[256,2048]{1,0:T(8,128)(2,1)S(1)} %get-tuple-element.30), kind=kOutput, calls=%fused_computation.63 | convolution fusion | flops 2149580544 | bytes 12583936 | tf_op jit(solution)/shard_map/dot_general | solution.py:30
  172.9 18.1 %collective-permute-done.5 = bf16[256,2048]{1,0:T(8,128)(2,1)} collective-permute-done((bf16[256,2048]{1,0:T(8,128)(2,1)}, bf16[256,2048]{1,0:T(8,128)(2,1)}, u32[]{:S(2)}, u32[]{:S(2)}) %collective-permute-start.5) | collective-permute-done | bytes 1048608 | tf_op jit(solution)/shard_map/ppermute | solution.py:782
  192.5 12.2 %fusion.11 = f32[1024,1536]{1,0:T(8,128)} fusion(bf16[1024,2048]{1,0:T(8,128)(2,1)S(1)} %constant_dynamic-update-slice_fusion.5, bf16[3072,2048]{1,0:T(8,128)(2,1)} %param.22, s32[]{:T(128)S(6)} %select_n.16), kind=kOutput, calls=%fused_computation.17 | convolution fusion | flops 6442450944 | bytes 16777220 | tf_op jit(solution)/shard_map/dot_general | solution.py:38
  204.7 12.3 %fusion.53 = f32[1024,1536]{1,0:T(8,128)} fusion(bf16[2048,1536]{1,0:T(8,128)(2,1)S(1)} %bitcast.79, bf16[256,2048]{1,0:T(8,128)(2,1)S(1)} %collective-permute-done.6, bf16[256,2048]{1,0:T(8,128)(2,1)} %collective-permute-done.5, bf16[256,2048]{1,0:T(8,128)(2,1)S(1)} %collective-permute-done.4, bf16[256,2048]{1,0:T(8,128)(2,1)} %multiply_convert_fusion.2), kind=kOutput, calls=%fused_computation.109 | convolution fusion | flops 6459228160 | bytes 16777216 | tf_op jit(solution)/shard_map/dot_general | solution.py:30
  217.0 20.4 %multiply_convert_fusion = (bf16[1024,1536]{1,0:T(8,128)(2,1)}, bf16[1024,1536]{1,0:T(8,128)(2,1)}, bf16[1024,1536]{1,0:T(8,128)(2,1)}) fusion(f32[1024,1536]{1,0:T(8,128)} %fusion.53, f32[1024,1536]{1,0:T(8,128)} %fusion.11, bf16[2048,1536]{1,0:T(8,128)(2,1)} %get-tuple-element.37, bf16[256,2048]{1,0:T(8,128)(2,1)S(1)} %collective-permute-done.6, ...), kind=kOutput, calls=%fused_computation.10 | convolution fusion | flops 6500122624 | bytes 32505856 | tf_op jit(solution)/shard_map/dot_general | solution.py:30
  237.4 11.3 %convolution_convert_fusion = bf16[1536,2048]{1,0:T(8,128)(2,1)} fusion(bf16[1024,1536]{1,0:T(8,128)(2,1)} %get-tuple-element.56, bf16[1024,2048]{1,0:T(8,128)(2,1)} %copy-done.23), kind=kOutput, calls=%fused_computation.2 | convolution fusion | flops 6445596672 | bytes 13631488 | tf_op jit(solution)/shard_map/dot_general | solution.py:34
  248.7 6.2 fusion.38
  254.9 5.7 convolution_add_fusion.1
  260.7 5.8 fusion.9
  267.3 4.9 fusion.35
  272.4 6.1 convolution_add_fusion
  282.7 5.5 fusion.7
  293.0 14.7 %collective-permute-done.11 = bf16[256,2048]{1,0:T(8,128)(2,1)} collective-permute-done((bf16[256,2048]{1,0:T(8,128)(2,1)}, bf16[256,2048]{1,0:T(8,128)(2,1)}, u32[]{:S(2)}, u32[]{:S(2)}) %collective-permute-start.11) | collective-permute-done | bytes 1048608 | tf_op jit(solution)/shard_map/ppermute | solution.py:782
  307.7 4.3 multiply_reduce_fusion
  312.1 17.2 %collective-permute-done.18 = bf16[256,2048]{1,0:T(8,128)(2,1)} collective-permute-done((bf16[256,2048]{1,0:T(8,128)(2,1)}, bf16[256,2048]{1,0:T(8,128)(2,1)}, u32[]{:S(2)}, u32[]{:S(2)}) %collective-permute-start.18) | collective-permute-done | bytes 1048608 | tf_op jit(solution)/shard_map/ppermute | solution.py:782
  329.3 7.1 %fusion.55 = (bf16[256,2048]{1,0:T(8,128)(2,1)S(1)}, f32[256,2048]{1,0:T(8,128)}, bf16[256,2048]{1,0:T(8,128)(2,1)}) fusion(f32[256]{0:T(256)S(1)} %broadcast_multiply_fusion.1, f32[256,2048]{1,0:T(8,128)} %get-tuple-element.71, f32[2048]{0:T(1024)S(1)} %bitcast.64, bf16[256,2048]{1,0:T(8,128)(2,1)} %collective-permute-done.12, ...), kind=kLoop, calls=%fused_computation.111 | loop fusion | flops 9437184 | bytes 15738880 | tf_op jit(solution)/shard_map/convert_element_type | solution.py:872
  338.9 16.9 %attend_back.1 = (bf16[256,2048]{1,0:T(8,128)(2,1)S(1)}, f32[1280,256]{1,0:T(8,128)S(1)}) custom-call(s32[1,256]{1,0:T(1,128)S(1)} %maximum_subtract_fusion.lo_ref, bf16[256,2048]{1,0:T(8,128)(2,1)S(1)} %copy-done.8, bf16[1280,256]{1,0:T(8,128)(2,1)S(1)} %constant_dynamic-update-slice_fusion.kv_ref, bf16[256,2048]{1,0:T(8,128)(2,1)S(1)} %convolution_convert_fusion.4.do_ref, ...), custom_call_target="tpu_custom_call" | custom-call | flops 6039797760 | bytes 6291456 | tf_op jit(solution)/shard_map/attend_back/pallas_call | solution.py:127
  356.8 5.0 collective-permute-start.13
  377.7 7.6 %fusion.24 = (f32[2048]{0:T(1024)S(1)}, f32[256]{0:T(256)S(1)}, f32[256,2048]{1,0:T(8,128)}) fusion(bf16[256,2048]{1,0:T(8,128)(2,1)S(1)} %get-tuple-element.30, f32[256]{0:T(256)S(1)} %copy-done.32, f32[2048]{0:T(1024)S(1)} %bitcast.68, f32[256,2048]{1,0:T(8,128)S(1)} %fusion.59, bf16[256,2048]{1,0:T(8,128)(2,1)S(1)} %copy-done.6, ...), kind=kOutput, calls=%fused_computation.43 | convolution fusion | flops 2151675648 | bytes 14698496 | tf_op jit(solution)/shard_map/dot_general | solution.py:38
  392.1 233.0 %sum_grads.1 = (bf16[4,64,1536]{2,1,0:T(8,128)(2,1)}, bf16[4,64,1536]{2,1,0:T(8,128)(2,1)}, bf16[4,64,512]{2,1,0:T(8,128)(2,1)}, bf16[64,2048]{1,0:T(8,128)(2,1)...) custom-call(bf16[1024,2048]{1,0:T(8,128)(2,1)} %pad_maximum_fusion.refs_0_, ...), custom_call_target="tpu_custom_call" | custom-call | flops 17448304640 | bytes 419430400 | tf_op jit(solution)/shard_map/sum_grads/pallas_call | solution.py:696
  638.5 31.5 %collective-permute-done.20 = bf16[192,2048]{1,0:T(8,128)(2,1)S(1)} collective-permute-done((bf16[192,2048]{1,0:T(8,128)(2,1)}, bf16[192,2048]{1,0:T(8,128)(2,1)S(1)}, u32[]{:S(2)}, u32[]{:S(2)}) %collective-permute-start.20) | collective-permute-done | bytes 786464 | tf_op jit(solution)/shard_map/ppermute | solution.py:817
  (197 shorter events, 83.7 us)
Async XLA Ops:
  7.2 622.3 %reduce-scatter.2.cloned.1.call-start = ((), (), s32[]{:S(2)}) async-start(), calls=%async_computation.1 | async-start | bytes 7077888 | tf_op jit(solution)/shard_map/reduce_scatter | solution.py:809
  122.1 48.2 %collective-permute-start.7 = (bf16[256,2048]{1,0:T(8,128)(2,1)}, bf16[256,2048]{1,0:T(8,128)(2,1)}, u32[]{:S(2)}, u32[]{:S(2)}) collective-permute-start(bf16[256,2048]{1,0:T(8,128)(2,1)} %get-tuple-element.36), channel_id=1, source_target_pairs={{0,2},{2,0},{1,3},{3,1},{4,6},{6,4},{5,7},{7,5},{8,10},{10,8},{9,1... | collective-permute-start | bytes 3145736 | tf_op jit(solution)/shard_map/ppermute | solution.py:779
  122.5 45.9 %collective-permute-start.8 = (bf16[256,2048]{1,0:T(8,128)(2,1)}, bf16[256,2048]{1,0:T(8,128)(2,1)}, u32[]{:S(2)}, u32[]{:S(2)}) collective-permute-start(bf16[256,2048]{1,0:T(8,128)(2,1)} %get-tuple-element.36), channel_id=1, source_target_pairs={{0,1},{1,0},{2,3},{3,2},{4,5},{5,4},{6,7},{7,6},{8,9},{9,8},{10,11... | collective-permute-start | bytes 3145736 | tf_op jit(solution)/shard_map/ppermute | solution.py:782
  125.2 14.9 %collective-permute-start = (bf16[256,256]{1,0:T(8,128)(2,1)S(1)}, bf16[256,256]{1,0:T(8,128)(2,1)S(1)}, u32[]{:S(2)}, u32[]{:S(2)}) collective-permute-start(bf16[256,256]{1,0:T(8,128)(2,1)S(1)} %convolution_convert_fusion.6), channel_id=1, source_target_pairs={{0,8},{2,10},{4,12},{6,14},{8,16},{10,18},{12,20},{14,22},{16,24},... | collective-permute-start | bytes 393224 | tf_op jit(solution)/shard_map/ppermute | solution.py:786
  128.9 13.4 %collective-permute-start.1 = (bf16[256,256]{1,0:T(8,128)(2,1)S(1)}, bf16[256,256]{1,0:T(8,128)(2,1)S(1)}, u32[]{:S(2)}, u32[]{:S(2)}) collective-permute-start(bf16[256,256]{1,0:T(8,128)(2,1)S(1)} %convolution_convert_fusion.6), channel_id=1, source_target_pairs={{0,6},{2,8},{4,10},{6,12},{8,14},{10,16},{12,18},{14,20},{16,22},{... | collective-permute-start | bytes 393224 | tf_op jit(solution)/shard_map/ppermute | solution.py:786
  130.9 11.5 %collective-permute-start.2 = (bf16[256,256]{1,0:T(8,128)(2,1)S(1)}, bf16[256,256]{1,0:T(8,128)(2,1)S(1)}, u32[]{:S(2)}, u32[]{:S(2)}) collective-permute-start(bf16[256,256]{1,0:T(8,128)(2,1)S(1)} %convolution_convert_fusion.6), channel_id=1, source_target_pairs={{0,4},{2,6},{4,8},{6,10},{8,12},{10,14},{12,16},{14,18},{16,20},{1... | collective-permute-start | bytes 393224 | tf_op jit(solution)/shard_map/ppermute | solution.py:786
  140.1 6.3 collective-permute-start.3
  167.9 23.1 %collective-permute-start.5 = (bf16[256,2048]{1,0:T(8,128)(2,1)}, bf16[256,2048]{1,0:T(8,128)(2,1)}, u32[]{:S(2)}, u32[]{:S(2)}) collective-permute-start(bf16[256,2048]{1,0:T(8,128)(2,1)} %multiply_convert_fusion.2), channel_id=1, source_target_pairs={{0,1},{1,0},{2,3},{3,2},{4,5},{5,4},{6,7},{7,6},{8,9},{9,8},{10,11... | collective-permute-start | bytes 3145736 | tf_op jit(solution)/shard_map/ppermute | solution.py:782
  168.5 22.5 %collective-permute-start.9 = (bf16[256,2048]{1,0:T(8,128)(2,1)}, bf16[256,2048]{1,0:T(8,128)(2,1)}, u32[]{:S(2)}, u32[]{:S(2)}) collective-permute-start(bf16[256,2048]{1,0:T(8,128)(2,1)} %collective-permute-done.8), channel_id=1, source_target_pairs={{0,2},{2,0},{1,3},{3,1},{4,6},{6,4},{5,7},{7,5},{8,10},{10,8},{9,1... | collective-permute-start | bytes 3145736 | tf_op jit(solution)/shard_map/ppermute | solution.py:779
  169.8 34.9 %collective-permute-start.4 = (bf16[256,2048]{1,0:T(8,128)(2,1)}, bf16[256,2048]{1,0:T(8,128)(2,1)S(1)}, u32[]{:S(2)}, u32[]{:S(2)}) collective-permute-start(bf16[256,2048]{1,0:T(8,128)(2,1)} %multiply_convert_fusion.2), channel_id=1, source_target_pairs={{0,2},{2,0},{1,3},{3,1},{4,6},{6,4},{5,7},{7,5},{8,10},{10,8},{9,1... | collective-permute-start | bytes 3145736 | tf_op jit(solution)/shard_map/ppermute | solution.py:779
  191.0 13.7 %collective-permute-start.6 = (bf16[256,2048]{1,0:T(8,128)(2,1)}, bf16[256,2048]{1,0:T(8,128)(2,1)S(1)}, u32[]{:S(2)}, u32[]{:S(2)}) collective-permute-start(bf16[256,2048]{1,0:T(8,128)(2,1)} %collective-permute-done.5), channel_id=1, source_target_pairs={{0,2},{2,0},{1,3},{3,1},{4,6},{6,4},{5,7},{7,5},{8,10},{10,8},{9,1... | collective-permute-start | bytes 3145736 | tf_op jit(solution)/shard_map/ppermute | solution.py:779
  266.7 13.4 %collective-permute-start.10 = (bf16[256,2048]{1,0:T(8,128)(2,1)S(1)}, bf16[256,2048]{1,0:T(8,128)(2,1)S(1)}, u32[]{:S(2)}, u32[]{:S(2)}) collective-permute-start(bf16[256,2048]{1,0:T(8,128)(2,1)S(1)} %slice.162), channel_id=1, source_target_pairs={{0,2},{2,0},{1,3},{3,1},{4,6},{6,4},{5,7},{7,5},{8,10},{10,8},{9,1... | collective-permute-start | bytes 3145736 | tf_op jit(solution)/shard_map/ppermute | solution.py:779
  272.3 17.8 %collective-permute-start.17 = (bf16[256,2048]{1,0:T(8,128)(2,1)S(1)}, bf16[256,2048]{1,0:T(8,128)(2,1)S(1)}, u32[]{:S(2)}, u32[]{:S(2)}) collective-permute-start(bf16[256,2048]{1,0:T(8,128)(2,1)S(1)} %slice.160), channel_id=1, source_target_pairs={{0,2},{2,0},{1,3},{3,1},{4,6},{6,4},{5,7},{7,5},{8,10},{10,8},{9,1... | collective-permute-start | bytes 3145736 | tf_op jit(solution)/shard_map/ppermute | solution.py:779
  279.6 13.3 %collective-permute-start.12 = (bf16[256,2048]{1,0:T(8,128)(2,1)}, bf16[256,2048]{1,0:T(8,128)(2,1)}, u32[]{:S(2)}, u32[]{:S(2)}) collective-permute-start(bf16[256,2048]{1,0:T(8,128)(2,1)} %slice.161), channel_id=1, source_target_pairs={{0,2},{2,0},{1,3},{3,1},{4,6},{6,4},{5,7},{7,5},{8,10},{10,8},{9,1... | collective-permute-start | bytes 3145736 | tf_op jit(solution)/shard_map/ppermute | solution.py:779
  281.4 26.3 %collective-permute-start.11 = (bf16[256,2048]{1,0:T(8,128)(2,1)}, bf16[256,2048]{1,0:T(8,128)(2,1)}, u32[]{:S(2)}, u32[]{:S(2)}) collective-permute-start(bf16[256,2048]{1,0:T(8,128)(2,1)} %fusion.31), channel_id=1, source_target_pairs={{0,1},{1,0},{2,3},{3,2},{4,5},{5,4},{6,7},{7,6},{8,9},{9,8},{10,11... | collective-permute-start | bytes 3145736 | tf_op jit(solution)/shard_map/ppermute | solution.py:782
  289.5 22.6 %collective-permute-start.19 = (bf16[256,2048]{1,0:T(8,128)(2,1)}, bf16[256,2048]{1,0:T(8,128)(2,1)}, u32[]{:S(2)}, u32[]{:S(2)}) collective-permute-start(bf16[256,2048]{1,0:T(8,128)(2,1)} %slice.159), channel_id=1, source_target_pairs={{0,2},{2,0},{1,3},{3,1},{4,6},{6,4},{5,7},{7,5},{8,10},{10,8},{9,1... | collective-permute-start | bytes 3145736 | tf_op jit(solution)/shard_map/ppermute | solution.py:779
  291.3 38.0 %collective-permute-start.18 = (bf16[256,2048]{1,0:T(8,128)(2,1)}, bf16[256,2048]{1,0:T(8,128)(2,1)}, u32[]{:S(2)}, u32[]{:S(2)}) collective-permute-start(bf16[256,2048]{1,0:T(8,128)(2,1)} %fusion.29), channel_id=1, source_target_pairs={{0,1},{1,0},{2,3},{3,2},{4,5},{5,4},{6,7},{7,6},{8,9},{9,8},{10,11... | collective-permute-start | bytes 3145736 | tf_op jit(solution)/shard_map/ppermute | solution.py:782
  293.0 36.3 %copy-start.11 = (f32[512,2048]{1,0:T(8,128)S(1)}, f32[512,2048]{1,0:T(8,128)}, u32[]{:S(2)}) copy-start(f32[512,2048]{1,0:T(8,128)} %copy-done.10) | copy-start | bytes 12582916
  356.8 18.4 %collective-permute-start.13 = (bf16[256,256]{1,0:T(8,128)(2,1)}, bf16[256,256]{1,0:T(8,128)(2,1)S(1)}, u32[]{:S(2)}, u32[]{:S(2)}) collective-permute-start(bf16[256,256]{1,0:T(8,128)(2,1)} %get-tuple-element.62), channel_id=1, source_target_pairs={{8,0},{10,2},{12,4},{14,6},{16,8},{18,10},{20,12},{22,14},{24,16},... | collective-permute-start | bytes 393224 | tf_op jit(solution)/shard_map/ppermute | solution.py:786
  361.9 13.4 %collective-permute-start.14 = (bf16[256,256]{1,0:T(8,128)(2,1)}, bf16[256,256]{1,0:T(8,128)(2,1)}, u32[]{:S(2)}, u32[]{:S(2)}) collective-permute-start(bf16[256,256]{1,0:T(8,128)(2,1)} %get-tuple-element.65), channel_id=1, source_target_pairs={{6,0},{8,2},{10,4},{12,6},{14,8},{16,10},{18,12},{20,14},{22,16},{... | collective-permute-start | bytes 393224 | tf_op jit(solution)/shard_map/ppermute | solution.py:786
  364.3 11.0 %collective-permute-start.15 = (bf16[256,256]{1,0:T(8,128)(2,1)}, bf16[256,256]{1,0:T(8,128)(2,1)}, u32[]{:S(2)}, u32[]{:S(2)}) collective-permute-start(bf16[256,256]{1,0:T(8,128)(2,1)} %get-tuple-element.64), channel_id=1, source_target_pairs={{4,0},{6,2},{8,4},{10,6},{12,8},{14,10},{16,12},{18,14},{20,16},{2... | collective-permute-start | bytes 393224 | tf_op jit(solution)/shard_map/ppermute | solution.py:786
  367.1 8.8 %collective-permute-start.16 = (bf16[256,256]{1,0:T(8,128)(2,1)}, bf16[256,256]{1,0:T(8,128)(2,1)}, u32[]{:S(2)}, u32[]{:S(2)}) collective-permute-start(bf16[256,256]{1,0:T(8,128)(2,1)} %get-tuple-element.63), channel_id=1, source_target_pairs={{2,0},{4,2},{6,4},{8,6},{10,8},{12,10},{14,12},{16,14},{18,16},{20... | collective-permute-start | bytes 393224 | tf_op jit(solution)/shard_map/ppermute | solution.py:786
  629.5 40.6 %collective-permute-start.20 = (bf16[192,2048]{1,0:T(8,128)(2,1)}, bf16[192,2048]{1,0:T(8,128)(2,1)S(1)}, u32[]{:S(2)}, u32[]{:S(2)}) collective-permute-start(bf16[192,2048]{1,0:T(8,128)(2,1)} %reduce-scatter.2.cloned.1.call-done), channel_id=1, source_target_pairs={{0,0},{1,16},{2,8},{3,24},{4,1},{5,17},{6,9},{7,25},{8,2},{9,18},{... | collective-permute-start | bytes 2359304 | tf_op jit(solution)/shard_map/ppermute | solution.py:817
  632.3 39.1 %copy-start.1 = (bf16[1,256,2048]{2,1,0:T(8,128)(2,1)S(1)}, bf16[1,256,2048]{2,1,0:T(8,128)(2,1)}, u32[]{:S(2)}) copy-start(bf16[1,256,2048]{2,1,0:T(8,128)(2,1)} %param.23) | copy-start | bytes 3145732
  (44 other events, 391.8 us)
Sparse Core Ops, SparseCore 0:
  248.8 122.3 reduce-scatter.1

commit v5 on v4

--- a/solution.py
+++ b/solution.py
@@ -2,6 +2,7 @@
 
 import jax
 import jax.numpy as jnp
+import numpy as np
 from jax import lax
 from jax.experimental import pallas as pl
 from jax.experimental.pallas import tpu as pltpu
@@ -19,6 +20,8 @@
 epsilon = 1e-06
 neg_large = -1e30
 scale = HD ** (-0.5)
+root = (2.0 / np.pi) ** 0.5
+cubic = 0.044715
 BF = jnp.bfloat16
 F32 = jnp.float32
 CTX = ("a", "b", "c")
@@ -426,6 +429,261 @@
     )(*ins)
 
 
+def mlp_kernel(sizes, own_ref, *refs):
+    size_a, size_b, size_x = sizes
+    ranks = 2 * size_x
+    cots_in, refs = refs[:ranks], refs[ranks:]
+    weights_in, refs = refs[:3], refs[3:]
+    grad_ref, rows_out, dg_out, du_out, part_out, down_out, refs = *refs[:6], refs[6:]
+    rows, cot, w_gate, w_up, w_down, hid, dg, du = refs[:8]
+    to_core, in_core, to_x, in_x, total, part_stage, down_stage = refs[8:15]
+    load_sem, ag_send, ag_recv, core_send, core_recv, x_send, x_recv, out_sem, stage_sem = refs[15:]
+    ia, ib, ic, ix = (lax.axis_index(name) for name in ALL)
+    hidden_units = w_down.shape[0]
+    tok, width = own_ref.shape
+    tiles, _, tile = total.shape
+    unit = hid.shape[2] // (hid.shape[2] // 512 if hid.shape[2] % 512 == 0 else hid.shape[2] // 256)
+
+    loads = [
+        pltpu.make_async_copy(own_ref, rows.at[0], load_sem.at[0]),
+        pltpu.make_async_copy(weights_in[0], w_gate, load_sem.at[1]),
+        pltpu.make_async_copy(weights_in[1], w_up, load_sem.at[2]),
+        pltpu.make_async_copy(
+            weights_in[2].at[pl.ds(pl.multiple_of(ic * hidden_units, hidden_units), hidden_units), :],
+            w_down,
+            load_sem.at[3],
+        ),
+    ]
+    for b in range(ranks):
+        loads.append(pltpu.make_async_copy(cots_in[b], cot.at[b], load_sem.at[4 + b]))
+    for copy in loads:
+        copy.start()
+
+    partner = (ia, ib, 1 - ic, ix)
+
+    def across(step):
+        return ia, ib, ic, (ix + size_x + step) % size_x
+
+    barrier = pltpu.get_barrier_semaphore()
+    greeted = [partner] + [across(s) for s in range(1, size_x)]
+    for device in greeted:
+        pl.semaphore_signal(barrier, inc=1, device_id=device, device_id_type=MESH)
+    pl.semaphore_wait(barrier, len(greeted))
+
+    def remote(src, dst, sent, came, device):
+        return pltpu.make_async_remote_copy(
+            src_ref=src,
+            dst_ref=dst,
+            send_sem=sent,
+            recv_sem=came,
+            device_id=device,
+            device_id_type=MESH,
+        )
+
+    def gather(b):
+        if b == 1:
+            return remote(own_ref, rows.at[1], ag_send.at[1], ag_recv.at[1], partner)
+        if b % 2:
+            return remote(rows.at[b - 1], rows.at[b], ag_send.at[b], ag_recv.at[b], partner)
+        return remote(own_ref, rows.at[b], ag_send.at[b], ag_recv.at[b], across(b // 2))
+
+    def core_copy(s):
+        return remote(to_core.at[s], in_core.at[s], core_send.at[s], core_recv.at[s], partner)
+
+    def x_copy(s, t):
+        return remote(
+            to_x.at[s, t], in_x.at[s, t], x_send.at[s, t], x_recv.at[s, t], across(-s)
+        )
+
+    def results(b):
+        to = pl.ds(b * tok, tok)
+        return [
+            pltpu.make_async_copy(rows.at[b], rows_out.at[to, :], out_sem.at[0, b]),
+            pltpu.make_async_copy(dg.at[b], dg_out.at[to, :], out_sem.at[1, b]),
+            pltpu.make_async_copy(du.at[b], du_out.at[to, :], out_sem.at[2, b]),
+        ]
+
+    def forward(b):
+        def step(t, carry):
+            units = pl.ds(pl.multiple_of(t * unit, unit), unit)
+            gate = mm(rows[b], w_gate[:, units])
+            upward = mm(rows[b], w_up[:, units])
+            d_hidden = mm_nt(cot[b], w_down[units, :])
+            square = gate * gate
+            bent = jnp.tanh(root * gate * (1.0 + cubic * square))
+            half = 0.5 * (1.0 + bent)
+            act = gate * half
+            slope = half + 0.5 * gate * (1.0 - bent * bent) * root * (1.0 + 3.0 * cubic * square)
+            hid[b, :, units] = (act * upward).astype(BF)
+            dg[b, :, units] = (d_hidden * upward * slope).astype(BF)
+            du[b, :, units] = (d_hidden * act).astype(BF)
+            return carry
+
+        lax.fori_loop(0, hid.shape[2] // unit, step, 0)
+        for copy in results(b):
+            copy.start()
+
+    def backward(b):
+        s, other = b // 2, b % 2
+        if not other:
+            core_copy(s).wait_recv()
+
+        def step(t, carry):
+            at = pl.ds(pl.multiple_of(t * tile, tile), tile)
+            value = mm_nt(dg[b], w_gate[at, :]) + mm_nt(du[b], w_up[at, :])
+            if other:
+                to_core[s, t] = value.astype(BF)
+                return carry
+            value = value + in_core[s, t].astype(F32)
+            if s:
+                to_x[s, t] = value.astype(BF)
+                x_copy(s, t).start()
+            else:
+                total[t] = value
+            return carry
+
+        lax.fori_loop(0, tiles, step, 0)
+        if other:
+            core_copy(s).start()
+
+    def part_copy(b):
+        return pltpu.make_async_copy(part_stage.at[b % 2], part_out.at[b], stage_sem.at[b % 2])
+
+    def branch(b):
+        if b >= 2:
+            part_copy(b - 2).wait()
+
+        def step(t, carry):
+            at = pl.ds(pl.multiple_of(t * tile, tile), tile)
+            part_stage[b % 2, :, at] = mm(hid[b], w_down[:, at]).astype(BF)
+            return carry
+
+        lax.fori_loop(0, tiles, step, 0)
+        part_copy(b).start()
+
+    depth = down_stage.shape[1]
+    strips = hidden_units // depth
+
+    def down_copy(t, slot):
+        to = pl.ds(pl.multiple_of(t * depth, depth), depth)
+        return pltpu.make_async_copy(down_stage.at[slot], down_out.at[to, :], stage_sem.at[2 + slot])
+
+    def down_step(t, carry):
+        slot = t % 2
+
+        @pl.when(t >= 2)
+        def _():
+            down_copy(t - 2, slot).wait()
+
+        units = pl.ds(pl.multiple_of(t * depth, depth), depth)
+        value = mm_tn(hid[0, :, units], cot[0])
+        for b in range(1, ranks):
+            value = value + mm_tn(hid[b, :, units], cot[b])
+        down_stage[slot] = value.astype(BF)
+        down_copy(t, slot).start()
+        return carry
+
+    gather(1).start()
+    for s in range(1, size_x):
+        gather(2 * s).start()
+    for copy in loads:
+        copy.wait()
+    forward(0)
+    gather(1).wait_recv()
+    forward(1)
+    backward(1)
+    for s in range(1, size_x):
+        gather(2 * s).wait_recv()
+        gather(2 * s + 1).start()
+        forward(2 * s)
+        gather(2 * s + 1).wait_recv()
+        forward(2 * s + 1)
+        backward(2 * s + 1)
+        backward(2 * s)
+    backward(0)
+    lax.fori_loop(0, strips, down_step, 0)
+    for b in range(ranks):
+        branch(b)
+    for s in range(1, size_x):
+        for t in range(tiles):
+            x_copy(s, t).wait()
+    for t in range(tiles):
+        value = total[t]
+        for s in range(1, size_x):
+            value = value + in_x[s, t].astype(F32)
+        grad_ref[:, t * tile : (t + 1) * tile] = value
+    for b in range(1, ranks):
+        gather(b).wait_send()
+    for s in range(size_x):
+        core_copy(s).wait_send()
+    for b in range(ranks):
+        for copy in results(b):
+            copy.wait()
+    part_copy(ranks - 2).wait()
+    part_copy(ranks - 1).wait()
+    down_copy(strips - 2, (strips - 2) % 2).wait()
+    down_copy(strips - 1, (strips - 1) % 2).wait()
+
+
+def feed_forward(sizes, normed, cots, w_gate, w_up, down_weight):
+    ranks = 2 * sizes[2]
+    size_x = sizes[2]
+    tok, width = normed.shape
+    units = w_gate.shape[1]
+    tile = 512
+    tiles = width // tile
+    sem = pltpu.SemaphoreType.DMA
+    hbm = pl.BlockSpec(memory_space=pl.ANY)
+    return pl.pallas_call(
+        functools.partial(mlp_kernel, sizes),
+        in_specs=[hbm] * (4 + ranks),
+        out_specs=[pl.BlockSpec(memory_space=pltpu.VMEM)] + [hbm] * 5,
+        out_shape=[
+            jax.ShapeDtypeStruct((tok, width), F32),
+            jax.ShapeDtypeStruct((ranks * tok, width), BF),
+            jax.ShapeDtypeStruct((ranks * tok, units), BF),
+            jax.ShapeDtypeStruct((ranks * tok, units), BF),
+            jax.ShapeDtypeStruct((ranks, tok, width), BF),
+            jax.ShapeDtypeStruct((units, width), BF),
+        ],
+        scratch_shapes=[
+            pltpu.VMEM((ranks, tok, width), BF),
+            pltpu.VMEM((ranks, tok, width), BF),
+            pltpu.VMEM((width, units), BF),
+            pltpu.VMEM((width, units), BF),
+            pltpu.VMEM((units, width), BF),
+            pltpu.VMEM((ranks, tok, units), BF),
+            pltpu.VMEM((ranks, tok, units), BF),
+            pltpu.VMEM((ranks, tok, units), BF),
+            pltpu.VMEM((size_x, tiles, tok, tile), BF),
+            pltpu.VMEM((size_x, tiles, tok, tile), BF),
+            pltpu.VMEM((size_x, tiles, tok, tile), BF),
+            pltpu.VMEM((size_x, tiles, tok, tile), BF),
+            pltpu.VMEM((tiles, tok, tile), F32),
+            pltpu.VMEM((2, tok, width), BF),
+            pltpu.VMEM((2, 256, width), BF),
+            sem((4 + ranks,)),
+            sem((ranks,)),
+            sem((ranks,)),
+            sem((size_x,)),
+            sem((size_x,)),
+            sem((size_x, tiles)),
+            sem((size_x, tiles)),
+            sem((3, ranks)),
+            sem((4,)),
+        ],
+        compiler_params=pltpu.CompilerParams(
+            collective_id=2, has_side_effects=True, vmem_limit_bytes=62 * 1024 * 1024
+        ),
+        cost_estimate=pl.CostEstimate(
+            flops=14 * ranks * tok * width * units,
+            bytes_accessed=60 * 1024 * 1024,
+            transcendentals=0,
+        ),
+        name="feed_forward",
+    )(normed, *cots, w_gate, w_up, down_weight)
+
+
 class Job:
     def __init__(self, phase, left, right, rows, cols, by_rank):
         self.phase, self.left, self.right = phase, left, right
@@ -438,12 +696,12 @@
     n_ctx = 2 * chips
     ranks = 2 * size_x
     count = len(jobs)
-    ins, refs = refs[:11], refs[11:]
+    ins, refs = refs[:12], refs[12:]
     outs, refs = refs[:count], refs[count:]
     dealt, refs = refs[:2], refs[2:]
     gain_out, refs = refs[0], refs[1:]
     held, refs = refs[:8], refs[8:]
-    gain_ctx, gain_x, refs = refs[0], refs[1], refs[2:]
+    gain_ctx, gain_x, parts_in, resid_in, block_out, refs = *refs[:5], refs[5:]
     recv, refs = refs[:count], refs[count:]
     send, refs = refs[:count], refs[count:]
     done, refs = refs[:count], refs[count:]
@@ -515,12 +773,22 @@
 
     def deal_copy(t, k):
         e = (own + k) % n_ctx
-        rows = ins[8 + t].shape[0] // n_ctx
-        src = ins[8 + t].at[pl.ds(pl.multiple_of(e * rows, rows), rows), :]
+        source = block_out if t == 0 else ins[9]
+        rows = source.shape[0] // n_ctx
+        src = source.at[pl.ds(pl.multiple_of(e * rows, rows), rows), :]
         dst = dealt[t].at[pl.ds(pl.multiple_of(own * rows, rows), rows), :]
         if k == 0:
             return pltpu.make_async_copy(src, dst, load_sem.at[8 + t])
         return remote(src, dst, deal_send.at[t, k], deal_recv.at[t, k], ctx_device(k))
+
+    def part_copy(b):
+        src, dst = ins[8].at[b], parts_in.at[b]
+        if b == 0:
+            return pltpu.make_async_copy(src, dst, own_sem.at[count])
+        device = (ia, ib, (ic + b) % 2, (ix + size_x - b // 2) % size_x)
+        return remote(src, dst, group_send.at[0, b], group_recv.at[0, b], device)
+
+    resid_copy = pltpu.make_async_copy(ins[11], resid_in, load_sem.at[11])
 
     def gain_copy(k):
         src, dst = ins[10].at[(own + k) % n_ctx], gain_ctx.at[k]
@@ -595,9 +863,11 @@
             for i in range(3, 8):
                 for k in range(ranks):
                     group_copy(i, k).start()
-            for t in range(2):
-                for k in range(n_ctx):
-                    deal_copy(t, k).start()
+            for b in range(ranks):
+                part_copy(b).start()
+            resid_copy.start()
+            for k in range(n_ctx):
+                deal_copy(1, k).start()
 
         def step_of(step, carry):
             parity = step % 2
@@ -622,6 +892,15 @@
             gain_x[0] = jnp.sum(gain_ctx[...], axis=0)
             for s in range(1, size_x):
                 gain_copy_x(s).start()
+            resid_copy.wait()
+            for b in range(ranks):
+                part_copy(b).wait()
+            summed = resid_in[...]
+            for b in range(ranks):
+                summed = summed + parts_in[b].astype(F32)
+            block_out[...] = summed.astype(BF)
+            for k in range(n_ctx):
+                deal_copy(0, k).start()
         last = chips - 2
         for j in mine:
             cols = jobs[j].cols // 2
@@ -700,7 +979,13 @@
         + [pl.BlockSpec(memory_space=pltpu.VMEM)],
         out_shape=outs,
         scratch_shapes=held
-        + [pltpu.VMEM((2 * chips,) + gain_shape, F32), pltpu.VMEM((size_x,) + gain_shape, F32)]
+        + [
+            pltpu.VMEM((2 * chips,) + gain_shape, F32),
+            pltpu.VMEM((size_x,) + gain_shape, F32),
+            pltpu.VMEM((ranks, tok, width), BF),
+            pltpu.VMEM((tok, width), F32),
+            pltpu.VMEM((tok, width), BF),
+        ]
         + recv
         + send
         + done
@@ -716,7 +1001,7 @@
             sem((count, 2, chips - 1)),
             sem((count, ranks)),
             sem((count, ranks)),
-            sem((count,)),
+            sem((count + 1,)),
         ],
         compiler_params=pltpu.CompilerParams(
             collective_id=0, has_side_effects=True, vmem_limit_bytes=60 * 1024 * 1024
@@ -793,17 +1078,7 @@
         for step in range(1, size_x):
             got = to_x(array, step)
             parts += [got, to_core(got)]
-        return jnp.concatenate(parts, 0)
-
-    def group_sum(part_of):
-        total = None
-        for step in list(range(1, size_x)) + [0]:
-            both = part_of(step)
-            summed = both[:tok] + to_core(both[tok:].astype(BF)).astype(F32)
-            if step:
-                summed = to_x(summed.astype(BF), size_x - step).astype(F32)
-            total = summed if total is None else total + summed
-        return total
+        return parts
 
     def sum_rows(grad):
         summed = lax.psum_scatter(
@@ -830,8 +1105,8 @@
     gains = gains.reshape(size_x, 2, -1).astype(F32)
     gain_one = gains[:, 0].reshape(-1)
     gain_two = gains[:, 1].reshape(-1)
-    down_part = down_weight.shape[0] // 2
-    w_down = lax.dynamic_slice(down_weight, (ic * down_part, 0), (down_part, width))
+
+    cot_parts = group_rows(cot)
 
     inputs = inputs_low.astype(F32)
     unit_one, inv_one = norm_stats(inputs)
@@ -848,25 +1123,10 @@
     resid = inputs + mm(context, w_out)
 
     unit_two, inv_two = norm_stats(resid)
-    normed_mlp = group_rows((unit_two * gain_two).astype(BF))
-    cot_rows = group_rows(cot)
-    gate = mm(normed_mlp, w_gate)
-    upward = mm(normed_mlp, w_up)
-    d_hidden = mm_nt(cot_rows, w_down)
-    act, pull = jax.vjp(lambda v: jax.nn.gelu(v, approximate=True), gate)
-    hidden = (act * upward).astype(BF)
-    d_gate = pull(d_hidden * upward)[0].astype(BF)
-    d_upward = (d_hidden * act).astype(BF)
-
-    def rows_of(array, step):
-        return array[2 * step * tok : 2 * (step + 1) * tok]
-
-    d_normed_mlp = group_sum(
-        lambda step: mm_nt(rows_of(d_gate, step), w_gate) + mm_nt(rows_of(d_upward, step), w_up)
+    d_normed_mlp, mlp_rows, d_gate, d_upward, mlp_parts, down_grad = feed_forward(
+        sizes, (unit_two * gain_two).astype(BF), cot_parts, w_gate, w_up, down_weight
     )
-    down_grad = sum_rows(mm_tn(hidden, cot_rows))
-    branch_mlp = group_sum(lambda step: mm(rows_of(hidden, step), w_down))
-    block_output = (resid + branch_mlp).astype(BF)
+    down_grad = sum_rows(down_grad)
     d_resid_part, mlp_gain_grad = norm_back(unit_two, inv_two, gain_two, d_normed_mlp)
     d_resid = cot.astype(F32) + d_resid_part
     d_branch = d_resid.astype(BF)
@@ -887,7 +1147,7 @@
     sums = sum_grads(
         sizes,
         [
-            normed_mlp,
+            mlp_rows,
             d_gate,
             d_upward,
             normed.T,
@@ -895,9 +1155,10 @@
             d_branch,
             d_queries,
             d_pairs,
-            block_output,
+            mlp_parts,
             (d_resid + d_inputs).astype(BF),
             gain_grads.reshape(n_ctx, 8, 128),
+            resid,
         ],
     )
     gate_grad, up_grad, query_grad = (

time: 684 us -> 638 us (0.933)
  Pallas kernels: 370 us -> 476 us
  matrix products: 122 us -> 32.1 us
  waiting for transfers between devices: 85.7 us -> 40.6 us
  other arithmetic: 30.4 us -> 20.3 us
    pallas_call x0 -> x1, Pallas kernels: none -> 71.9 us  [feed_forward(): pl.pallas_call(functools.partial(mlp_kernel, sizes), in_specs=[hbm] * (4...]
    dot_general x9 -> x5, matrix products: 61.7 us -> 13.1 us  [mm(): return jnp.dot(left, right, preferred_element_type=F32)]
    ppermute x4 -> x1, waiting for transfers between devices: 50 us -> 3.58 us  [to_x(): lax.ppermute(array, 'x', [(i, (i + step) % size_x) for i in range(size_x)])]
    pallas_call x1, Pallas kernels: 233 us -> 267 us  [sum_grads(): pl.pallas_call(functools.partial(grads_kernel, sizes, jobs), in_specs=[pl...]
    dot_general x8 -> x3, matrix products: 45.6 us -> 15.6 us  [mm_nt(): lax.dot_general(left, right, (((1,), (1,)), ((), ())), preferred_element_...]
    dot_general x3 -> x2, matrix products: 14.7 us -> 3.4 us  [mm_tn(): lax.dot_general(left, right, (((0,), (0,)), ((), ())), preferred_element_...]
  transfers between devices with their start and end apart: 22 -> 13, of which waited for: 5 -> 4; matrix products, arithmetic and copies ran while one was open for 18% -> 10% of each run, Pallas kernels for 38% -> 47%
where the time goes in v5:
time: 638 us; the launch traced here: 631 us
  Pallas kernels  476 us (75%)
  waiting for transfers between devices  40.6 us (6%)
  matrix products  32.1 us (5%)
  starting transfers between devices  27.5 us (4%)
  other arithmetic  20.3 us (3%)
  local copies, waits for them, and re-layouts  19.6 us (3%)
  between operations  15 us (2%)
    pallas_call x1, Pallas kernels, sum_grads(): pl.pallas_call(functools.partial(grads_kernel, sizes, jobs), in_specs=[pl...  267 us
    pallas_call x1, Pallas kernels, fetch(): pl.pallas_call(functools.partial(fetch_kernel, sizes, pieces, len(ins), l...  110 us
    pallas_call x1, Pallas kernels, feed_forward(): pl.pallas_call(functools.partial(mlp_kernel, sizes), in_specs=[hbm] * (4...  71.9 us
    ppermute x1, waiting for transfers between devices, sum_rows(): return lax.ppermute(summed, ALL, keep_pairs).astype(F32)  29.5 us
    ppermute x8, starting transfers between devices, shift_ctx(): return lax.ppermute(array, CTX, pairs)  22.7 us
    pallas_call x1, Pallas kernels, attend_back(): pl.pallas_call(attend_back_kernel, grid=(blocks, groups), in_specs=[pl.Bl...  16.7 us
    dot_general x3, matrix products, mm_nt(): lax.dot_general(left, right, (((1,), (1,)), ((), ())), preferred_element_...  15.6 us
    dot_general x5, matrix products, mm(): return jnp.dot(left, right, preferred_element_type=F32)  13.1 us
  transfers between devices with their start and end apart: 13, of which 4 were waited for; matrix products, arithmetic and copies ran while one was open for 10% of the time, Pallas kernels for 47%

profile of v5, /device:TPU:20, one launch (start us, length us, event | category | flops | bytes accessed | tf_op | source)
XLA Modules:
  0.0 631.3 jit_solution(6255434306477742455)
XLA Ops:
  10.6 109.8 %fetch.1 = (bf16[256,2048]{1,0:T(8,128)(2,1)S(1)}, bf16[256,2048]{1,0:T(8,128)(2,1)S(1)}, bf16[2048,2048]{1,0:T(8,128)(2,1)}, bf16[2048,256]{1,0:T(8,128)(2,1)S(...) custom-call(bf16[256,2048]{1,0:T(8,128)(2,1)S(1)} %convolution_conve, ...), custom_call_target="tpu_custom_call" | custom-call | bytes 314572800 | tf_op jit(solution)/shard_map/fetch/pallas_call | solution.py:401
  121.3 2.3 collective-permute-start.3
  123.6 3.6 collective-permute-start.2
  132.8 5.8 convolution_convert_fusion.4.q_ref
  141.8 10.9 %attend.1 = (bf16[256,2048]{1,0:T(8,128)(2,1)S(1)}, f32[8,1,512]{2,1,0:T(1,128)S(1)}) custom-call(s32[1,256]{1,0:T(1,128)S(1)} %maximum_subtract_fusion.lo_ref, bf16[256,2048]{1,0:T(8,128)(2,1)S(1)} %convolution_convert_fusion.4.q_ref, bf16[1280,256]{1,0:T(8,128)(2,1)S(1)} %constant_dynamic-update-slice_fusion.kv_ref), custom_call_target="tpu_custom_call" | custom-call | flops 2415919104 | bytes 4194304 | tf_op jit(solution)/shard_map/attend/pallas_call | solution.py:102
  152.8 3.6 collective-permute-done.5.refs_2_
  156.4 5.9 multiply_reduce_fusion.2
  165.8 71.9 %feed_forward.1 = (f32[256,2048]{1,0:T(8,128)}, bf16[1024,2048]{1,0:T(8,128)(2,1)}, bf16[1024,1536]{1,0:T(8,128)(2,1)}, bf16[1024,1536]{1,0:T(8,128)(2,1)}, bf16...) custom-call(bf16[256,2048]{1,0:T(8,128)(2,1)} %multiply_convert_fusion.own_ref, bf16[256,2048]{1,0:T(8,128)(2,1)} %copy-done.2, ...), custom_call_target="tpu_custom_call" | custom-call | flops 45097156608 | bytes 62914560 | tf_op jit(solution)/shard_map/feed_forward/pallas_call | solution.py:637
  237.8 2.9 multiply_reduce_fusion
  241.0 2.3 fusion.23.refs_5_
  243.3 6.3 convolution_convert_fusion.3.do_ref
  249.5 16.7 %attend_back.1 = (bf16[256,2048]{1,0:T(8,128)(2,1)S(1)}, f32[1280,256]{1,0:T(8,128)S(1)}) custom-call(s32[1,256]{1,0:T(1,128)S(1)} %maximum_subtract_fusion.lo_ref, bf16[256,2048]{1,0:T(8,128)(2,1)S(1)} %copy-done.12, bf16[1280,256]{1,0:T(8,128)(2,1)S(1)} %copy-done.8, bf16[256,2048]{1,0:T(8,128)(2,1)S(1)} %convolution_convert_fusion.3.do_ref, ...), custom_call_target="tpu_custom_call" | custom-call | flops 6039797760 | bytes 6291456 | tf_op jit(solution)/shard_map/attend_back/pallas_call | solution.py:130
  268.1 4.4 collective-permute-start.7
  272.5 2.6 collective-permute-start.10
  275.1 4.1 collective-permute-start.9
  279.2 1.9 collective-permute-start.8
  281.1 2.5 copy.29
  284.3 7.4 %collective-permute-done.9 = bf16[256,256]{1,0:T(8,128)(2,1)} collective-permute-done((bf16[256,256]{1,0:T(8,128)(2,1)}, bf16[256,256]{1,0:T(8,128)(2,1)}, u32[]{:S(2)}, u32[]{:S(2)}) %collective-permute-start.9) | collective-permute-done | bytes 131104 | tf_op jit(solution)/shard_map/ppermute | solution.py:1071
  294.9 7.6 %fusion.11 = (f32[2048]{0:T(1024)S(1)}, f32[256]{0:T(256)S(1)}, f32[256,2048]{1,0:T(8,128)}) fusion(bf16[256,2048]{1,0:T(8,128)(2,1)S(1)} %get-tuple-element.36, f32[256]{0:T(256)S(1)} %copy-done.34, f32[2048]{0:T(1024)S(1)} %bitcast.60, f32[256,2048]{1,0:T(8,128)S(1)} %fusion.27, bf16[256,2048]{1,0:T(8,128)(2,1)S(1)} %copy-done.10, ...), kind=kOutput, calls=%fused_computation.21 | convolution fusion | flops 2151675648 | bytes 14698496 | tf_op jit(solution)/shard_map/dot_general | solution.py:41
  303.4 5.3 fusion.10
  309.9 266.8 %sum_grads.1 = (bf16[4,64,1536]{2,1,0:T(8,128)(2,1)}, bf16[4,64,1536]{2,1,0:T(8,128)(2,1)}, bf16[4,64,512]{2,1,0:T(8,128)(2,1)}, bf16[64,2048]{1,0:T(8,128)(2,1)...) custom-call(bf16[1024,2048]{1,0:T(8,128)(2,1)} %get-tuple-element.45.refs_, ...), custom_call_target="tpu_custom_call" | custom-call | flops 17448304640 | bytes 419430400 | tf_op jit(solution)/shard_map/sum_grads/pallas_call | solution.py:975
  578.2 3.0 convert_bitcast_fusion
  581.1 3.1 collective-permute-start.11
  593.3 29.5 %collective-permute-done.11 = bf16[192,2048]{1,0:T(8,128)(2,1)S(1)} collective-permute-done((bf16[192,2048]{1,0:T(8,128)(2,1)}, bf16[192,2048]{1,0:T(8,128)(2,1)S(1)}, u32[]{:S(2)}, u32[]{:S(2)}) %collective-permute-start.11) | collective-permute-done | bytes 786464 | tf_op jit(solution)/shard_map/ppermute | solution.py:1092
  (142 shorter events, 36.3 us)
Async XLA Ops:
  7.2 573.9 %reduce-scatter.2.cloned.1.call-start = ((), (), s32[]{:S(2)}) async-start(), calls=%async_computation.1 | async-start | bytes 7077888 | tf_op jit(solution)/shard_map/reduce_scatter | solution.py:1084
  120.4 18.4 %copy-start.2 = (bf16[256,2048]{1,0:T(8,128)(2,1)}, bf16[256,2048]{1,0:T(8,128)(2,1)S(1)}, u32[]{:S(2)}) copy-start(bf16[256,2048]{1,0:T(8,128)(2,1)S(1)} %get-tuple-element.42.refs_0_) | copy-start | bytes 3145732
  120.4 12.3 %copy-start.38 = (s32[1,2]{1,0:T(1,128)S(1)}, s32[1,2]{1,0:T(1,128)}, u32[]{:S(2)}) copy-start(s32[1,2]{1,0:T(1,128)} %param.13) | copy-start | bytes 28
  120.7 17.9 %copy-start.33 = (f32[256]{0:T(256)}, f32[256]{0:T(256)S(1)}, u32[]{:S(2)}) copy-start(f32[256]{0:T(256)S(1)} %add_rsqrt_fusion.1) | copy-start | bytes 3076
  120.8 17.9 %copy-start.25 = (f32[2,1,1024]{2,1,0:T(1,128)}, f32[2,1,1024]{2,1,0:T(1,128)S(1)}, u32[]{:S(2)}) copy-start(f32[2,1,1024]{2,1,0:T(1,128)S(1)} %get-tuple-element.73) | copy-start | bytes 24580
  121.3 20.4 %collective-permute-start.3 = (bf16[256,256]{1,0:T(8,128)(2,1)S(1)}, bf16[256,256]{1,0:T(8,128)(2,1)S(1)}, u32[]{:S(2)}, u32[]{:S(2)}) collective-permute-start(bf16[256,256]{1,0:T(8,128)(2,1)S(1)} %convolution_convert_fusion.5), channel_id=1, source_target_pairs={{0,2},{2,4},{4,6},{6,8},{8,10},{10,12},{12,14},{14,16},{16,18},{18... | collective-permute-start | bytes 393224 | tf_op jit(solution)/shard_map/ppermute | solution.py:1071
  123.6 17.2 %collective-permute-start.2 = (bf16[256,256]{1,0:T(8,128)(2,1)S(1)}, bf16[256,256]{1,0:T(8,128)(2,1)}, u32[]{:S(2)}, u32[]{:S(2)}) collective-permute-start(bf16[256,256]{1,0:T(8,128)(2,1)S(1)} %convolution_convert_fusion.5), channel_id=1, source_target_pairs={{0,4},{2,6},{4,8},{6,10},{8,12},{10,14},{12,16},{14,18},{16,20},{1... | collective-permute-start | bytes 393224 | tf_op jit(solution)/shard_map/ppermute | solution.py:1071
  127.2 12.7 %collective-permute-start.1 = (bf16[256,256]{1,0:T(8,128)(2,1)S(1)}, bf16[256,256]{1,0:T(8,128)(2,1)}, u32[]{:S(2)}, u32[]{:S(2)}) collective-permute-start(bf16[256,256]{1,0:T(8,128)(2,1)S(1)} %convolution_convert_fusion.5), channel_id=1, source_target_pairs={{0,6},{2,8},{4,10},{6,12},{8,14},{10,16},{12,18},{14,20},{16,22},{... | collective-permute-start | bytes 393224 | tf_op jit(solution)/shard_map/ppermute | solution.py:1071
  129.1 9.6 %collective-permute-start = (bf16[256,256]{1,0:T(8,128)(2,1)S(1)}, bf16[256,256]{1,0:T(8,128)(2,1)}, u32[]{:S(2)}, u32[]{:S(2)}) collective-permute-start(bf16[256,256]{1,0:T(8,128)(2,1)S(1)} %convolution_convert_fusion.5), channel_id=1, source_target_pairs={{0,8},{2,10},{4,12},{6,14},{8,16},{10,18},{12,20},{14,22},{16,24},... | collective-permute-start | bytes 393224 | tf_op jit(solution)/shard_map/ppermute | solution.py:1071
  131.1 25.3 %collective-permute-start.5 = (bf16[256,2048]{1,0:T(8,128)(2,1)S(1)}, bf16[256,2048]{1,0:T(8,128)(2,1)}, u32[]{:S(2)}, u32[]{:S(2)}) collective-permute-start(bf16[256,2048]{1,0:T(8,128)(2,1)S(1)} %get-tuple-element.42.refs_0_), channel_id=1, source_target_pairs={{0,1},{1,0},{2,3},{3,2},{4,5},{5,4},{6,7},{7,6},{8,9},{9,8},{10,11... | collective-permute-start | bytes 3145736 | tf_op jit(solution)/shard_map/ppermute | solution.py:1067
  138.6 14.1 %copy-start.11 = (bf16[256,2048]{1,0:T(8,128)(2,1)}, bf16[256,2048]{1,0:T(8,128)(2,1)S(1)}, u32[]{:S(2)}) copy-start(bf16[256,2048]{1,0:T(8,128)(2,1)S(1)} %convolution_convert_fusion.4.q_ref) | copy-start | bytes 3145732
  138.8 24.9 %collective-permute-start.4 = (bf16[256,2048]{1,0:T(8,128)(2,1)S(1)}, bf16[256,2048]{1,0:T(8,128)(2,1)S(1)}, u32[]{:S(2)}, u32[]{:S(2)}) collective-permute-start(bf16[256,2048]{1,0:T(8,128)(2,1)S(1)} %get-tuple-element.42.refs_0_), channel_id=1, source_target_pairs={{0,2},{2,0},{1,3},{3,1},{4,6},{6,4},{5,7},{7,5},{8,10},{10,8},{9,1... | collective-permute-start | bytes 3145736 | tf_op jit(solution)/shard_map/ppermute | solution.py:1064
  141.8 10.9 %copy-start.7 = (bf16[1280,256]{1,0:T(8,128)(2,1)}, bf16[1280,256]{1,0:T(8,128)(2,1)S(1)}, u32[]{:S(2)}) copy-start(bf16[1280,256]{1,0:T(8,128)(2,1)S(1)} %constant_dynamic-update-slice_fusion.kv_ref) | copy-start | bytes 1966084
  156.4 7.5 %collective-permute-start.6 = (bf16[256,2048]{1,0:T(8,128)(2,1)}, bf16[256,2048]{1,0:T(8,128)(2,1)S(1)}, u32[]{:S(2)}, u32[]{:S(2)}) collective-permute-start(bf16[256,2048]{1,0:T(8,128)(2,1)} %collective-permute-done.5.refs_2_), channel_id=1, source_target_pairs={{0,2},{2,0},{1,3},{3,1},{4,6},{6,4},{5,7},{7,5},{8,10},{10,8},{9,1... | collective-permute-start | bytes 3145736 | tf_op jit(solution)/shard_map/ppermute | solution.py:1064
  162.2 78.5 %copy-start.29 = (f32[256]{0:T(256)}, f32[256]{0:T(256)S(1)}, u32[]{:S(2)}) copy-start(f32[256]{0:T(256)S(1)} %add_rsqrt_fusion) | copy-start | bytes 3076
  268.1 16.2 %collective-permute-start.7 = (bf16[256,256]{1,0:T(8,128)(2,1)}, bf16[256,256]{1,0:T(8,128)(2,1)S(1)}, u32[]{:S(2)}, u32[]{:S(2)}) collective-permute-start(bf16[256,256]{1,0:T(8,128)(2,1)} %get-tuple-element.68), channel_id=1, source_target_pairs={{8,0},{10,2},{12,4},{14,6},{16,8},{18,10},{20,12},{22,14},{24,16},... | collective-permute-start | bytes 393224 | tf_op jit(solution)/shard_map/ppermute | solution.py:1071
  272.5 11.8 %collective-permute-start.10 = (bf16[256,256]{1,0:T(8,128)(2,1)}, bf16[256,256]{1,0:T(8,128)(2,1)}, u32[]{:S(2)}, u32[]{:S(2)}) collective-permute-start(bf16[256,256]{1,0:T(8,128)(2,1)} %get-tuple-element.69), channel_id=1, source_target_pairs={{2,0},{4,2},{6,4},{8,6},{10,8},{12,10},{14,12},{16,14},{18,16},{20... | collective-permute-start | bytes 393224 | tf_op jit(solution)/shard_map/ppermute | solution.py:1071
  275.1 16.6 %collective-permute-start.9 = (bf16[256,256]{1,0:T(8,128)(2,1)}, bf16[256,256]{1,0:T(8,128)(2,1)}, u32[]{:S(2)}, u32[]{:S(2)}) collective-permute-start(bf16[256,256]{1,0:T(8,128)(2,1)} %get-tuple-element.70), channel_id=1, source_target_pairs={{4,0},{6,2},{8,4},{10,6},{12,8},{14,10},{16,12},{18,14},{20,16},{2... | collective-permute-start | bytes 393224 | tf_op jit(solution)/shard_map/ppermute | solution.py:1071
  279.2 12.6 %collective-permute-start.8 = (bf16[256,256]{1,0:T(8,128)(2,1)}, bf16[256,256]{1,0:T(8,128)(2,1)}, u32[]{:S(2)}, u32[]{:S(2)}) collective-permute-start(bf16[256,256]{1,0:T(8,128)(2,1)} %get-tuple-element.71), channel_id=1, source_target_pairs={{6,0},{8,2},{10,4},{12,6},{14,8},{16,10},{18,12},{20,14},{22,16},{... | collective-permute-start | bytes 393224 | tf_op jit(solution)/shard_map/ppermute | solution.py:1071
  284.3 10.5 %copy-start.10 = (bf16[256,2048]{1,0:T(8,128)(2,1)S(1)}, bf16[256,2048]{1,0:T(8,128)(2,1)}, u32[]{:S(2)}) copy-start(bf16[256,2048]{1,0:T(8,128)(2,1)} %copy-done.9) | copy-start | bytes 3145732
  284.3 10.5 %copy-start.26 = (f32[2,1,1024]{2,1,0:T(1,128)S(1)}, f32[2,1,1024]{2,1,0:T(1,128)}, u32[]{:S(2)}) copy-start(f32[2,1,1024]{2,1,0:T(1,128)} %copy-done.25) | copy-start | bytes 24580
  284.3 10.5 %copy-start.34 = (f32[256]{0:T(256)S(1)}, f32[256]{0:T(256)}, u32[]{:S(2)}) copy-start(f32[256]{0:T(256)} %copy-done.33) | copy-start | bytes 3076
  581.1 41.7 %collective-permute-start.11 = (bf16[192,2048]{1,0:T(8,128)(2,1)}, bf16[192,2048]{1,0:T(8,128)(2,1)S(1)}, u32[]{:S(2)}, u32[]{:S(2)}) collective-permute-start(bf16[192,2048]{1,0:T(8,128)(2,1)} %reduce-scatter.2.cloned.1.call-done), channel_id=1, source_target_pairs={{0,0},{1,16},{2,8},{3,24},{4,1},{5,17},{6,9},{7,25},{8,2},{9,18},{... | collective-permute-start | bytes 2359304 | tf_op jit(solution)/shard_map/ppermute | solution.py:1092
  590.8 33.3 %copy-start.1 = (bf16[1,256,2048]{2,1,0:T(8,128)(2,1)S(1)}, bf16[1,256,2048]{2,1,0:T(8,128)(2,1)}, u32[]{:S(2)}) copy-start(bf16[1,256,2048]{2,1,0:T(8,128)(2,1)} %param.23) | copy-start | bytes 3145732
  (28 other events, 124.8 us)
Sparse Core Ops, SparseCore 0:
  237.9 152.2 reduce-scatter.1

commit v6 on v5

--- a/solution.py
+++ b/solution.py
@@ -51,26 +51,20 @@
     )
 
 
-def bias_of(lo_ref, qb):
+def bias_of(lo, qb):
     key = lax.broadcasted_iota(jnp.int32, (SPAN, QBLK), 0) + qb * QBLK
     query = lax.broadcasted_iota(jnp.int32, (SPAN, QBLK), 1) + (WINDOW + qb * QBLK)
-    allowed = (key >= lo_ref[...]) & (key <= query)
+    allowed = (key >= lo) & (key <= query)
     bias = jnp.where(allowed, 0.0, neg_large).astype(F32)
     return jnp.concatenate([bias] * HEADS_STEP, 1)
 
 
-def attend_kernel(lo_ref, q_ref, kv_ref, o_ref, lse_ref):
-    qb = pl.program_id(0)
-    rows = pl.ds(pl.multiple_of(qb * QBLK, QBLK), SPAN)
-    keys = kv_ref[rows, :HD]
-    values = kv_ref[rows, HD:]
-    scores = mm_nt(keys, stack_heads(q_ref[...])) * scale + bias_of(lo_ref, qb)
+def attend_block(bias, queries, keys, values):
+    scores = mm_nt(keys, queries) * scale + bias
     top = jnp.max(scores, axis=0, keepdims=True)
     raised = jnp.exp(scores - top)
     total = jnp.sum(raised, axis=0, keepdims=True)
-    out_t = mm_tn(values, raised.astype(BF)) * (1.0 / total)
-    o_ref[...] = unstack_heads(out_t).astype(BF)
-    lse_ref[0] = top + jnp.log(total)
+    return mm_tn(values, raised.astype(BF)) * (1.0 / total), top + jnp.log(total)
 
 
 def attend_back_kernel(lo_ref, q_ref, kv_ref, do_ref, lse_ref, dq_ref, dkv_ref):
@@ -85,7 +79,7 @@
     values = kv_ref[rows, HD:]
     queries = stack_heads(q_ref[...])
     d_out = stack_heads(do_ref[...])
-    scores = mm_nt(keys, queries) * scale + bias_of(lo_ref, qb)
+    scores = mm_nt(keys, queries) * scale + bias_of(lo_ref[...], qb)
     probs = jnp.exp(scores - lse_ref[0])
     d_probs = mm_nt(values, d_out)
     delta = jnp.sum(probs * d_probs, axis=0, keepdims=True)
@@ -93,34 +87,6 @@
     dq_ref[...] = unstack_heads(mm_tn(keys, d_scores) * scale).astype(BF)
     dkv_ref[rows, :HD] += mm(d_scores, queries) * scale
     dkv_ref[rows, HD:] += mm(probs.astype(BF), d_out)
-
-
-def attend(queries, window, low):
-    tok = queries.shape[0]
-    groups = H // HEADS_STEP
-    blocks = tok // QBLK
-    return pl.pallas_call(
-        attend_kernel,
-        grid=(blocks, groups),
-        in_specs=[
-            pl.BlockSpec((1, QBLK), lambda i, j: (0, i)),
-            pl.BlockSpec((QBLK, HEADS_STEP * HD), lambda i, j: (i, j)),
-            pl.BlockSpec((WINDOW + tok, 2 * HD), lambda i, j: (0, 0)),
-        ],
-        out_specs=[
-            pl.BlockSpec((QBLK, HEADS_STEP * HD), lambda i, j: (i, j)),
-            pl.BlockSpec((1, 1, ROWS), lambda i, j: (i * groups + j, 0, 0)),
-        ],
-        out_shape=[
-            jax.ShapeDtypeStruct((tok, H * HD), BF),
-            jax.ShapeDtypeStruct((blocks * groups, 1, ROWS), F32),
-        ],
-        compiler_params=pltpu.CompilerParams(vmem_limit_bytes=48 * 1024 * 1024),
-        cost_estimate=pl.CostEstimate(
-            flops=4 * tok * H * HD * SPAN, bytes_accessed=4 * 1024 * 1024, transcendentals=0
-        ),
-        name="attend",
-    )(low, queries, window)
 
 
 def attend_back(queries, window, low, d_context, lse):
@@ -192,8 +158,11 @@
 def fetch_kernel(sizes, pieces, n_in, n_dealt, *refs):
     size_a, size_b, size_x = sizes
     n_ctx = size_a * size_b * 2
-    ins, refs = refs[:n_in], refs[n_in:]
+    ins, low_ref, refs = refs[:n_in], refs[n_in], refs[n_in + 1 :]
     outs, refs = refs[:n_in], refs[n_in:]
+    normed_ref, query_ref, window_out, context_ref, lse_ref, cot_rows, refs = *refs[:6], refs[6:]
+    tok_in, w_query, w_kv, gain_in, window, refs = *refs[:5], refs[5:]
+    load_sem, halo_send, halo_recv, cot_send, cot_recv, refs = *refs[:5], refs[5:]
     n_weights = n_in - n_dealt - 1
     stages, refs = refs[:n_weights], refs[n_weights:]
     keep_sem, own_sem, deal_send, deal_recv, gain_send, gain_recv = refs[:6]
@@ -317,6 +286,114 @@
             cols = full.shape[1]
             src = shard.at[:, pl.ds(pl.multiple_of(rank * cols, cols), cols)]
         return pltpu.make_async_copy(src, stage, sem)
+
+    tok = tok_in.shape[0]
+    halo = WINDOW // tok
+    at_query, at_kv = n_dealt, n_dealt + 1
+
+    def load(src, dst, n):
+        copy = pltpu.make_async_copy(src, dst, load_sem.at[n])
+        copy.start()
+        copy.wait()
+
+    def core_parts_in(i):
+        for s in range(1, size_x):
+            for kind in pieces[i].relays:
+                if kind >= 4:
+                    relay(i, s, kind, True).wait_recv()
+        keep_copy(pieces[i].at, 1).wait()
+
+    def halo_copy(k):
+        e = own + k
+        device = (e // 2 // size_b, e // 2 % size_b, e % 2, ix)
+        src = window.at[pl.ds(WINDOW, tok), :]
+        dst = window.at[pl.ds((halo - k) * tok, tok), :]
+        return remote(src, dst, halo_send.at[k - 1], halo_recv.at[k - 1], device)
+
+    def normalise():
+        for k in range(n_ctx):
+            deal_copy(0, k).wait()
+        for s in range(size_x):
+            gain_copy(s).wait()
+        load(outs[0], tok_in, 0)
+        load(outs[g], gain_in, 1)
+        gain = []
+        for x in range(size_x):
+            values = gain_in[x].astype(F32)
+            gain += [values[r : r + 1, :] for r in range(values.shape[0] // 2)]
+        values = tok_in[...].astype(F32)
+        unit, _ = norm_stats(values)
+        normed_ref[...] = (unit * jnp.concatenate(gain, 1)).astype(BF)
+
+    def keys_values():
+        core_parts_in(1)
+        load(outs[at_kv], w_kv, 2)
+        window[WINDOW:, :] = mm(normed_ref[...], w_kv[...]).astype(BF)
+        for k in range(1, halo + 1):
+
+            @pl.when(own + k < n_ctx)
+            def _():
+                halo_copy(k).start()
+
+            @pl.when(own < k)
+            def _():
+                window[(halo - k) * tok : (halo - k + 1) * tok, :] = jnp.zeros((tok, 2 * HD), BF)
+
+    def project():
+        core_parts_in(0)
+        load(outs[at_query], w_query, 3)
+
+        def step(t, carry):
+            cols = pl.ds(pl.multiple_of(t * 512, 512), 512)
+            query_ref[:, cols] = mm(normed_ref[...], w_query[:, cols]).astype(BF)
+            return carry
+
+        lax.fori_loop(0, H * HD // 512, step, 0)
+
+    def halo_in():
+        for k in range(1, halo + 1):
+
+            @pl.when(own >= k)
+            def _():
+                halo_copy(k).wait_recv()
+
+    def cot_copy(b):
+        sems = (cot_send.at[b], cot_recv.at[b])
+        if b % 2:
+            src = outs[1] if b == 1 else cot_rows.at[b - 2]
+            return remote(src, cot_rows.at[b - 1], *sems, (ia, ib, 1 - ic, ix))
+        device = (ia, ib, ic, (ix + b // 2) % size_x)
+        return remote(outs[1], cot_rows.at[b - 1], *sems, device)
+
+    def spread_cotangent():
+        for k in range(n_ctx):
+            deal_copy(1, k).wait()
+        for s in range(1, size_x):
+            cot_copy(2 * s).start()
+        cot_copy(1).start()
+
+    def attend(qb):
+        low = low_ref[:, qb * QBLK : (qb + 1) * QBLK]
+        bias = bias_of(low, qb)
+        keys = window[qb * QBLK : qb * QBLK + SPAN, :HD]
+        values = window[qb * QBLK : qb * QBLK + SPAN, HD:]
+        rows = slice(qb * QBLK, (qb + 1) * QBLK)
+
+        def step(t, carry):
+            width = HEADS_STEP * HD
+            cols = pl.ds(pl.multiple_of(t * width, width), width)
+            out_t, lse = attend_block(bias, stack_heads(query_ref[rows, cols]), keys, values)
+            context_ref[rows, cols] = unstack_heads(out_t).astype(BF)
+            lse_ref[qb * (H // HEADS_STEP) + t] = lse
+            return carry
+
+        lax.fori_loop(0, H // HEADS_STEP, step, 0)
+
+    blocks = tok // QBLK
+    tasks = {2 * size_x - 1: [normalise, keys_values], 2 * size_x: [spread_cotangent, project]}
+    for qb in range(blocks):
+        task = functools.partial(attend, qb)
+        tasks[2 * size_x + 1 + qb] = [halo_in, task] if qb == 0 else [task]
 
     ahead = 4
     order = [(i, s) for i in range(len(pieces)) for s in range(1, size_x)]
@@ -361,24 +438,35 @@
             if pieces[i].shared:
                 relay(i, s, 7).start()
                 relay(i, s, 8).start()
+        for task in tasks.get(n, []):
+            task()
+
+    for s in range(1, size_x):
+        cot_copy(2 * s).wait_recv()
+        cot_copy(2 * s + 1).start()
+    window_out[...] = window[...]
+    for k in range(1, halo + 1):
+
+        @pl.when(own + k < n_ctx)
+        def _():
+            halo_copy(k).wait_send()
 
     for n, (i, s) in enumerate(order):
         if n + ahead >= len(order):
             x_copy(i, s).wait_send()
         for kind in pieces[i].relays:
             relay(i, s, kind).wait_send()
-            if kind >= 4:
+            if kind >= 4 and i > 1:
                 relay(i, s, kind, True).wait_recv()
-    for t in range(n_dealt):
-        for k in range(n_ctx):
-            deal_copy(t, k).wait()
-    for s in range(size_x):
-        gain_copy(s).wait()
-    for w in range(n_dealt, n_dealt + n_weights):
+    for b in range(1, 2 * size_x):
+        cot_copy(b).wait_send()
+        if b % 2:
+            cot_copy(b).wait_recv()
+    for w in range(n_dealt + 2, n_dealt + n_weights):
         keep_copy(w, 1).wait()
 
 
-def fetch(sizes, dealt, shared, split, gains):
+def fetch(sizes, dealt, shared, split, gains, low):
     size_a, size_b, size_x = sizes
     n_ctx = size_a * size_b * 2
     ins = dealt + shared + split + [gains]
@@ -391,19 +479,41 @@
     pieces = []
     first = len(dealt)
     pieces.append(Piece(first, shared[0].shape[0], True, True, 0, 1))
+    pieces.append(Piece(first + 1, shared[1].shape[0], False, True, 0, 1))
     for part in range(2):
         for n, a in enumerate(split):
             pieces.append(Piece(first + len(shared) + n, a.shape[0], True, False, part, 2))
-    for n, a in enumerate(shared[1:]):
-        pieces.append(Piece(first + 1 + n, a.shape[0], False, True, 0, 1))
+    pieces.append(Piece(first + 2, shared[2].shape[0], False, True, 0, 1))
     count = len(pieces)
+    tok, width = dealt[0].shape
     sem = pltpu.SemaphoreType.DMA
+    vmem = pl.BlockSpec(memory_space=pltpu.VMEM)
     return pl.pallas_call(
         functools.partial(fetch_kernel, sizes, pieces, len(ins), len(dealt)),
-        in_specs=[pl.BlockSpec(memory_space=pl.ANY)] * len(ins),
-        out_specs=[pl.BlockSpec(memory_space=pl.ANY)] * len(outs),
-        out_shape=outs,
+        in_specs=[pl.BlockSpec(memory_space=pl.ANY)] * len(ins) + [vmem],
+        out_specs=[pl.BlockSpec(memory_space=pl.ANY)] * len(outs) + [vmem] * 5 + [pl.BlockSpec(memory_space=pl.ANY)],
+        out_shape=outs
+        + [
+            jax.ShapeDtypeStruct((tok, width), BF),
+            jax.ShapeDtypeStruct((tok, H * HD), BF),
+            jax.ShapeDtypeStruct((WINDOW + tok, 2 * HD), BF),
+            jax.ShapeDtypeStruct((tok, H * HD), BF),
+            jax.ShapeDtypeStruct((tok // QBLK * (H // HEADS_STEP), 1, ROWS), F32),
+            jax.ShapeDtypeStruct((2 * size_x - 1, tok, width), BF),
+        ],
         scratch_shapes=[
+            pltpu.VMEM((tok, width), BF),
+            pltpu.VMEM((width, H * HD), BF),
+            pltpu.VMEM((width, 2 * HD), BF),
+            pltpu.VMEM((size_x,) + gains.shape, BF),
+            pltpu.VMEM((WINDOW + tok, 2 * HD), BF),
+            sem((4,)),
+            sem((WINDOW // tok,)),
+            sem((WINDOW // tok,)),
+            sem((2 * size_x,)),
+            sem((2 * size_x,)),
+        ]
+        + [
             pltpu.VMEM((a.shape[0], o.shape[1]), BF)
             for a, o in zip(ins[len(dealt) : -1], outs[len(dealt) : -1])
         ]
@@ -420,19 +530,19 @@
             sem((count, size_x, 9)),
         ],
         compiler_params=pltpu.CompilerParams(
-            collective_id=1, has_side_effects=True, vmem_limit_bytes=48 * 1024 * 1024
+            collective_id=1, has_side_effects=True, vmem_limit_bytes=60 * 1024 * 1024
         ),
         cost_estimate=pl.CostEstimate(
             flops=0, bytes_accessed=300 * 1024 * 1024, transcendentals=0
         ),
         name="fetch",
-    )(*ins)
+    )(*ins, low)
 
 
 def mlp_kernel(sizes, own_ref, *refs):
     size_a, size_b, size_x = sizes
     ranks = 2 * size_x
-    cots_in, refs = refs[:ranks], refs[ranks:]
+    cots_in, refs = refs[:2], refs[2:]
     weights_in, refs = refs[:3], refs[3:]
     grad_ref, rows_out, dg_out, du_out, part_out, down_out, refs = *refs[:6], refs[6:]
     rows, cot, w_gate, w_up, w_down, hid, dg, du = refs[:8]
@@ -454,8 +564,8 @@
             load_sem.at[3],
         ),
     ]
-    for b in range(ranks):
-        loads.append(pltpu.make_async_copy(cots_in[b], cot.at[b], load_sem.at[4 + b]))
+    loads.append(pltpu.make_async_copy(cots_in[0], cot.at[0], load_sem.at[4]))
+    loads.append(pltpu.make_async_copy(cots_in[1], cot.at[pl.ds(1, ranks - 1)], load_sem.at[5]))
     for copy in loads:
         copy.start()
 
@@ -625,7 +735,7 @@
     down_copy(strips - 1, (strips - 1) % 2).wait()
 
 
-def feed_forward(sizes, normed, cots, w_gate, w_up, down_weight):
+def feed_forward(sizes, normed, cot, cot_rows, w_gate, w_up, down_weight):
     ranks = 2 * sizes[2]
     size_x = sizes[2]
     tok, width = normed.shape
@@ -636,7 +746,7 @@
     hbm = pl.BlockSpec(memory_space=pl.ANY)
     return pl.pallas_call(
         functools.partial(mlp_kernel, sizes),
-        in_specs=[hbm] * (4 + ranks),
+        in_specs=[hbm] * 6,
         out_specs=[pl.BlockSpec(memory_space=pltpu.VMEM)] + [hbm] * 5,
         out_shape=[
             jax.ShapeDtypeStruct((tok, width), F32),
@@ -662,7 +772,7 @@
             pltpu.VMEM((tiles, tok, tile), F32),
             pltpu.VMEM((2, tok, width), BF),
             pltpu.VMEM((2, 256, width), BF),
-            sem((4 + ranks,)),
+            sem((6,)),
             sem((ranks,)),
             sem((ranks,)),
             sem((size_x,)),
@@ -681,7 +791,7 @@
             transcendentals=0,
         ),
         name="feed_forward",
-    )(normed, *cots, w_gate, w_up, down_weight)
+    )(normed, cot, cot_rows, w_gate, w_up, down_weight)
 
 
 class Job:
@@ -1052,19 +1162,9 @@
     width = tokens.shape[2]
     piece = tok // n_ctx
     halo = WINDOW // tok
-    swap = [(0, 1), (1, 0)]
 
     def pick(array, index, axis=0):
         return lax.dynamic_index_in_dim(array, index, axis, keepdims=False)
-
-    def put(array, part, index, axis=0):
-        return lax.dynamic_update_index_in_dim(array, part, index, axis)
-
-    def to_core(array):
-        return lax.ppermute(array, "c", swap)
-
-    def to_x(array, step):
-        return lax.ppermute(array, "x", [(i, (i + step) % size_x) for i in range(size_x)])
 
     def shift_ctx(array, step):
         pairs = [(i, i + step) for i in range(n_ctx) if 0 <= i + step < n_ctx]
@@ -1072,13 +1172,6 @@
 
     def from_x(step):
         return (ix + size_x - step) % size_x
-
-    def group_rows(array):
-        parts = [array, to_core(array)]
-        for step in range(1, size_x):
-            got = to_x(array, step)
-            parts += [got, to_core(got)]
-        return parts
 
     def sum_rows(grad):
         summed = lax.psum_scatter(
@@ -1095,36 +1188,32 @@
     deal = (own_deal[:, None] == jnp.arange(tok, dtype=jnp.int32)[None, :]).astype(BF)
 
     gains = jnp.stack([attn_gain, mlp_gain]).reshape(-1, 128)
-    inputs_low, cot, w_query, w_kv, w_out, w_gate, w_up, gains = fetch(
+    stream = own * tok + jnp.arange(tok, dtype=jnp.int32)
+    ends = jnp.cumsum(lengths[0])
+    starts = jnp.max(jnp.where(stream[:, None] >= ends[None, :], ends[None, :], 0), axis=1)
+    low = jnp.maximum(starts, stream - (WINDOW - 1)) - (own * tok - WINDOW)
+    low = low.astype(jnp.int32)[None, :]
+    inputs_low, cot, w_query, w_kv, w_out, w_gate, w_up, gains, *attended = fetch(
         sizes,
         [mm(deal, tokens[0]).astype(BF), mm(deal, cotangent[0]).astype(BF)],
         [query_weight, kv_weight, out_weight],
         [gate_weight, up_weight],
         gains,
+        low,
     )
+    normed, queries, window, context, lse, cot_rows = attended
     gains = gains.reshape(size_x, 2, -1).astype(F32)
     gain_one = gains[:, 0].reshape(-1)
     gain_two = gains[:, 1].reshape(-1)
 
-    cot_parts = group_rows(cot)
 
     inputs = inputs_low.astype(F32)
     unit_one, inv_one = norm_stats(inputs)
-    normed = (unit_one * gain_one).astype(BF)
-    pairs = mm(normed, w_kv).astype(BF)
-    window = jnp.concatenate([shift_ctx(pairs, halo - j) for j in range(halo)] + [pairs], 0)
-    queries = mm(normed, w_query).astype(BF)
-    stream = own * tok + jnp.arange(tok, dtype=jnp.int32)
-    ends = jnp.cumsum(lengths[0])
-    starts = jnp.max(jnp.where(stream[:, None] >= ends[None, :], ends[None, :], 0), axis=1)
-    low = jnp.maximum(starts, stream - (WINDOW - 1)) - (own * tok - WINDOW)
-    low = low.astype(jnp.int32)[None, :]
-    context, lse = attend(queries, window, low)
     resid = inputs + mm(context, w_out)
 
     unit_two, inv_two = norm_stats(resid)
     d_normed_mlp, mlp_rows, d_gate, d_upward, mlp_parts, down_grad = feed_forward(
-        sizes, (unit_two * gain_two).astype(BF), cot_parts, w_gate, w_up, down_weight
+        sizes, (unit_two * gain_two).astype(BF), cot, cot_rows, w_gate, w_up, down_weight
     )
     down_grad = sum_rows(down_grad)
     d_resid_part, mlp_gain_grad = norm_back(unit_two, inv_two, gain_two, d_normed_mlp)

time: 638 us -> 610 us (0.956)
  starting transfers between devices: 27.5 us -> 15.8 us
  waiting for transfers between devices: 40.6 us -> 30 us
  Pallas kernels: 476 us -> 483 us
    pallas_call x1, Pallas kernels: 110 us -> 131 us  [fetch(): pl.pallas_call(functools.partial(fetch_kernel, sizes, pieces, len(ins), l...]
    pallas_call x2 -> x1, Pallas kernels: 82.8 us -> 71.1 us  [feed_forward(): pl.pallas_call(functools.partial(mlp_kernel, sizes), in_specs=[hbm] * 6,...]
    ppermute x8 -> x4, starting transfers between devices: 22.7 us -> 12.5 us  [shift_ctx(): return lax.ppermute(array, CTX, pairs)]
    ppermute x8 -> x4, waiting for transfers between devices: 7.52 us -> 0.01 us  [shift_ctx(): return lax.ppermute(array, CTX, pairs)]
    dot_general x5 -> x3, matrix products: 13.1 us -> 9.28 us  [mm(): return jnp.dot(left, right, preferred_element_type=F32)]
  transfers between devices with their start and end apart: 13 -> 6, of which waited for: 4 -> 1; matrix products, arithmetic and copies ran while one was open for 10% -> 7% of each run, Pallas kernels for 47% -> 46%
where the time goes in v6:
time: 610 us; the launch traced here: 605 us
  Pallas kernels  483 us (79%)
  waiting for transfers between devices  30 us (5%)
  matrix products  27.5 us (5%)
  other arithmetic  17.2 us (3%)
  local copies, waits for them, and re-layouts  17.1 us (3%)
  starting transfers between devices  15.8 us (3%)
  between operations  14.8 us (2%)
    pallas_call x1, Pallas kernels, sum_grads(): pl.pallas_call(functools.partial(grads_kernel, sizes, jobs), in_specs=[pl...  264 us
    pallas_call x1, Pallas kernels, fetch(): pl.pallas_call(functools.partial(fetch_kernel, sizes, pieces, len(ins), l...  131 us
    pallas_call x1, Pallas kernels, feed_forward(): pl.pallas_call(functools.partial(mlp_kernel, sizes), in_specs=[hbm] * 6,...  71.1 us
    ppermute x1, waiting for transfers between devices, sum_rows(): return lax.ppermute(summed, ALL, keep_pairs).astype(F32)  30 us
    pallas_call x1, Pallas kernels, attend_back(): pl.pallas_call(attend_back_kernel, grid=(blocks, groups), in_specs=[pl.Bl...  16.7 us
    dot_general x3, matrix products, mm_nt(): lax.dot_general(left, right, (((1,), (1,)), ((), ())), preferred_element_...  14.9 us
    ppermute x4, starting transfers between devices, shift_ctx(): return lax.ppermute(array, CTX, pairs)  12.5 us
  transfers between devices with their start and end apart: 6, of which 1 were waited for; matrix products, arithmetic and copies ran while one was open for 7% of the time, Pallas kernels for 46%

profile of v6, /device:TPU:20, one launch (start us, length us, event | category | flops | bytes accessed | tf_op | source)
XLA Modules:
  0.0 605.4 jit_solution(13092816896530960168)
XLA Ops:
  9.0 1.5 convolution_convert_fusion.1.refs_1_
  10.4 1.5 convolution_convert_fusion.2.refs_0_
  13.2 131.1 %fetch.1 = (bf16[256,2048]{1,0:T(8,128)(2,1)}, bf16[256,2048]{1,0:T(8,128)(2,1)}, bf16[2048,2048]{1,0:T(8,128)(2,1)}, bf16[2048,256]{1,0:T(8,128)(2,1)}, bf16[20...) custom-call(bf16[256,2048]{1,0:T(8,128)(2,1)} %convolution_convert_f, ...), custom_call_target="tpu_custom_call" | custom-call | bytes 314572800 | tf_op jit(solution)/shard_map/fetch/pallas_call | solution.py:491
  144.3 6.4 %multiply_reduce_fusion.2 = (f32[256]{0:T(256)S(1)}, f32[256,2048]{1,0:T(8,128)S(1)}) fusion(bf16[256,2048]{1,0:T(8,128)(2,1)} %get-tuple-element.41, bf16[2048,2048]{1,0:T(8,128)(2,1)} %get-tuple-element.42, bf16[256,2048]{1,0:T(8,128)(2,1)} %get-tuple-element.40), kind=kOutput, calls=%fused_computation.24 | convolution fusion | flops 2149580544 | bytes 12583936 | tf_op jit(solution)/shard_map/dot_general | solution.py:33
  153.2 71.1 %feed_forward.1 = (f32[256,2048]{1,0:T(8,128)}, bf16[1024,2048]{1,0:T(8,128)(2,1)}, bf16[1024,1536]{1,0:T(8,128)(2,1)}, bf16[1024,1536]{1,0:T(8,128)(2,1)}, bf16...) custom-call(bf16[256,2048]{1,0:T(8,128)(2,1)} %multiply_convert_fusion.own_ref, ...), custom_call_target="tpu_custom_call" | custom-call | flops 45097156608 | bytes 62914560 | tf_op jit(solution)/shard_map/feed_forward/pallas_call | solution.py:747
  224.4 1.6 copy-done.8
  226.0 2.9 multiply_reduce_fusion
  229.7 6.8 %convolution_convert_fusion.3.do_ref = bf16[256,2048]{1,0:T(8,128)(2,1)S(1)} fusion(bf16[256,2048]{1,0:T(8,128)(2,1)S(1)} %fusion.18.refs_5_, bf16[2048,2048]{1,0:T(8,128)(2,1)} %get-tuple-element.42), kind=kOutput, calls=%fused_computation.11 | convolution fusion | flops 2148007936 | bytes 10485760 | tf_op jit(solution)/shard_map/dot_general | solution.py:41
  236.5 16.7 %attend_back.1 = (bf16[256,2048]{1,0:T(8,128)(2,1)S(1)}, f32[1280,256]{1,0:T(8,128)S(1)}) custom-call(s32[1,256]{1,0:T(1,128)S(1)} %copy-done.2, bf16[256,2048]{1,0:T(8,128)(2,1)S(1)} %copy-done.3, bf16[1280,256]{1,0:T(8,128)(2,1)S(1)} %copy-done.4, bf16[256,2048]{1,0:T(8,128)(2,1)S(1)} %convolution_convert_fusion.3.do_ref, f32[8,1,512]{2,1,0:T(1,128)S(1)} %copy-done.5), custom_call_target="tpu_custom_call" | custom-call | flops 6039797760 | bytes 6291456 | tf_op jit(solution)/shard_map/attend_back/pallas_call | solution.py:96
  254.2 3.3 collective-permute-start
  257.6 3.1 collective-permute-start.1
  260.7 3.4 collective-permute-start.2
  264.1 2.7 collective-permute-start.3
  266.8 2.7 copy.30
  270.8 2.3 copy.29
  273.4 6.0 fusion.22
  280.6 2.1 fusion.9
  283.6 4.7 fusion.8.refs_9_
  288.3 264.1 %sum_grads.1 = (bf16[4,64,1536]{2,1,0:T(8,128)(2,1)}, bf16[4,64,1536]{2,1,0:T(8,128)(2,1)}, bf16[4,64,512]{2,1,0:T(8,128)(2,1)}, bf16[64,2048]{1,0:T(8,128)(2,1)...) custom-call(bf16[1024,2048]{1,0:T(8,128)(2,1)} %get-tuple-element.48.refs_, ...), custom_call_target="tpu_custom_call" | custom-call | flops 17448304640 | bytes 419430400 | tf_op jit(solution)/shard_map/sum_grads/pallas_call | solution.py:1085
  552.3 1.8 convert_bitcast_fusion
  556.7 3.3 collective-permute-start.4
  563.1 1.9 convolution_bitcast_fusion
  565.0 1.5 fusion.3
  567.1 30.0 %collective-permute-done.4 = bf16[192,2048]{1,0:T(8,128)(2,1)S(1)} collective-permute-done((bf16[192,2048]{1,0:T(8,128)(2,1)}, bf16[192,2048]{1,0:T(8,128)(2,1)S(1)}, u32[]{:S(2)}, u32[]{:S(2)}) %collective-permute-start.4) | collective-permute-done | bytes 786464 | tf_op jit(solution)/shard_map/ppermute | solution.py:1185
  (110 shorter events, 18.5 us)
Async XLA Ops:
  7.2 549.5 %reduce-scatter.2.cloned.1.call-start = ((), (), s32[]{:S(2)}) async-start(), calls=%async_computation.1 | async-start | bytes 7077888 | tf_op jit(solution)/shard_map/reduce_scatter | solution.py:1177
  144.3 6.4 %copy-start.31 = (bf16[2,16,128]{2,1,0:T(8,128)(2,1)S(1)}, bf16[2,16,128]{2,1,0:T(8,128)(2,1)}, u32[]{:S(2)}) copy-start(bf16[2,16,128]{2,1,0:T(8,128)(2,1)} %get-tuple-element.43) | copy-start | bytes 24580
  150.7 78.2 %copy-start.27 = (f32[256]{0:T(256)}, f32[256]{0:T(256)S(1)}, u32[]{:S(2)}) copy-start(f32[256]{0:T(256)S(1)} %add_rsqrt_fusion.1) | copy-start | bytes 3076
  229.6 6.9 %copy-start.19 = (bf16[256,2048]{1,0:T(8,128)(2,1)}, bf16[256,2048]{1,0:T(8,128)(2,1)S(1)}, u32[]{:S(2)}) copy-start(bf16[256,2048]{1,0:T(8,128)(2,1)S(1)} %fusion.18.refs_5_) | copy-start | bytes 3145732
  229.6 6.9 %copy-start.2 = (s32[1,256]{1,0:T(1,128)S(1)}, s32[1,256]{1,0:T(1,128)}, u32[]{:S(2)}) copy-start(s32[1,256]{1,0:T(1,128)} %maximum_subtract_fusion.refs_8_.lo_ref) | copy-start | bytes 3076
  229.6 6.9 %copy-start.3 = (bf16[256,2048]{1,0:T(8,128)(2,1)S(1)}, bf16[256,2048]{1,0:T(8,128)(2,1)}, u32[]{:S(2)}) copy-start(bf16[256,2048]{1,0:T(8,128)(2,1)} %get-tuple-element.53.q_ref) | copy-start | bytes 3145732
  229.6 6.9 %copy-start.4 = (bf16[1280,256]{1,0:T(8,128)(2,1)S(1)}, bf16[1280,256]{1,0:T(8,128)(2,1)}, u32[]{:S(2)}) copy-start(bf16[1280,256]{1,0:T(8,128)(2,1)} %get-tuple-element.54.kv_ref) | copy-start | bytes 1966084
  229.6 6.9 %copy-start.5 = (f32[8,1,512]{2,1,0:T(1,128)S(1)}, f32[8,1,512]{2,1,0:T(1,128)}, u32[]{:S(2)}) copy-start(f32[8,1,512]{2,1,0:T(1,128)} %get-tuple-element.55.lse_ref) | copy-start | bytes 49156
  253.2 20.1 %copy-start.6 = (bf16[256,2048]{1,0:T(8,128)(2,1)}, bf16[256,2048]{1,0:T(8,128)(2,1)S(1)}, u32[]{:S(2)}) copy-start(bf16[256,2048]{1,0:T(8,128)(2,1)S(1)} %get-tuple-element.56.refs_6_) | copy-start | bytes 3145732
  254.2 25.2 %collective-permute-start = (bf16[256,256]{1,0:T(8,128)(2,1)}, bf16[256,256]{1,0:T(8,128)(2,1)S(1)}, u32[]{:S(2)}, u32[]{:S(2)}) collective-permute-start(bf16[256,256]{1,0:T(8,128)(2,1)} %get-tuple-element.74), channel_id=1, source_target_pairs={{8,0},{10,2},{12,4},{14,6},{16,8},{18,10},{20,12},{22,14},{24,16},... | collective-permute-start | bytes 393224 | tf_op jit(solution)/shard_map/ppermute | solution.py:1171
  257.6 21.8 %collective-permute-start.1 = (bf16[256,256]{1,0:T(8,128)(2,1)}, bf16[256,256]{1,0:T(8,128)(2,1)}, u32[]{:S(2)}, u32[]{:S(2)}) collective-permute-start(bf16[256,256]{1,0:T(8,128)(2,1)} %get-tuple-element.77), channel_id=1, source_target_pairs={{6,0},{8,2},{10,4},{12,6},{14,8},{16,10},{18,12},{20,14},{22,16},{... | collective-permute-start | bytes 393224 | tf_op jit(solution)/shard_map/ppermute | solution.py:1171
  260.7 18.7 %collective-permute-start.2 = (bf16[256,256]{1,0:T(8,128)(2,1)}, bf16[256,256]{1,0:T(8,128)(2,1)}, u32[]{:S(2)}, u32[]{:S(2)}) collective-permute-start(bf16[256,256]{1,0:T(8,128)(2,1)} %get-tuple-element.76), channel_id=1, source_target_pairs={{4,0},{6,2},{8,4},{10,6},{12,8},{14,10},{16,12},{18,14},{20,16},{2... | collective-permute-start | bytes 393224 | tf_op jit(solution)/shard_map/ppermute | solution.py:1171
  264.1 9.0 %copy-start.11 = (bf16[256,2048]{1,0:T(8,128)(2,1)S(1)}, bf16[256,2048]{1,0:T(8,128)(2,1)}, u32[]{:S(2)}) copy-start(bf16[256,2048]{1,0:T(8,128)(2,1)} %get-tuple-element.40) | copy-start | bytes 3145732
  264.1 15.3 %collective-permute-start.3 = (bf16[256,256]{1,0:T(8,128)(2,1)}, bf16[256,256]{1,0:T(8,128)(2,1)}, u32[]{:S(2)}, u32[]{:S(2)}) collective-permute-start(bf16[256,256]{1,0:T(8,128)(2,1)} %get-tuple-element.75), channel_id=1, source_target_pairs={{2,0},{4,2},{6,4},{8,6},{10,8},{12,10},{14,12},{16,14},{18,16},{20... | collective-permute-start | bytes 393224 | tf_op jit(solution)/shard_map/ppermute | solution.py:1171
  273.4 7.2 %copy-start.12 = (bf16[256,2048]{1,0:T(8,128)(2,1)S(1)}, bf16[256,2048]{1,0:T(8,128)(2,1)}, u32[]{:S(2)}) copy-start(bf16[256,2048]{1,0:T(8,128)(2,1)} %get-tuple-element.40) | copy-start | bytes 3145732
  273.4 7.2 %copy-start.18 = (bf16[2048,256]{1,0:T(8,128)(2,1)S(1)}, bf16[2048,256]{1,0:T(8,128)(2,1)}, u32[]{:S(2)}) copy-start(bf16[2048,256]{1,0:T(8,128)(2,1)} %get-tuple-element.60) | copy-start | bytes 3145732
  555.4 4.6 copy-start.22
  555.4 5.5 copy-start.21
  556.7 5.0 copy-start.24
  556.7 6.4 %copy-start.15 = (bf16[256,2048]{1,0:T(8,128)(2,1)S(1)}, bf16[256,2048]{1,0:T(8,128)(2,1)}, u32[]{:S(2)}) copy-start(bf16[256,2048]{1,0:T(8,128)(2,1)} %get-tuple-element.62) | copy-start | bytes 3145732
  556.7 6.4 %copy-start.26 = (s32[1,1,256]{2,1,0:T(1,128)S(1)}, s32[1,1,256]{2,1,0:T(1,128)}, u32[]{:S(2)}) copy-start(s32[1,1,256]{2,1,0:T(1,128)} %copy-done.25) | copy-start | bytes 3076
  556.7 40.4 %collective-permute-start.4 = (bf16[192,2048]{1,0:T(8,128)(2,1)}, bf16[192,2048]{1,0:T(8,128)(2,1)S(1)}, u32[]{:S(2)}, u32[]{:S(2)}) collective-permute-start(bf16[192,2048]{1,0:T(8,128)(2,1)} %reduce-scatter.2.cloned.1.call-done), channel_id=1, source_target_pairs={{0,0},{1,16},{2,8},{3,24},{4,1},{5,17},{6,9},{7,25},{8,2},{9,18},{... | collective-permute-start | bytes 2359304 | tf_op jit(solution)/shard_map/ppermute | solution.py:1185
  560.9 4.1 copy-start.17
  565.0 33.4 %copy-start.1 = (bf16[1,256,2048]{2,1,0:T(8,128)(2,1)S(1)}, bf16[1,256,2048]{2,1,0:T(8,128)(2,1)}, u32[]{:S(2)}) copy-start(bf16[1,256,2048]{2,1,0:T(8,128)(2,1)} %param.23) | copy-start | bytes 3145732
  (16 other events, 39.6 us)
Sparse Core Ops, SparseCore 0:
  224.5 155.4 reduce-scatter.1

commit v7 on v6

--- a/solution.py
+++ b/solution.py
@@ -65,58 +65,6 @@
     raised = jnp.exp(scores - top)
     total = jnp.sum(raised, axis=0, keepdims=True)
     return mm_tn(values, raised.astype(BF)) * (1.0 / total), top + jnp.log(total)
-
-
-def attend_back_kernel(lo_ref, q_ref, kv_ref, do_ref, lse_ref, dq_ref, dkv_ref):
-    qb = pl.program_id(0)
-
-    @pl.when((qb == 0) & (pl.program_id(1) == 0))
-    def _():
-        dkv_ref[...] = jnp.zeros_like(dkv_ref)
-
-    rows = pl.ds(pl.multiple_of(qb * QBLK, QBLK), SPAN)
-    keys = kv_ref[rows, :HD]
-    values = kv_ref[rows, HD:]
-    queries = stack_heads(q_ref[...])
-    d_out = stack_heads(do_ref[...])
-    scores = mm_nt(keys, queries) * scale + bias_of(lo_ref[...], qb)
-    probs = jnp.exp(scores - lse_ref[0])
-    d_probs = mm_nt(values, d_out)
-    delta = jnp.sum(probs * d_probs, axis=0, keepdims=True)
-    d_scores = (probs * (d_probs - delta)).astype(BF)
-    dq_ref[...] = unstack_heads(mm_tn(keys, d_scores) * scale).astype(BF)
-    dkv_ref[rows, :HD] += mm(d_scores, queries) * scale
-    dkv_ref[rows, HD:] += mm(probs.astype(BF), d_out)
-
-
-def attend_back(queries, window, low, d_context, lse):
-    tok = queries.shape[0]
-    groups = H // HEADS_STEP
-    blocks = tok // QBLK
-    return pl.pallas_call(
-        attend_back_kernel,
-        grid=(blocks, groups),
-        in_specs=[
-            pl.BlockSpec((1, QBLK), lambda i, j: (0, i)),
-            pl.BlockSpec((QBLK, HEADS_STEP * HD), lambda i, j: (i, j)),
-            pl.BlockSpec((WINDOW + tok, 2 * HD), lambda i, j: (0, 0)),
-            pl.BlockSpec((QBLK, HEADS_STEP * HD), lambda i, j: (i, j)),
-            pl.BlockSpec((1, 1, ROWS), lambda i, j: (i * groups + j, 0, 0)),
-        ],
-        out_specs=[
-            pl.BlockSpec((QBLK, HEADS_STEP * HD), lambda i, j: (i, j)),
-            pl.BlockSpec((WINDOW + tok, 2 * HD), lambda i, j: (0, 0)),
-        ],
-        out_shape=[
-            jax.ShapeDtypeStruct((tok, H * HD), BF),
-            jax.ShapeDtypeStruct((WINDOW + tok, 2 * HD), F32),
-        ],
-        compiler_params=pltpu.CompilerParams(vmem_limit_bytes=48 * 1024 * 1024),
-        cost_estimate=pl.CostEstimate(
-            flops=10 * tok * H * HD * SPAN, bytes_accessed=6 * 1024 * 1024, transcendentals=0
-        ),
-        name="attend_back",
-    )(low, queries, window, d_context, lse)
 
 
 def snake(pos, size_a, size_b):
@@ -144,6 +92,222 @@
 def kept_slot(a, b, size_a, size_b):
     half = size_a * size_b // 2
     return (1 - b % 2) * half + a * (size_b // 2) + b // 2
+
+
+def back_kernel(sizes, low_ref, q_ref, kv_ref, branch_ref, lse_ref, down_in, *refs):
+    size_a, size_b, size_x = sizes
+    weights_in, refs = refs[:3], refs[3:]
+    dq_ref, pairs_ref, sum_ref, normed_ref, refs = *refs[:4], refs[4:]
+    w_out, w_query, w_kv, do_ref, refs = *refs[:4], refs[4:]
+    dkv, down, recv, send, halo_out, halo_in = refs[:6]
+    load_sem, send_sem, recv_sem, halo_send, halo_recv = refs[6:]
+    chips = size_a * size_b
+    n_ctx = chips * 2
+    ia, ib, ic, ix = (lax.axis_index(name) for name in ALL)
+    own = (ia * size_b + ib) * 2 + ic
+    place = snake_place(ia, ib, size_a, size_b)
+    tok = q_ref.shape[0]
+    halo = WINDOW // tok
+    groups = H // HEADS_STEP
+    blocks = tok // QBLK * groups
+    part = down.shape[0] // chips
+    quarter = down.shape[1] // 4
+    chains = [(way, sub) for way in range(2) for sub in range(2)]
+    last = chips - 2
+
+    loading = pltpu.make_async_copy(down_in, down, load_sem.at[0])
+    loading.start()
+    weights = [
+        pltpu.make_async_copy(src, dst, load_sem.at[1 + n])
+        for n, (src, dst) in enumerate(zip(weights_in, (w_out, w_query, w_kv)))
+    ]
+    for copy in weights:
+        copy.start()
+    dkv[...] = jnp.zeros_like(dkv)
+
+    def on_ring(step):
+        return snake((place + 2 * chips + step) % chips, size_a, size_b)
+
+    def ctx_device(step):
+        e = (own + n_ctx + step) % n_ctx
+        return e // 2 // size_b, e // 2 % size_b, e % 2, ix
+
+    barrier = pltpu.get_barrier_semaphore()
+    for k in range(1, n_ctx):
+        pl.semaphore_signal(barrier, inc=1, device_id=ctx_device(k), device_id_type=MESH)
+    pl.semaphore_wait(barrier, n_ctx - 1)
+
+    def remote(src, dst, sent, came, device):
+        return pltpu.make_async_remote_copy(
+            src_ref=src,
+            dst_ref=dst,
+            send_sem=sent,
+            recv_sem=came,
+            device_id=device,
+            device_id_type=MESH,
+        )
+
+    def ring_copy(way, sub, step, parity):
+        return remote(
+            send.at[way, sub, parity],
+            recv.at[way, sub, step],
+            send_sem.at[way, sub, parity],
+            recv_sem.at[way, sub, step],
+            on_ring(1 - 2 * way) + (ic, ix),
+        )
+
+    def columns(way, sub):
+        return slice((2 * way + sub) * quarter, (2 * way + sub + 1) * quarter)
+
+    def chunk(way, sub, step):
+        a, b = on_ring(step * (2 * way - 1))
+        rows = pl.ds(pl.multiple_of(kept_slot(a, b, size_a, size_b) * part, part), part)
+        return down[rows, columns(way, sub)]
+
+    def advance(step):
+        parity = step % 2
+        for way, sub in chains:
+            value = chunk(way, sub, step + 1).astype(F32)
+            ring_copy(way, sub, step - 1, 1 - parity).wait_recv()
+            value = value + recv[way, sub, step - 1].astype(F32)
+
+            @pl.when(step >= 2)
+            def _():
+                ring_copy(way, sub, step - 2, parity).wait_send()
+
+            send[way, sub, parity] = value.astype(BF)
+            ring_copy(way, sub, step, parity).start()
+
+    def attend_step(t):
+        qb, hg = t // groups, t % groups
+        width = HEADS_STEP * HD
+        block = pl.ds(pl.multiple_of(qb * QBLK, QBLK), QBLK)
+        cols = pl.ds(pl.multiple_of(hg * width, width), width)
+        rows = pl.ds(pl.multiple_of(qb * QBLK, QBLK), SPAN)
+        keys = kv_ref[rows, :HD]
+        values = kv_ref[rows, HD:]
+        queries = stack_heads(q_ref[block, cols])
+        d_out = stack_heads(do_ref[block, cols])
+        scores = mm_nt(keys, queries) * scale + bias_of(low_ref[qb], qb)
+        probs = jnp.exp(scores - lse_ref[t])
+        d_probs = mm_nt(values, d_out)
+        delta = jnp.sum(probs * d_probs, axis=0, keepdims=True)
+        d_scores = (probs * (d_probs - delta)).astype(BF)
+        dq_ref[block, cols] = unstack_heads(mm_tn(keys, d_scores) * scale).astype(BF)
+        dkv[rows, :HD] += mm(d_scores, queries) * scale
+        dkv[rows, HD:] += mm(probs.astype(BF), d_out)
+
+    def halo_copy(k):
+        sems = (halo_send.at[k - 1], halo_recv.at[k - 1])
+        return remote(halo_out.at[k - 1], halo_in.at[k - 1], *sems, ctx_device(-k))
+
+    def both(step, carry):
+        advance(step)
+        attend_step(2 * step - 2)
+        attend_step(2 * step - 1)
+        return carry
+
+    def alone(step, carry):
+        advance(step)
+        return carry
+
+    tile = 512
+
+    def context_step(t, carry):
+        at = pl.ds(pl.multiple_of(t * tile, tile), tile)
+        do_ref[:, at] = mm_nt(branch_ref[...], w_out[at, :]).astype(BF)
+        return carry
+
+    def normed_step(t, carry):
+        at = pl.ds(pl.multiple_of(t * tile, tile), tile)
+        normed_ref[:, at] = mm_nt(dq_ref[...], w_query[at, :]) + mm_nt(pairs_ref[...], w_kv[at, :])
+        return carry
+
+    loading.wait()
+    for way, sub in chains:
+        send[way, sub, 0] = chunk(way, sub, 1)
+        ring_copy(way, sub, 0, 0).start()
+    weights[0].wait()
+    lax.fori_loop(0, w_out.shape[0] // tile, context_step, 0)
+    busy = blocks // 2
+    lax.fori_loop(1, busy + 1, both, 0)
+    for k in range(1, halo + 1):
+
+        @pl.when(own >= k)
+        def _():
+            halo_out[k - 1] = dkv[(halo - k) * tok : (halo - k + 1) * tok, :].astype(BF)
+            halo_copy(k).start()
+
+    lax.fori_loop(busy + 1, busy + 2, alone, 0)
+    for k in range(1, halo + 1):
+
+        @pl.when(own + k < n_ctx)
+        def _():
+            halo_copy(k).wait_recv()
+            dkv[WINDOW:, :] += halo_in[k - 1].astype(F32)
+
+    pairs_ref[...] = dkv[WINDOW:, :].astype(BF)
+    for copy in weights[1:]:
+        copy.wait()
+    lax.fori_loop(0, w_query.shape[0] // tile, normed_step, 0)
+    lax.fori_loop(busy + 2, last + 1, alone, 0)
+    for way, sub in chains:
+        value = chunk(way, sub, chips).astype(F32)
+        ring_copy(way, sub, last, last % 2).wait_recv()
+        value = value + recv[way, sub, last].astype(F32)
+        sum_ref[:, columns(way, sub)] = value.astype(BF)
+    for way, sub in chains:
+        ring_copy(way, sub, last - 1, (last - 1) % 2).wait_send()
+        ring_copy(way, sub, last, last % 2).wait_send()
+    for k in range(1, halo + 1):
+
+        @pl.when(own >= k)
+        def _():
+            halo_copy(k).wait_send()
+
+
+def attend_back(sizes, queries, window, low, d_branch, lse, down, w_out, w_query, w_kv):
+    chips = sizes[0] * sizes[1]
+    tok = queries.shape[0]
+    halo = WINDOW // tok
+    part, width = down.shape[0] // chips, down.shape[1]
+    sem = pltpu.SemaphoreType.DMA
+    vmem = pl.BlockSpec(memory_space=pltpu.VMEM)
+    return pl.pallas_call(
+        functools.partial(back_kernel, sizes),
+        in_specs=[vmem] * 5 + [pl.BlockSpec(memory_space=pl.ANY)] * 4,
+        out_specs=[vmem] * 4,
+        out_shape=[
+            jax.ShapeDtypeStruct((tok, H * HD), BF),
+            jax.ShapeDtypeStruct((tok, 2 * HD), BF),
+            jax.ShapeDtypeStruct((part, width), BF),
+            jax.ShapeDtypeStruct((tok, width), F32),
+        ],
+        scratch_shapes=[
+            pltpu.VMEM(w_out.shape, BF),
+            pltpu.VMEM(w_query.shape, BF),
+            pltpu.VMEM(w_kv.shape, BF),
+            pltpu.VMEM((tok, H * HD), BF),
+            pltpu.VMEM((WINDOW + tok, 2 * HD), F32),
+            pltpu.VMEM(down.shape, BF),
+            pltpu.VMEM((2, 2, chips - 1, part, width // 4), BF),
+            pltpu.VMEM((2, 2, 2, part, width // 4), BF),
+            pltpu.VMEM((halo, tok, 2 * HD), BF),
+            pltpu.VMEM((halo, tok, 2 * HD), BF),
+            sem((4,)),
+            sem((2, 2, 2)),
+            sem((2, 2, chips - 1)),
+            sem((halo,)),
+            sem((halo,)),
+        ],
+        compiler_params=pltpu.CompilerParams(
+            collective_id=3, has_side_effects=True, vmem_limit_bytes=60 * 1024 * 1024
+        ),
+        cost_estimate=pl.CostEstimate(
+            flops=10 * tok * H * HD * SPAN, bytes_accessed=100 * 1024 * 1024, transcendentals=0
+        ),
+        name="attend_back",
+    )(low.reshape(tok // QBLK, 1, QBLK), queries, window, d_branch, lse, down, w_out, w_query, w_kv)
 
 
 class Piece:
@@ -806,17 +970,18 @@
     n_ctx = 2 * chips
     ranks = 2 * size_x
     count = len(jobs)
-    ins, refs = refs[:12], refs[12:]
+    ins, refs = refs[:13], refs[13:]
     outs, refs = refs[:count], refs[count:]
+    down_out, refs = refs[0], refs[1:]
     dealt, refs = refs[:2], refs[2:]
     gain_out, refs = refs[0], refs[1:]
     held, refs = refs[:8], refs[8:]
-    gain_ctx, gain_x, parts_in, resid_in, block_out, refs = *refs[:5], refs[5:]
+    gain_ctx, gain_x, resid_in, part_own, part_core, part_x, refs = *refs[:6], refs[6:]
     recv, refs = refs[:count], refs[count:]
     send, refs = refs[:count], refs[count:]
     done, refs = refs[:count], refs[count:]
-    load_sem, group_send, group_recv, deal_send, deal_recv = refs[:5]
-    gain_send, gain_recv, send_sem, recv_sem, done_send, done_recv, own_sem = refs[5:]
+    load_sem, group_send, group_recv, deal_send, deal_recv, part_sem = refs[:6]
+    gain_send, gain_recv, send_sem, recv_sem, done_send, done_recv, own_sem = refs[6:]
     ia, ib, ic, ix = (lax.axis_index(name) for name in ALL)
     own = (ia * size_b + ib) * 2 + ic
     rank = ix * 2 + ic
@@ -826,7 +991,7 @@
         return snake((place + 2 * chips + step) % chips, size_a, size_b)
 
     def member(k):
-        return (ic + k // size_x) % 2, (ix + k % size_x) % size_x
+        return (ic + k) % 2, (ix + k // 2) % size_x
 
     def ctx_device(k):
         e = (own + k) % n_ctx
@@ -862,10 +1027,12 @@
 
     barrier = pltpu.get_barrier_semaphore()
     greeted = [ctx_device(k) for k in range(1, n_ctx)] + [from_id]
-    greeted += [(ia, ib) + member(k) for k in range(ranks) if k % size_x]
+    greeted += [(ia, ib) + member(k) for k in range(2, ranks)]
     for device in greeted:
         pl.semaphore_signal(barrier, inc=1, device_id=device, device_id_type=MESH)
     pl.semaphore_wait(barrier, len(greeted))
+
+    passed_on = (3, 5)
 
     def group_copy(i, k):
         c, x = member(k)
@@ -879,11 +1046,13 @@
             src = src.at[:, pl.ds(pl.multiple_of(target * cols, cols), cols)]
         if k == 0:
             return pltpu.make_async_copy(src, dst, load_sem.at[i])
+        if k % 2 and k > 1 and i in passed_on:
+            src, x = held[i].at[k - 1], ix
         return remote(src, dst, group_send.at[i, k], group_recv.at[i, k], (ia, ib, c, x))
 
     def deal_copy(t, k):
         e = (own + k) % n_ctx
-        source = block_out if t == 0 else ins[9]
+        source = part_own.at[0] if t == 0 else ins[9]
         rows = source.shape[0] // n_ctx
         src = source.at[pl.ds(pl.multiple_of(e * rows, rows), rows), :]
         dst = dealt[t].at[pl.ds(pl.multiple_of(own * rows, rows), rows), :]
@@ -891,13 +1060,20 @@
             return pltpu.make_async_copy(src, dst, load_sem.at[8 + t])
         return remote(src, dst, deal_send.at[t, k], deal_recv.at[t, k], ctx_device(k))
 
-    def part_copy(b):
-        src, dst = ins[8].at[b], parts_in.at[b]
-        if b == 0:
-            return pltpu.make_async_copy(src, dst, own_sem.at[count])
-        device = (ia, ib, (ic + b) % 2, (ix + size_x - b // 2) % size_x)
-        return remote(src, dst, group_send.at[0, b], group_recv.at[0, b], device)
-
+    def part_load(step):
+        return pltpu.make_async_copy(ins[8].at[2 * step], part_own.at[step], part_sem.at[step])
+
+    def part_core_copy(step):
+        device = (ia, ib, 1 - ic, ix)
+        src, dst = ins[8].at[2 * step + 1], part_core.at[step]
+        return remote(src, dst, group_send.at[0, step], group_recv.at[0, step], device)
+
+    def part_x_copy(step):
+        device = (ia, ib, ic, (ix + size_x - step) % size_x)
+        src, dst = part_own.at[step], part_x.at[step - 1]
+        return remote(src, dst, group_send.at[1, step], group_recv.at[1, step], device)
+
+    down_copy = remote(ins[12], down_out, done_send.at[count, 0], done_recv.at[count, 0], kept_id)
     resid_copy = pltpu.make_async_copy(ins[11], resid_in, load_sem.at[11])
 
     def gain_copy(k):
@@ -959,81 +1135,126 @@
                 )
         return copies
 
+    def begin(j):
+        for way in range(2):
+            send[j][way, 0] = product(j, way, 1).astype(BF)
+            ring_copy(j, way, 0, 0).start()
+
+    def advance(j, step):
+        parity = step % 2
+        for way in range(2):
+            part = product(j, way, step + 1)
+            ring_copy(j, way, step - 1, 1 - parity).wait_recv()
+            part = part + recv[j][way, step - 1].astype(F32)
+
+            @pl.when(step >= 2)
+            def _():
+                ring_copy(j, way, step - 2, parity).wait_send()
+
+            send[j][way, parity] = part.astype(BF)
+            ring_copy(j, way, step, parity).start()
+
+    last = chips - 2
+
+    def finish(j):
+        cols = jobs[j].cols // 2
+        for way in range(2):
+            part = product(j, way, chips)
+            ring_copy(j, way, last, last % 2).wait_recv()
+            part = part + recv[j][way, last].astype(F32)
+            done[j][:, way * cols : (way + 1) * cols] = part.astype(BF)
+        for copy in deliver(j):
+            copy.start()
+        for way in range(2):
+            ring_copy(j, way, last - 1, (last - 1) % 2).wait_send()
+            ring_copy(j, way, last, last % 2).wait_send()
+
+    early = [j for j in range(count) if jobs[j].phase == 0]
+    late = [j for j in range(count) if jobs[j].phase == 1]
+    lag = 3
+
+    def early_step(step, carry):
+        for j in early:
+            advance(j, step)
+        return carry
+
+    def both_step(step, carry):
+        for j in late:
+            advance(j, step - lag)
+        for j in early:
+            advance(j, step)
+        return carry
+
+    def late_step(step, carry):
+        for j in late:
+            advance(j, step)
+        return carry
+
     for copy in loads:
         copy.wait()
-    for phase in range(2):
-        mine = [j for j in range(count) if jobs[j].phase == phase]
-        for j in mine:
-            for way in range(2):
-                send[j][way, 0] = product(j, way, 1).astype(BF)
-                ring_copy(j, way, 0, 0).start()
-        if phase == 0:
-            for k in range(n_ctx):
-                gain_copy(k).start()
-            for i in range(3, 8):
-                for k in range(ranks):
-                    group_copy(i, k).start()
-            for b in range(ranks):
-                part_copy(b).start()
-            resid_copy.start()
-            for k in range(n_ctx):
-                deal_copy(1, k).start()
-
-        def step_of(step, carry):
-            parity = step % 2
-            for j in mine:
-                for way in range(2):
-                    part = product(j, way, step + 1)
-                    ring_copy(j, way, step - 1, 1 - parity).wait_recv()
-                    part = part + recv[j][way, step - 1].astype(F32)
-
-                    @pl.when(step >= 2)
-                    def _():
-                        ring_copy(j, way, step - 2, parity).wait_send()
-
-                    send[j][way, parity] = part.astype(BF)
-                    ring_copy(j, way, step, parity).start()
-            return carry
-
-        lax.fori_loop(1, chips - 1, step_of, 0)
-        if phase == 0:
-            for k in range(n_ctx):
-                gain_copy(k).wait()
-            gain_x[0] = jnp.sum(gain_ctx[...], axis=0)
-            for s in range(1, size_x):
-                gain_copy_x(s).start()
-            resid_copy.wait()
-            for b in range(ranks):
-                part_copy(b).wait()
-            summed = resid_in[...]
-            for b in range(ranks):
-                summed = summed + parts_in[b].astype(F32)
-            block_out[...] = summed.astype(BF)
-            for k in range(n_ctx):
-                deal_copy(0, k).start()
-        last = chips - 2
-        for j in mine:
-            cols = jobs[j].cols // 2
-            for way in range(2):
-                part = product(j, way, chips)
-                ring_copy(j, way, last, last % 2).wait_recv()
-                part = part + recv[j][way, last].astype(F32)
-                done[j][:, way * cols : (way + 1) * cols] = part.astype(BF)
-            for copy in deliver(j):
-                copy.start()
-            for way in range(2):
-                ring_copy(j, way, last - 1, (last - 1) % 2).wait_send()
-                ring_copy(j, way, last, last % 2).wait_send()
-        if phase == 0:
-            for i in range(3, 8):
-                for k in range(ranks):
-                    group_copy(i, k).wait()
+    for j in early:
+        begin(j)
+    for step in range(size_x):
+        part_load(step).start()
+        part_core_copy(step).start()
+    for i in (6, 7, 5, 4, 3):
+        for k in range(ranks):
+            if not (k % 2 and k > 1 and i in passed_on):
+                group_copy(i, k).start()
+    resid_copy.start()
+    for k in range(n_ctx):
+        gain_copy(k).start()
+    for k in range(n_ctx):
+        deal_copy(1, k).start()
+    down_copy.start()
+    lax.fori_loop(1, 2, early_step, 0)
+    for step in range(size_x):
+        part_load(step).wait()
+        part_core_copy(step).wait()
+    for step in range(1, size_x):
+        summed = part_own[step].astype(F32) + part_core[step].astype(F32)
+        part_own[step] = summed.astype(BF)
+        part_x_copy(step).start()
+    lax.fori_loop(2, lag, early_step, 0)
+    for i in reversed(passed_on):
+        for k in range(2, ranks, 2):
+            group_copy(i, k).wait_recv()
+            group_copy(i, k + 1).start()
+    for k in range(n_ctx):
+        gain_copy(k).wait()
+    gain_x[0] = jnp.sum(gain_ctx[...], axis=0)
+    for s in range(1, size_x):
+        gain_copy_x(s).start()
+    lax.fori_loop(lag, lag + 1, early_step, 0)
+    for i in range(3, 8):
+        for k in range(ranks):
+            if k and k % 2 == 0 and i in passed_on:
+                group_copy(i, k).wait_send()
+            else:
+                group_copy(i, k).wait()
+    for j in late:
+        begin(j)
+    resid_copy.wait()
+    summed = resid_in[...] + part_own[0].astype(F32) + part_core[0].astype(F32)
+    for step in range(1, size_x):
+        part_x_copy(step).wait()
+        summed = summed + part_x[step - 1].astype(F32)
+    part_own[0] = summed.astype(BF)
+    for k in range(n_ctx):
+        deal_copy(0, k).start()
+    lax.fori_loop(lag + 1, last + 1, both_step, 0)
+    for j in early:
+        finish(j)
+    lax.fori_loop(last + 1 - lag, last + 1, late_step, 0)
+    for j in late:
+        finish(j)
     for s in range(1, size_x):
         gain_copy_x(s).wait()
     gain_out[...] = jnp.sum(gain_x[...], axis=0)
     for t in range(2):
         for k in range(n_ctx):
             deal_copy(t, k).wait()
+    down_copy.wait()
     for j in range(count):
         for copy in deliver(j):
             copy.wait()
@@ -1078,6 +1299,7 @@
         done.append(pltpu.VMEM((part, job.cols), BF))
         flops += 2 * job.rows * job.cols * normed_mlp.shape[0]
     count = len(jobs)
+    outs.append(jax.ShapeDtypeStruct(ins[12].shape, BF))
     outs += [jax.ShapeDtypeStruct((tok, width), BF)] * 2
     gain_shape = ins[10].shape[1:]
     outs.append(jax.ShapeDtypeStruct(gain_shape, F32))
@@ -1085,16 +1307,17 @@
     return pl.pallas_call(
         functools.partial(grads_kernel, sizes, jobs),
         in_specs=[pl.BlockSpec(memory_space=pl.ANY)] * len(ins),
-        out_specs=[pl.BlockSpec(memory_space=pl.ANY)] * (count + 2)
+        out_specs=[pl.BlockSpec(memory_space=pl.ANY)] * (count + 3)
         + [pl.BlockSpec(memory_space=pltpu.VMEM)],
         out_shape=outs,
         scratch_shapes=held
         + [
             pltpu.VMEM((2 * chips,) + gain_shape, F32),
             pltpu.VMEM((size_x,) + gain_shape, F32),
-            pltpu.VMEM((ranks, tok, width), BF),
             pltpu.VMEM((tok, width), F32),
-            pltpu.VMEM((tok, width), BF),
+            pltpu.VMEM((size_x, tok, width), BF),
+            pltpu.VMEM((size_x, tok, width), BF),
+            pltpu.VMEM((size_x - 1, tok, width), BF),
         ]
         + recv
         + send
@@ -1107,14 +1330,15 @@
             sem((3, 2 * chips)),
             sem((size_x,)),
             sem((size_x,)),
+            sem((size_x,)),
             sem((count, 2, 2)),
             sem((count, 2, chips - 1)),
-            sem((count, ranks)),
-            sem((count, ranks)),
-            sem((count + 1,)),
+            sem((count + 1, ranks)),
+            sem((count + 1, ranks)),
+            sem((count,)),
         ],
         compiler_params=pltpu.CompilerParams(
-            collective_id=0, has_side_effects=True, vmem_limit_bytes=60 * 1024 * 1024
+            collective_id=0, has_side_effects=True, vmem_limit_bytes=63 * 1024 * 1024
         ),
         cost_estimate=pl.CostEstimate(
             flops=flops, bytes_accessed=400 * 1024 * 1024, transcendentals=0
@@ -1166,24 +1390,6 @@
     def pick(array, index, axis=0):
         return lax.dynamic_index_in_dim(array, index, axis, keepdims=False)
 
-    def shift_ctx(array, step):
-        pairs = [(i, i + step) for i in range(n_ctx) if 0 <= i + step < n_ctx]
-        return lax.ppermute(array, CTX, pairs)
-
-    def from_x(step):
-        return (ix + size_x - step) % size_x
-
-    def sum_rows(grad):
-        summed = lax.psum_scatter(
-            grad.astype(BF), ("a", "b"), scatter_dimension=0, tiled=True
-        )
-        keep_pairs = []
-        for g in range(chips):
-            for c in range(2):
-                for x in range(size_x):
-                    keep_pairs.append(((g * 2 + c) * size_x + x, (x * 2 + c) * chips + g))
-        return lax.ppermute(summed, ALL, keep_pairs).astype(F32)
-
     own_deal = pick(dealing[0], own)
     deal = (own_deal[:, None] == jnp.arange(tok, dtype=jnp.int32)[None, :]).astype(BF)
 
@@ -1215,19 +1421,13 @@
     d_normed_mlp, mlp_rows, d_gate, d_upward, mlp_parts, down_grad = feed_forward(
         sizes, (unit_two * gain_two).astype(BF), cot, cot_rows, w_gate, w_up, down_weight
     )
-    down_grad = sum_rows(down_grad)
     d_resid_part, mlp_gain_grad = norm_back(unit_two, inv_two, gain_two, d_normed_mlp)
     d_resid = cot.astype(F32) + d_resid_part
     d_branch = d_resid.astype(BF)
 
-    d_context = mm_nt(d_branch, w_out).astype(BF)
-    d_queries, d_window = attend_back(queries, window, low, d_context, lse)
-    d_pairs = d_window[halo * tok :]
-    for j in range(halo):
-        part = d_window[j * tok : (j + 1) * tok].astype(BF)
-        d_pairs = d_pairs + shift_ctx(part, j - halo).astype(F32)
-    d_pairs = d_pairs.astype(BF)
-    d_normed = mm_nt(d_queries, w_query) + mm_nt(d_pairs, w_kv)
+    d_queries, d_pairs, down_sum, d_normed = attend_back(
+        sizes, queries, window, low, d_branch, lse, down_grad, w_out, w_query, w_kv
+    )
     d_inputs, attn_gain_grad = norm_back(unit_one, inv_one, gain_one, d_normed)
     gain_part = width // (n_ctx * size_x)
     gain_grads = jnp.stack([attn_gain_grad, mlp_gain_grad]).reshape(2, n_ctx, size_x, gain_part)
@@ -1248,15 +1448,16 @@
             (d_resid + d_inputs).astype(BF),
             gain_grads.reshape(n_ctx, 8, 128),
             resid,
+            down_sum,
         ],
     )
     gate_grad, up_grad, query_grad = (
         v.transpose(1, 0, 2).reshape(v.shape[1], -1).astype(F32) for v in sums[:3]
     )
-    out_grad, kv_grad = (v.astype(F32) for v in sums[3:5])
-    block_output = mm_tn(deal, sums[5]).astype(BF)
-    token_grad = mm_tn(deal, sums[6])
-    gain_grads = lax.dynamic_slice(sums[7].reshape(-1), (ix * 2 * gain_part,), (2 * gain_part,))
+    out_grad, kv_grad, down_grad = (v.astype(F32) for v in sums[3:6])
+    block_output = mm_tn(deal, sums[6]).astype(BF)
+    token_grad = mm_tn(deal, sums[7])
+    gain_grads = lax.dynamic_slice(sums[8].reshape(-1), (ix * 2 * gain_part,), (2 * gain_part,))
     attn_gain_grad, mlp_gain_grad = gain_grads[:gain_part], gain_grads[gain_part:]
     return (
         block_output[None],

time: 610 us -> 605 us (level)
  Pallas kernels: 483 us -> 547 us
  waiting for transfers between devices: 30 us -> 0 us
  starting transfers between devices: 15.8 us -> 0 us
  between operations: 14.8 us -> 1.15 us
  matrix products: 27.5 us -> 14.7 us
    pallas_call x1, Pallas kernels: 16.7 us -> 74.1 us  [attend_back(): pl.pallas_call(functools.partial(back_kernel, sizes), in_specs=[vmem] * 5...]
    ppermute x5 -> x0, waiting for transfers between devices: 30 us -> none  [the longest x1 30 us: sum_rows(): return lax.ppermute(summed, ALL, keep_pairs).astype(F32)]
    ppermute x5 -> x0, starting transfers between devices: 15.8 us -> none  [the longest x4 12.5 us: shift_ctx(): return lax.ppermute(array, CTX, pairs)]
    dot_general x3 -> x0, matrix products: 14.9 us -> none  [mm_nt(): lax.dot_general(left, right, (((1,), (1,)), ((), ())), preferred_element_...]
    pallas_call x1, Pallas kernels: 264 us -> 271 us  [sum_grads(): pl.pallas_call(functools.partial(grads_kernel, sizes, jobs), in_specs=[pl...]
  transfers between devices with their start and end apart: 6 -> 0, of which waited for: 1 -> 0; matrix products, arithmetic and copies ran while one was open for 7% -> 0% of each run, Pallas kernels for 46% -> 0%
where the time goes in v7:
time: 605 us; the launch traced here: 596 us
  Pallas kernels  547 us (90%)
  other arithmetic  19.5 us (3%)
  matrix products  14.7 us (2%)
  local copies, waits for them, and re-layouts  13.6 us (2%)
    pallas_call x1, Pallas kernels, sum_grads(): pl.pallas_call(functools.partial(grads_kernel, sizes, jobs), in_specs=[pl...  271 us
    pallas_call x1, Pallas kernels, fetch(): pl.pallas_call(functools.partial(fetch_kernel, sizes, pieces, len(ins), l...  131 us
    pallas_call x1, Pallas kernels, attend_back(): pl.pallas_call(functools.partial(back_kernel, sizes), in_specs=[vmem] * 5...  74.1 us
    pallas_call x1, Pallas kernels, feed_forward(): pl.pallas_call(functools.partial(mlp_kernel, sizes), in_specs=[hbm] * 6,...  71.4 us

profile of v7, /device:TPU:20, one launch (start us, length us, event | category | flops | bytes accessed | tf_op | source)
XLA Modules:
  0.0 596.4 jit_solution(15710976418441954465)
XLA Ops:
  0.7 0.9 reduce-window.8
  4.8 2.7 convolution_convert_fusion.1.refs_1_
  7.5 1.5 convolution_convert_fusion.2.refs_0_
  9.0 131.2 %fetch.1 = (bf16[256,2048]{1,0:T(8,128)(2,1)}, bf16[256,2048]{1,0:T(8,128)(2,1)}, bf16[2048,2048]{1,0:T(8,128)(2,1)}, bf16[2048,256]{1,0:T(8,128)(2,1)}, bf16[20...) custom-call(bf16[256,2048]{1,0:T(8,128)(2,1)} %convolution_convert_f, ...), custom_call_target="tpu_custom_call" | custom-call | bytes 314572800 | tf_op jit(solution)/shard_map/fetch/pallas_call | solution.py:655
  141.0 2.4 copy.29
  143.4 1.3 copy.30
  144.7 5.8 multiply_reduce_fusion.2
  150.5 1.3 copy-done.2
  151.8 1.2 multiply_convert_fusion.own_ref
  153.1 71.4 %feed_forward.1 = (f32[256,2048]{1,0:T(8,128)}, bf16[1024,2048]{1,0:T(8,128)(2,1)}, bf16[1024,1536]{1,0:T(8,128)(2,1)}, bf16[1024,1536]{1,0:T(8,128)(2,1)}, bf16...) custom-call(bf16[256,2048]{1,0:T(8,128)(2,1)} %multiply_convert_fusion.own_ref, ...), custom_call_target="tpu_custom_call" | custom-call | flops 45097156608 | bytes 62914560 | tf_op jit(solution)/shard_map/feed_forward/pallas_call | solution.py:911
  224.5 2.9 multiply_reduce_fusion
  227.5 3.7 fusion.10
  231.2 74.1 %attend_back.1 = (bf16[256,2048]{1,0:T(8,128)(2,1)}, bf16[256,256]{1,0:T(8,128)(2,1)}, bf16[192,2048]{1,0:T(8,128)(2,1)}, f32[256,2048]{1,0:T(8,128)}) custom-call(s32[2,1,128]{2,1,0:T(1,128)} %maximum_subtract_fusion.low_ref, bf16[256,2048]{1,0:T(8,128)(2,1)} %get-tuple-element.56.q_ref, bf16[1280,256]{1,0:T(8,128)(2,1)} %get-tuple-element.57.kv_ref, ...), custom_call_target="tpu_custom_call" | custom-call | flops 6039797760 | bytes 104857600 | tf_op jit(solution)/shard_map/attend_back/pallas_call | solution.py:276
  305.4 2.4 fusion.9
  307.8 3.8 fusion.8.refs_9_
  312.5 270.8 %sum_grads.1 = (bf16[4,64,1536]{2,1,0:T(8,128)(2,1)}, bf16[4,64,1536]{2,1,0:T(8,128)(2,1)}, bf16[4,64,512]{2,1,0:T(8,128)(2,1)}, bf16[64,2048]{1,0:T(8,128)(2,1)...) custom-call(bf16[1024,2048]{1,0:T(8,128)(2,1)} %get-tuple-element.51, ...), custom_call_target="tpu_custom_call" | custom-call | flops 17448304640 | bytes 419430400 | tf_op jit(solution)/shard_map/sum_grads/pallas_call | solution.py:1307
  583.3 0.8 dynamic_slice.8
  584.1 2.8 fusion.3
  588.2 0.8 copy.34
  589.1 0.8 convert_element_type.83
  589.9 1.9 convolution_bitcast_fusion
  592.0 1.3 copy.35
  593.5 1.3 copy.36
  594.8 1.3 convert_element_type.90
  (57 shorter events, 6.8 us)
Async XLA Ops:
  0.6 1.0 copy-start
  0.7 6.9 %copy-start.9 = (bf16[1,256,2048]{2,1,0:T(8,128)(2,1)S(1)}, bf16[1,256,2048]{2,1,0:T(8,128)(2,1)}, u32[]{:S(2)}) copy-start(bf16[1,256,2048]{2,1,0:T(8,128)(2,1)} %param.12) | copy-start | bytes 3145732
  140.2 3.2 copy-start.8
  141.0 3.7 copy-start.5
  150.5 1.3 copy-start.2
  224.4 3.1 copy-start.3
  305.3 2.4 copy-start.4
  305.3 2.5 copy-start.6
  583.2 4.3 copy-start.15
  583.3 4.9 copy-start.14
  583.3 5.8 copy-start.13
  584.1 5.8 copy-start.7
  589.0 2.7 copy-start.12
  591.9 1.3 copy-start.11
  593.3 2.8 copy-start.1
  593.5 1.3 copy-start.10

commit v8 on v7

--- a/solution.py
+++ b/solution.py
@@ -976,7 +976,7 @@
     dealt, refs = refs[:2], refs[2:]
     gain_out, refs = refs[0], refs[1:]
     held, refs = refs[:8], refs[8:]
-    gain_ctx, gain_x, resid_in, part_own, part_core, part_x, refs = *refs[:6], refs[6:]
+    gain_ctx, gain_x, resid_in, part_own, part_core, part_x, down_passed, refs = *refs[:7], refs[7:]
     recv, refs = refs[:count], refs[count:]
     send, refs = refs[:count], refs[count:]
     done, refs = refs[:count], refs[count:]
@@ -997,9 +997,12 @@
         e = (own + k) % n_ctx
         return e // 2 // size_b, e // 2 % size_b, e % 2, ix
 
+    def keeper(row_chunk):
+        chip = row_chunk // ranks
+        return chip // size_b, chip % size_b, (row_chunk // size_x) % 2, row_chunk % size_x
+
     kept = rank * chips + kept_slot(ia, ib, size_a, size_b)
-    kept_chip = kept // ranks
-    kept_id = (kept_chip // size_b, kept_chip % size_b, (kept // size_x) % 2, kept % size_x)
+    kept_id = keeper(kept)
     flat = own * size_x + ix
     from_rank = flat // chips
     from_slot = flat % chips
@@ -1073,7 +1076,17 @@
         src, dst = part_own.at[step], part_x.at[step - 1]
         return remote(src, dst, group_send.at[1, step], group_recv.at[1, step], device)
 
-    down_copy = remote(ins[12], down_out, done_send.at[count, 0], done_recv.at[count, 0], kept_id)
+    crossing = size_x == 2
+    down_sem = (done_send.at[count, 0], done_recv.at[count, 0])
+    down_copy = remote(ins[12], down_out, *down_sem, kept_id)
+    if crossing:
+        straight = kept % size_x == ix
+        hop_sem = (done_send.at[count, 1], done_recv.at[count, 1])
+        down_hop = remote(ins[12], down_passed, *hop_sem, (ia, ib, ic, 1 - ix))
+        passed_id = keeper(((1 - ix) * 2 + ic) * chips + kept_slot(ia, ib, size_a, size_b))
+        pass_sem = (done_send.at[count, 2], done_recv.at[count, 0])
+        down_pass = remote(down_passed, down_out, *pass_sem, passed_id)
+
     resid_copy = pltpu.make_async_copy(ins[11], resid_in, load_sem.at[11])
 
     def gain_copy(k):
@@ -1206,7 +1219,18 @@
         gain_copy(k).start()
     for k in range(n_ctx):
         deal_copy(1, k).start()
-    down_copy.start()
+    if crossing:
+
+        @pl.when(straight)
+        def _():
+            down_copy.start()
+
+        @pl.when(jnp.logical_not(straight))
+        def _():
+            down_hop.start()
+
+    else:
+        down_copy.start()
     lax.fori_loop(1, 2, early_step, 0)
     for step in range(size_x):
         part_load(step).wait()
@@ -1216,6 +1240,13 @@
         part_own[step] = summed.astype(BF)
         part_x_copy(step).start()
     lax.fori_loop(2, lag, early_step, 0)
+    if crossing:
+
+        @pl.when(straight)
+        def _():
+            down_hop.wait_recv()
+            down_pass.start()
+
     for i in reversed(passed_on):
         for k in range(2, ranks, 2):
             group_copy(i, k).wait_recv()
@@ -1254,7 +1285,20 @@
     for t in range(2):
         for k in range(n_ctx):
             deal_copy(t, k).wait()
-    down_copy.wait()
+    down_copy.wait_recv()
+    if crossing:
+
+        @pl.when(straight)
+        def _():
+            down_copy.wait_send()
+            down_pass.wait_send()
+
+        @pl.when(jnp.logical_not(straight))
+        def _():
+            down_hop.wait_send()
+
+    else:
+        down_copy.wait_send()
     for j in range(count):
         for copy in deliver(j):
             copy.wait()
@@ -1318,6 +1362,7 @@
             pltpu.VMEM((size_x, tok, width), BF),
             pltpu.VMEM((size_x, tok, width), BF),
             pltpu.VMEM((size_x - 1, tok, width), BF),
+            pltpu.VMEM(ins[12].shape, BF),
         ]
         + recv
         + send

time: 605 us -> 600 us (level)
  no operation moved by 1% of the time
where the time goes in v8:
time: 600 us; the launch traced here: 591 us
  Pallas kernels  542 us (90%)
  other arithmetic  19.5 us (3%)
  matrix products  14.7 us (2%)
  local copies, waits for them, and re-layouts  13.6 us (2%)
    pallas_call x1, Pallas kernels, sum_grads(): pl.pallas_call(functools.partial(grads_kernel, sizes, jobs), in_specs=[pl...  265 us
    pallas_call x1, Pallas kernels, fetch(): pl.pallas_call(functools.partial(fetch_kernel, sizes, pieces, len(ins), l...  131 us
    pallas_call x1, Pallas kernels, attend_back(): pl.pallas_call(functools.partial(back_kernel, sizes), in_specs=[vmem] * 5...  74.1 us
    pallas_call x1, Pallas kernels, feed_forward(): pl.pallas_call(functools.partial(mlp_kernel, sizes), in_specs=[hbm] * 6,...  71.4 us

profile of v8, /device:TPU:20, one launch (start us, length us, event | category | flops | bytes accessed | tf_op | source)
XLA Modules:
  0.0 591.1 jit_solution(12517696017236083693)
XLA Ops:
  0.7 0.9 reduce-window.8
  4.8 2.7 convolution_convert_fusion.1.refs_1_
  7.5 1.5 convolution_convert_fusion.2.refs_0_
  9.0 131.2 %fetch.1 = (bf16[256,2048]{1,0:T(8,128)(2,1)}, bf16[256,2048]{1,0:T(8,128)(2,1)}, bf16[2048,2048]{1,0:T(8,128)(2,1)}, bf16[2048,256]{1,0:T(8,128)(2,1)}, bf16[20...) custom-call(bf16[256,2048]{1,0:T(8,128)(2,1)} %convolution_convert_f, ...), custom_call_target="tpu_custom_call" | custom-call | bytes 314572800 | tf_op jit(solution)/shard_map/fetch/pallas_call | solution.py:655
  141.0 2.4 copy.29
  143.4 1.3 copy.30
  144.7 5.8 multiply_reduce_fusion.2
  150.5 1.3 copy-done.2
  151.8 1.2 multiply_convert_fusion.own_ref
  153.1 71.4 %feed_forward.1 = (f32[256,2048]{1,0:T(8,128)}, bf16[1024,2048]{1,0:T(8,128)(2,1)}, bf16[1024,1536]{1,0:T(8,128)(2,1)}, bf16[1024,1536]{1,0:T(8,128)(2,1)}, bf16...) custom-call(bf16[256,2048]{1,0:T(8,128)(2,1)} %multiply_convert_fusion.own_ref, ...), custom_call_target="tpu_custom_call" | custom-call | flops 45097156608 | bytes 62914560 | tf_op jit(solution)/shard_map/feed_forward/pallas_call | solution.py:911
  224.5 2.9 multiply_reduce_fusion
  227.5 3.7 fusion.10
  231.2 74.1 %attend_back.1 = (bf16[256,2048]{1,0:T(8,128)(2,1)}, bf16[256,256]{1,0:T(8,128)(2,1)}, bf16[192,2048]{1,0:T(8,128)(2,1)}, f32[256,2048]{1,0:T(8,128)}) custom-call(s32[2,1,128]{2,1,0:T(1,128)} %maximum_subtract_fusion.low_ref, bf16[256,2048]{1,0:T(8,128)(2,1)} %get-tuple-element.56.q_ref, bf16[1280,256]{1,0:T(8,128)(2,1)} %get-tuple-element.57.kv_ref, ...), custom_call_target="tpu_custom_call" | custom-call | flops 6039797760 | bytes 104857600 | tf_op jit(solution)/shard_map/attend_back/pallas_call | solution.py:276
  305.4 2.4 fusion.9
  307.8 3.8 fusion.8.refs_9_
  312.5 265.5 %sum_grads.1 = (bf16[4,64,1536]{2,1,0:T(8,128)(2,1)}, bf16[4,64,1536]{2,1,0:T(8,128)(2,1)}, bf16[4,64,512]{2,1,0:T(8,128)(2,1)}, bf16[64,2048]{1,0:T(8,128)(2,1)...) custom-call(bf16[1024,2048]{1,0:T(8,128)(2,1)} %get-tuple-element.51, ...), custom_call_target="tpu_custom_call" | custom-call | flops 17448304640 | bytes 419430400 | tf_op jit(solution)/shard_map/sum_grads/pallas_call | solution.py:1351
  578.0 0.8 dynamic_slice.8
  578.8 2.8 fusion.3
  582.9 0.8 copy.34
  583.8 0.8 convert_element_type.83
  584.6 1.9 convolution_bitcast_fusion
  586.7 1.3 copy.35
  588.2 1.3 copy.36
  589.5 1.3 convert_element_type.90
  (57 shorter events, 6.8 us)
Async XLA Ops:
  0.6 1.0 copy-start
  0.7 6.9 %copy-start.9 = (bf16[1,256,2048]{2,1,0:T(8,128)(2,1)S(1)}, bf16[1,256,2048]{2,1,0:T(8,128)(2,1)}, u32[]{:S(2)}) copy-start(bf16[1,256,2048]{2,1,0:T(8,128)(2,1)} %param.12) | copy-start | bytes 3145732
  140.2 3.2 copy-start.8
  141.0 3.7 copy-start.5
  150.5 1.3 copy-start.2
  224.4 3.1 copy-start.3
  305.3 2.4 copy-start.4
  305.3 2.5 copy-start.6
  578.0 4.3 copy-start.15
  578.0 4.9 copy-start.14
  578.0 5.8 copy-start.13
  578.8 5.8 copy-start.7
  583.8 2.7 copy-start.12
  586.7 1.3 copy-start.11
  588.0 2.8 copy-start.1
  588.2 1.3 copy-start.10

commit v9 on v8

--- a/solution.py
+++ b/solution.py
@@ -325,6 +325,7 @@
     ins, low_ref, refs = refs[:n_in], refs[n_in], refs[n_in + 1 :]
     outs, refs = refs[:n_in], refs[n_in:]
     normed_ref, query_ref, window_out, context_ref, lse_ref, cot_rows, refs = *refs[:6], refs[6:]
+    normed_t_ref, context_t_ref, refs = *refs[:2], refs[2:]
     tok_in, w_query, w_kv, gain_in, window, refs = *refs[:5], refs[5:]
     load_sem, halo_send, halo_recv, cot_send, cot_recv, refs = *refs[:5], refs[5:]
     n_weights = n_in - n_dealt - 1
@@ -489,6 +490,14 @@
         unit, _ = norm_stats(values)
         normed_ref[...] = (unit * jnp.concatenate(gain, 1)).astype(BF)
 
+    def transpose():
+        def step(t, carry):
+            at = pl.ds(pl.multiple_of(t * HD, HD), HD)
+            normed_t_ref[at, :] = normed_ref[:, at].astype(F32).T.astype(BF)
+            return carry
+
+        lax.fori_loop(0, normed_ref.shape[1] // HD, step, 0)
+
     def keys_values():
         core_parts_in(1)
         load(outs[at_kv], w_kv, 2)
@@ -548,6 +557,9 @@
             cols = pl.ds(pl.multiple_of(t * width, width), width)
             out_t, lse = attend_block(bias, stack_heads(query_ref[rows, cols]), keys, values)
             context_ref[rows, cols] = unstack_heads(out_t).astype(BF)
+            for h in range(HEADS_STEP):
+                at = pl.ds(pl.multiple_of((t * HEADS_STEP + h) * HD, HD), HD)
+                context_t_ref[at, rows] = out_t[:, h * QBLK : (h + 1) * QBLK].astype(BF)
             lse_ref[qb * (H // HEADS_STEP) + t] = lse
             return carry
 
@@ -559,6 +571,7 @@
         task = functools.partial(attend, qb)
         tasks[2 * size_x + 1 + qb] = [halo_in, task] if qb == 0 else [task]
 
+    tasks[2 * size_x + 1 + blocks] = [transpose]
     ahead = 4
     order = [(i, s) for i in range(len(pieces)) for s in range(1, size_x)]
     for k in range(n_ctx):
@@ -655,7 +668,7 @@
     return pl.pallas_call(
         functools.partial(fetch_kernel, sizes, pieces, len(ins), len(dealt)),
         in_specs=[pl.BlockSpec(memory_space=pl.ANY)] * len(ins) + [vmem],
-        out_specs=[pl.BlockSpec(memory_space=pl.ANY)] * len(outs) + [vmem] * 5 + [pl.BlockSpec(memory_space=pl.ANY)],
+        out_specs=[pl.BlockSpec(memory_space=pl.ANY)] * len(outs) + [vmem] * 5 + [pl.BlockSpec(memory_space=pl.ANY)] + [vmem] * 2,
         out_shape=outs
         + [
             jax.ShapeDtypeStruct((tok, width), BF),
@@ -664,6 +677,8 @@
             jax.ShapeDtypeStruct((tok, H * HD), BF),
             jax.ShapeDtypeStruct((tok // QBLK * (H // HEADS_STEP), 1, ROWS), F32),
             jax.ShapeDtypeStruct((2 * size_x - 1, tok, width), BF),
+            jax.ShapeDtypeStruct((width, tok), BF),
+            jax.ShapeDtypeStruct((H * HD, tok), BF),
         ],
         scratch_shapes=[
             pltpu.VMEM((tok, width), BF),
@@ -1452,7 +1467,7 @@
         gains,
         low,
     )
-    normed, queries, window, context, lse, cot_rows = attended
+    _, queries, window, context, lse, cot_rows, normed_t, context_t = attended
     gains = gains.reshape(size_x, 2, -1).astype(F32)
     gain_one = gains[:, 0].reshape(-1)
     gain_two = gains[:, 1].reshape(-1)
@@ -1484,8 +1499,8 @@
             mlp_rows,
             d_gate,
             d_upward,
-            normed.T,
-            context.T,
+            normed_t,
+            context_t,
             d_branch,
             d_queries,
             d_pairs,

time: 600 us -> 598 us (level)
  no operation moved by 1% of the time
where the time goes in v9:
time: 598 us; the launch traced here: 589 us
  Pallas kernels  543 us (91%)
  other arithmetic  19.5 us (3%)
  matrix products  15.2 us (3%)
  local copies, waits for them, and re-layouts  9.93 us (2%)
    pallas_call x1, Pallas kernels, sum_grads(): pl.pallas_call(functools.partial(grads_kernel, sizes, jobs), in_specs=[pl...  265 us
    pallas_call x1, Pallas kernels, fetch(): pl.pallas_call(functools.partial(fetch_kernel, sizes, pieces, len(ins), l...  132 us
    pallas_call x1, Pallas kernels, attend_back(): pl.pallas_call(functools.partial(back_kernel, sizes), in_specs=[vmem] * 5...  74.1 us
    pallas_call x1, Pallas kernels, feed_forward(): pl.pallas_call(functools.partial(mlp_kernel, sizes), in_specs=[hbm] * 6,...  71.4 us

profile of v9, /device:TPU:20, one launch (start us, length us, event | category | flops | bytes accessed | tf_op | source)
XLA Modules:
  0.0 588.5 jit_solution(1481458754696735787)
XLA Ops:
  0.7 0.9 reduce-window.8
  2.8 0.7 stack.18
  4.8 2.7 convolution_convert_fusion.1.refs_1_
  7.5 1.5 convolution_convert_fusion.2.refs_0_
  9.0 131.8 %fetch.1 = (bf16[256,2048]{1,0:T(8,128)(2,1)}, bf16[256,2048]{1,0:T(8,128)(2,1)}, bf16[2048,2048]{1,0:T(8,128)(2,1)}, bf16[2048,256]{1,0:T(8,128)(2,1)}, bf16[20...) custom-call(bf16[256,2048]{1,0:T(8,128)(2,1)} %convolution_convert_f, ...), custom_call_target="tpu_custom_call" | custom-call | bytes 314572800 | tf_op jit(solution)/shard_map/fetch/pallas_call | solution.py:668
  140.8 0.7 reshape.165
  141.5 6.4 %multiply_reduce_fusion.2 = (f32[256]{0:T(256)S(1)}, f32[256,2048]{1,0:T(8,128)S(1)}) fusion(bf16[256,2048]{1,0:T(8,128)(2,1)} %get-tuple-element.45, bf16[2048,2048]{1,0:T(8,128)(2,1)} %get-tuple-element.46.refs_0_, bf16[256,2048]{1,0:T(8,128)(2,1)} %get-tuple-element.44), kind=kOutput, calls=%fused_computation.22 | convolution fusion | flops 2149580544 | bytes 12583936 | tf_op jit(solution)/shard_map/dot_general | solution.py:33
  147.9 1.3 copy-done.2
  149.2 1.2 multiply_convert_fusion.own_ref
  150.4 71.4 %feed_forward.1 = (f32[256,2048]{1,0:T(8,128)}, bf16[1024,2048]{1,0:T(8,128)(2,1)}, bf16[1024,1536]{1,0:T(8,128)(2,1)}, bf16[1024,1536]{1,0:T(8,128)(2,1)}, bf16...) custom-call(bf16[256,2048]{1,0:T(8,128)(2,1)} %multiply_convert_fusion.own_ref, ...), custom_call_target="tpu_custom_call" | custom-call | flops 45097156608 | bytes 62914560 | tf_op jit(solution)/shard_map/feed_forward/pallas_call | solution.py:926
  221.8 2.9 multiply_reduce_fusion
  224.9 3.7 fusion.10
  228.6 74.1 %attend_back.1 = (bf16[256,2048]{1,0:T(8,128)(2,1)}, bf16[256,256]{1,0:T(8,128)(2,1)}, bf16[192,2048]{1,0:T(8,128)(2,1)}, f32[256,2048]{1,0:T(8,128)}) custom-call(s32[2,1,128]{2,1,0:T(1,128)} %maximum_subtract_fusion.low_ref, bf16[256,2048]{1,0:T(8,128)(2,1)} %get-tuple-element.58.q_ref, bf16[1280,256]{1,0:T(8,128)(2,1)} %get-tuple-element.59.kv_ref, ...), custom_call_target="tpu_custom_call" | custom-call | flops 6039797760 | bytes 104857600 | tf_op jit(solution)/shard_map/attend_back/pallas_call | solution.py:276
  302.8 2.4 fusion.9
  305.3 3.8 fusion.8.refs_9_
  309.9 265.5 %sum_grads.1 = (bf16[4,64,1536]{2,1,0:T(8,128)(2,1)}, bf16[4,64,1536]{2,1,0:T(8,128)(2,1)}, bf16[4,64,512]{2,1,0:T(8,128)(2,1)}, bf16[64,2048]{1,0:T(8,128)(2,1)...) custom-call(bf16[1024,2048]{1,0:T(8,128)(2,1)} %get-tuple-element.52, ...), custom_call_target="tpu_custom_call" | custom-call | flops 17448304640 | bytes 419430400 | tf_op jit(solution)/shard_map/sum_grads/pallas_call | solution.py:1366
  575.4 0.8 dynamic_slice.8
  576.2 2.8 fusion.3
  580.4 0.8 copy.28
  581.2 0.8 convert_element_type.83
  582.0 1.9 convolution_bitcast_fusion
  584.1 1.3 copy.29
  585.6 1.3 copy.30
  586.9 1.3 convert_element_type.90
  (53 shorter events, 5.4 us)
Async XLA Ops:
  0.6 1.0 copy-start
  0.7 6.9 %copy-start.8 = (bf16[1,256,2048]{2,1,0:T(8,128)(2,1)S(1)}, bf16[1,256,2048]{2,1,0:T(8,128)(2,1)}, u32[]{:S(2)}) copy-start(bf16[1,256,2048]{2,1,0:T(8,128)(2,1)} %param.12) | copy-start | bytes 3145732
  147.9 1.3 copy-start.2
  221.8 3.1 copy-start.3
  221.8 3.1 copy-start.5
  302.8 2.4 copy-start.4
  302.8 2.5 copy-start.6
  575.4 4.3 copy-start.14
  575.4 4.9 copy-start.13
  575.4 5.8 copy-start.12
  576.2 5.8 copy-start.7
  581.2 2.7 copy-start.11
  584.1 1.3 copy-start.10
  585.4 2.8 copy-start.1
  585.6 1.3 copy-start.9

commit v10 on v9

--- a/solution.py
+++ b/solution.py
@@ -469,7 +469,7 @@
         keep_copy(pieces[i].at, 1).wait()
 
     def halo_copy(k):
-        e = own + k
+        e = (own + k) % n_ctx
         device = (e // 2 // size_b, e // 2 % size_b, e % 2, ix)
         src = window.at[pl.ds(WINDOW, tok), :]
         dst = window.at[pl.ds((halo - k) * tok, tok), :]

time: 598 us -> 598 us (level)
  no operation moved by 1% of the time
where the time goes in v10:
time: 598 us; the launch traced here: 589 us
  Pallas kernels  543 us (91%)
  other arithmetic  19.5 us (3%)
  matrix products  15.2 us (3%)
  local copies, waits for them, and re-layouts  9.93 us (2%)
    pallas_call x1, Pallas kernels, sum_grads(): pl.pallas_call(functools.partial(grads_kernel, sizes, jobs), in_specs=[pl...  265 us
    pallas_call x1, Pallas kernels, fetch(): pl.pallas_call(functools.partial(fetch_kernel, sizes, pieces, len(ins), l...  132 us
    pallas_call x1, Pallas kernels, attend_back(): pl.pallas_call(functools.partial(back_kernel, sizes), in_specs=[vmem] * 5...  74.1 us
    pallas_call x1, Pallas kernels, feed_forward(): pl.pallas_call(functools.partial(mlp_kernel, sizes), in_specs=[hbm] * 6,...  71.4 us

profile of v10, /device:TPU:20, one launch (start us, length us, event | category | flops | bytes accessed | tf_op | source)
XLA Modules:
  0.0 588.5 jit_solution(1961464674690438193)
XLA Ops:
  0.7 0.9 reduce-window.8
  2.8 0.7 stack.18
  4.8 2.7 convolution_convert_fusion.1.refs_1_
  7.5 1.5 convolution_convert_fusion.2.refs_0_
  9.0 131.8 %fetch.1 = (bf16[256,2048]{1,0:T(8,128)(2,1)}, bf16[256,2048]{1,0:T(8,128)(2,1)}, bf16[2048,2048]{1,0:T(8,128)(2,1)}, bf16[2048,256]{1,0:T(8,128)(2,1)}, bf16[20...) custom-call(bf16[256,2048]{1,0:T(8,128)(2,1)} %convolution_convert_f, ...), custom_call_target="tpu_custom_call" | custom-call | bytes 314572800 | tf_op jit(solution)/shard_map/fetch/pallas_call | solution.py:668
  140.8 0.7 reshape.165
  141.5 6.4 %multiply_reduce_fusion.2 = (f32[256]{0:T(256)S(1)}, f32[256,2048]{1,0:T(8,128)S(1)}) fusion(bf16[256,2048]{1,0:T(8,128)(2,1)} %get-tuple-element.45, bf16[2048,2048]{1,0:T(8,128)(2,1)} %get-tuple-element.46.refs_0_, bf16[256,2048]{1,0:T(8,128)(2,1)} %get-tuple-element.44), kind=kOutput, calls=%fused_computation.22 | convolution fusion | flops 2149580544 | bytes 12583936 | tf_op jit(solution)/shard_map/dot_general | solution.py:33
  147.9 1.3 copy-done.2
  149.2 1.2 multiply_convert_fusion.own_ref
  150.4 71.4 %feed_forward.1 = (f32[256,2048]{1,0:T(8,128)}, bf16[1024,2048]{1,0:T(8,128)(2,1)}, bf16[1024,1536]{1,0:T(8,128)(2,1)}, bf16[1024,1536]{1,0:T(8,128)(2,1)}, bf16...) custom-call(bf16[256,2048]{1,0:T(8,128)(2,1)} %multiply_convert_fusion.own_ref, ...), custom_call_target="tpu_custom_call" | custom-call | flops 45097156608 | bytes 62914560 | tf_op jit(solution)/shard_map/feed_forward/pallas_call | solution.py:926
  221.8 2.9 multiply_reduce_fusion
  224.9 3.7 fusion.10
  228.6 74.1 %attend_back.1 = (bf16[256,2048]{1,0:T(8,128)(2,1)}, bf16[256,256]{1,0:T(8,128)(2,1)}, bf16[192,2048]{1,0:T(8,128)(2,1)}, f32[256,2048]{1,0:T(8,128)}) custom-call(s32[2,1,128]{2,1,0:T(1,128)} %maximum_subtract_fusion.low_ref, bf16[256,2048]{1,0:T(8,128)(2,1)} %get-tuple-element.58.q_ref, bf16[1280,256]{1,0:T(8,128)(2,1)} %get-tuple-element.59.kv_ref, ...), custom_call_target="tpu_custom_call" | custom-call | flops 6039797760 | bytes 104857600 | tf_op jit(solution)/shard_map/attend_back/pallas_call | solution.py:276
  302.8 2.4 fusion.9
  305.3 3.8 fusion.8.refs_9_
  309.9 265.5 %sum_grads.1 = (bf16[4,64,1536]{2,1,0:T(8,128)(2,1)}, bf16[4,64,1536]{2,1,0:T(8,128)(2,1)}, bf16[4,64,512]{2,1,0:T(8,128)(2,1)}, bf16[64,2048]{1,0:T(8,128)(2,1)...) custom-call(bf16[1024,2048]{1,0:T(8,128)(2,1)} %get-tuple-element.52, ...), custom_call_target="tpu_custom_call" | custom-call | flops 17448304640 | bytes 419430400 | tf_op jit(solution)/shard_map/sum_grads/pallas_call | solution.py:1366
  575.4 0.8 dynamic_slice.8
  576.2 2.8 fusion.3
  580.4 0.8 copy.28
  581.2 0.8 convert_element_type.83
  582.0 1.9 convolution_bitcast_fusion
  584.1 1.3 copy.29
  585.6 1.3 copy.30
  586.9 1.3 convert_element_type.90
  (53 shorter events, 5.4 us)
Async XLA Ops:
  0.6 1.0 copy-start
  0.7 6.9 %copy-start.8 = (bf16[1,256,2048]{2,1,0:T(8,128)(2,1)S(1)}, bf16[1,256,2048]{2,1,0:T(8,128)(2,1)}, u32[]{:S(2)}) copy-start(bf16[1,256,2048]{2,1,0:T(8,128)(2,1)} %param.12) | copy-start | bytes 3145732
  147.9 1.3 copy-start.2
  221.8 3.1 copy-start.3
  221.8 3.1 copy-start.5
  302.8 2.4 copy-start.4
  302.8 2.5 copy-start.6
  575.4 4.3 copy-start.14
  575.4 4.9 copy-start.13
  575.4 5.8 copy-start.12
  576.2 5.8 copy-start.7
  581.2 2.7 copy-start.11
  584.1 1.3 copy-start.10
  585.4 2.8 copy-start.1
  585.6 1.3 copy-start.9
